TPU v7x, 32 devices: a whole 2x2x4 slice. The times are simulated.
32 devices in a mesh: fsdp: 8 (over z, x), rep: 4 (over y, core).
Axes of the slice: x: 2, y: 2, z: 4, core: 2. Of those that a mesh axis runs over, the one named last changes fastest.
Arguments:
- tokens: bfloat16 [16384, 768], P(('fsdp', 'rep')), may hold values from -6 to 6
- attn_gain: bfloat16 [768], P(('fsdp', 'rep')), may hold values from 0.5 to 1.5
- qkv_weight: bfloat16 [768, 2304], P(('fsdp', 'rep')), may hold values from -0.21875 to 0.21875
- out_weight: bfloat16 [768, 768], P(('fsdp', 'rep')), may hold values from -1.25 to 1.25
- ffn_gain: bfloat16 [768], P(('fsdp', 'rep')), may hold values from 0.5 to 1.5
- router_weight: bfloat16 [768, 8], P(('fsdp', 'rep')), may hold values from -0.15625 to 0.15625
- expert_in: bfloat16 [8, 768, 3072], P('fsdp', 'rep'), may hold values from -0.21875 to 0.21875
- expert_out: bfloat16 [8, 3072, 768], P('fsdp', 'rep'), may hold values from -0.15625 to 0.15625
- bias_table: float32 [12, 32], replicated, may hold values from -4 to 4
- seq_lengths: int32 [32, 4], P(('fsdp', 'rep')), may hold values from 1 to 384, 512 in all within a row
- bucket_map: int32 [384], replicated, may hold values from 0 to 31
- expert_ids: int32 [16384, 2], P(('fsdp', 'rep')), may hold values from 0 to 7, all different within a row; in each aligned block of 512 rows (0 to 511, 512 to 1023, ...) at most 256 rows name the same one
- cotangent: bfloat16 [16384, 768], P(('fsdp', 'rep')), may hold values from -6 to 6
Outputs:
- output: bfloat16 [16384, 768], P(('fsdp', 'rep'))
- token_grad: float32 [16384, 768], P(('fsdp', 'rep'))
- attn_gain_grad: float32 [768], P(('fsdp', 'rep'))
- qkv_grad: float32 [768, 2304], P(('fsdp', 'rep'))
- out_grad: float32 [768, 768], P(('fsdp', 'rep'))
- ffn_gain_grad: float32 [768], P(('fsdp', 'rep'))
- router_grad: float32 [768, 8], P(('fsdp', 'rep'))
- expert_in_grad: float32 [8, 768, 3072], P('fsdp', 'rep')
- expert_out_grad: float32 [8, 3072, 768], P('fsdp', 'rep')
- bias_grad: float32 [12, 32], replicated
Inputs may be any that keep to these rules, and one draw needn't show every extreme that they name: `seq_lengths`: each row lists the 4 sequences of one device in order and sums to 512; each row's longest is exactly 384. `expert_ids`: A token's two experts differ. In the rows of one device no expert is named by more than 256 rows, and in every draw some expert is named by exactly 256 rows of some device.
All inputs are finite; a program needn't handle non-finite values.
Results may differ from a plain program's by a relative error of at most 0.013.
Values may be sent and summed in bfloat16 or wider, within the bound.
No kernel may reach another device: no remote copies, remote signals or barrier semaphores. Data moves between devices by JAX's collectives and lax.ppermute only.
A program may use at most 192 MiB of HBM per device.

v0:
```python
import jax
import jax.numpy as jnp
from jax import lax
from jax.sharding import PartitionSpec as P

EPSILON = 1e-06
MASKED = -1e30
GELU_COEF = 0.7978845608028654


def rms_norm(values, gain_vector):
    return (
        values
        * lax.rsqrt(jnp.mean(values * values, axis=-1, keepdims=True) + EPSILON)
        * gain_vector
    )


def smooth_gelu(values):
    return (
        0.5 * values * (1.0 + jnp.tanh(GELU_COEF * (values + 0.044715 * values * values * values)))
    )


def times_trans(left_side, right_side):
    return lax.dot_general(
        left_side, right_side, (((1,), (1,)), ((), ())), preferred_element_type=jnp.float32
    )


def trans_times(left_side, right_side):
    return lax.dot_general(
        left_side, right_side, (((0,), (0,)), ((), ())), preferred_element_type=jnp.float32
    )


def seq_mask(lengths, row_count):
    seq_ends = jnp.cumsum(lengths, dtype=jnp.int32)
    places = jnp.arange(row_count, dtype=jnp.int32)
    segment = jnp.sum(
        (places[:, None] >= seq_ends[None, :]).astype(jnp.int32), axis=1, dtype=jnp.int32
    )
    offset = places[:, None] - places[None, :]
    return (segment[:, None] == segment[None, :]) & (offset >= 0)


def distance_onehot(bucket_map, row_count, buckets):
    longest = bucket_map.shape[0]
    tail_ids = jnp.broadcast_to(bucket_map[longest - 1 : longest], (row_count - longest,))
    extended = jnp.concatenate([bucket_map, tail_ids], axis=0)
    return (extended[:, None] == jnp.arange(buckets, dtype=jnp.int32)[None, :]).astype(jnp.float32)


def toeplitz(per_distance, row_count):
    head_count = per_distance.shape[0]
    padded = jnp.concatenate(
        [jnp.zeros((head_count, row_count - 1), jnp.float32), per_distance], axis=1
    )
    flipped = jnp.concatenate([padded[:, ::-1], jnp.zeros((head_count, 1), jnp.float32)], axis=1)
    tiled = jnp.tile(flipped, (1, row_count))
    width = 2 * row_count - 1
    window = tiled[:, row_count - 1 : row_count - 1 + row_count * width]
    return window.reshape(head_count, row_count, width)[:, :, :row_count]


def slot_position(device_ids, experts):
    flat_ids = device_ids.reshape(-1)
    chosen = (flat_ids[:, None] == jnp.arange(experts, dtype=jnp.int32)[None, :]).astype(jnp.int32)
    before = jnp.cumsum(chosen, axis=0, dtype=jnp.int32) - chosen
    position = jnp.sum(before * chosen, axis=1, dtype=jnp.int32)
    return position.reshape(device_ids.shape)


def shards(
    tokens,
    attn_gain,
    qkv_weight,
    out_weight,
    ffn_gain,
    router_weight,
    expert_in,
    expert_out,
    bias_table,
    seq_lengths,
    bucket_map,
    expert_ids,
    cotangent,
):
    row_count, model_width = tokens.shape
    head_count, buckets = bias_table.shape
    head_size = model_width // head_count
    experts = router_weight.shape[1]
    capacity = 4 * row_count // experts
    score_scale = head_size ** (-0.5)
    highest = lax.Precision.HIGHEST
    gathered = (
        lax.all_gather(attn_gain, ("fsdp", "rep"), axis=0, tiled=True),
        lax.all_gather(qkv_weight, ("fsdp", "rep"), axis=0, tiled=True),
        lax.all_gather(out_weight, ("fsdp", "rep"), axis=0, tiled=True),
        lax.all_gather(ffn_gain, ("fsdp", "rep"), axis=0, tiled=True),
        lax.all_gather(router_weight, ("fsdp", "rep"), axis=0, tiled=True),
    )
    gain_one, weight_qkv, weight_out, gain_two, weight_router = gathered
    full_in, full_out = (
        lax.all_gather(expert_in, "rep", axis=1, tiled=True),
        lax.all_gather(expert_out, "rep", axis=1, tiled=True),
    )
    weight_in = full_in[0]
    weight_back = full_out[0]
    allowed = seq_mask(seq_lengths[0], row_count)
    onehot_dist = distance_onehot(bucket_map, row_count, buckets)
    per_distance = lax.dot_general(
        bias_table, onehot_dist, (((1,), (1,)), ((), ())), precision=highest
    )
    bias_full = toeplitz(per_distance, row_count)
    inputs = tokens.astype(jnp.float32)
    normed_one = rms_norm(inputs, gain_one.astype(jnp.float32)).astype(jnp.bfloat16)
    packed = jnp.dot(normed_one, weight_qkv, preferred_element_type=jnp.float32).astype(
        jnp.bfloat16
    )
    queries = packed[:, :model_width].reshape(row_count, head_count, head_size)
    keys_all = packed[:, model_width : 2 * model_width].reshape(row_count, head_count, head_size)
    values_all = packed[:, 2 * model_width :].reshape(row_count, head_count, head_size)

    def score_of():
        raw_score = jnp.einsum(
            "ihd,jhd->hij", queries, keys_all, preferred_element_type=jnp.float32
        )
        biased = raw_score * score_scale + bias_full
        return jnp.where(allowed[None], biased, MASKED)

    score = score_of()
    row_peak = jnp.max(score, axis=-1, keepdims=True)
    log_total = row_peak + jnp.log(jnp.sum(jnp.exp(score - row_peak), axis=-1, keepdims=True))
    attn_probs = jnp.exp(score - log_total)
    attended = jnp.einsum(
        "hij,jhd->ihd",
        attn_probs.astype(jnp.bfloat16),
        values_all,
        preferred_element_type=jnp.float32,
    )
    attended = attended.astype(jnp.bfloat16).reshape(row_count, model_width)
    mixed_rows = inputs + jnp.dot(attended, weight_out, preferred_element_type=jnp.float32)
    normed_two = rms_norm(mixed_rows, gain_two.astype(jnp.float32)).astype(jnp.bfloat16)
    logits = jnp.dot(normed_two, weight_router, preferred_element_type=jnp.float32)
    choose = expert_ids[:, :, None] == jnp.arange(experts, dtype=jnp.int32)[None, None, :]
    picked = jnp.sum(jnp.where(choose, logits[:, None, :], 0.0), axis=2)
    gate_exp = jnp.exp(picked - jnp.max(picked, axis=1, keepdims=True))
    gate_values = gate_exp / jnp.sum(gate_exp, axis=1, keepdims=True)
    slot_ids = expert_ids * capacity + slot_position(expert_ids, experts)
    slot_rows = jnp.arange(experts * capacity, dtype=jnp.int32)
    first_map = (slot_rows[:, None] == slot_ids[None, :, 0]).astype(jnp.bfloat16)
    second_map = (slot_rows[:, None] == slot_ids[None, :, 1]).astype(jnp.bfloat16)
    dispatch = first_map + second_map
    sending = jnp.dot(dispatch, normed_two, preferred_element_type=jnp.float32).astype(jnp.bfloat16)
    arrived = lax.all_to_all(
        sending.reshape(experts, capacity, model_width),
        "fsdp",
        split_axis=0,
        concat_axis=0,
        tiled=True,
    )
    arrived = arrived.reshape(-1, model_width)
    block_rows = min(512, arrived.shape[0])
    arrived_blocks = arrived.reshape(-1, block_rows, model_width)

    def expert_forward(row_block):
        hidden = jnp.dot(row_block, weight_in, preferred_element_type=jnp.float32)
        active = smooth_gelu(hidden).astype(jnp.bfloat16)
        return jnp.dot(active, weight_back, preferred_element_type=jnp.float32).astype(jnp.bfloat16)

    produced = lax.map(expert_forward, arrived_blocks).reshape(-1, capacity, model_width)
    returned = lax.all_to_all(produced, "fsdp", split_axis=0, concat_axis=0, tiled=True).reshape(
        -1, model_width
    )
    first_out = trans_times(first_map, returned)
    second_out = trans_times(second_map, returned)
    output = mixed_rows + gate_values[:, 0:1] * first_out + gate_values[:, 1:2] * second_out
    regathered = (
        lax.all_gather(attn_gain, ("fsdp", "rep"), axis=0, tiled=True),
        lax.all_gather(qkv_weight, ("fsdp", "rep"), axis=0, tiled=True),
        lax.all_gather(out_weight, ("fsdp", "rep"), axis=0, tiled=True),
        lax.all_gather(ffn_gain, ("fsdp", "rep"), axis=0, tiled=True),
        lax.all_gather(router_weight, ("fsdp", "rep"), axis=0, tiled=True),
    )
    gain_one, weight_qkv, weight_out, gain_two, weight_router = regathered
    again_in, again_out = (
        lax.all_gather(expert_in, "rep", axis=1, tiled=True),
        lax.all_gather(expert_out, "rep", axis=1, tiled=True),
    )
    weight_in = again_in[0]
    weight_back = again_out[0]
    grad_rows = cotangent.astype(jnp.float32)
    d_gates = jnp.stack(
        [jnp.sum(first_out * grad_rows, axis=1), jnp.sum(second_out * grad_rows, axis=1)], axis=1
    )
    slot_grad = jnp.dot(
        first_map,
        (gate_values[:, 0:1] * grad_rows).astype(jnp.bfloat16),
        preferred_element_type=jnp.float32,
    )
    slot_grad = slot_grad + jnp.dot(
        second_map,
        (gate_values[:, 1:2] * grad_rows).astype(jnp.bfloat16),
        preferred_element_type=jnp.float32,
    )
    slot_grad = slot_grad.astype(jnp.bfloat16).reshape(experts, capacity, model_width)
    upstream = lax.all_to_all(slot_grad, "fsdp", split_axis=0, concat_axis=0, tiled=True).reshape(
        -1, block_rows, model_width
    )

    def expert_backward(totals, block_pair):
        row_block, incoming = block_pair
        hidden = jnp.dot(row_block, weight_in, preferred_element_type=jnp.float32)
        active, gelu_pull = jax.vjp(smooth_gelu, hidden)
        d_active = times_trans(incoming, weight_back)
        d_hidden = gelu_pull(d_active)[0].astype(jnp.bfloat16)
        grad_in = totals[0] + trans_times(row_block, d_hidden)
        grad_out = totals[1] + trans_times(active.astype(jnp.bfloat16), incoming)
        d_block = times_trans(d_hidden, weight_in).astype(jnp.bfloat16)
        return ((grad_in, grad_out), d_block)

    empty_in = jnp.zeros(weight_in.shape, jnp.float32)
    empty_out = jnp.zeros(weight_back.shape, jnp.float32)
    (grad_in, grad_out), d_blocks = lax.scan(
        expert_backward, (empty_in, empty_out), (arrived_blocks, upstream)
    )
    owned_in, owned_out = (
        lax.psum_scatter(
            grad_in.astype(jnp.bfloat16), "rep", scatter_dimension=0, tiled=True
        ).astype(jnp.float32),
        lax.psum_scatter(
            grad_out.astype(jnp.bfloat16), "rep", scatter_dimension=0, tiled=True
        ).astype(jnp.float32),
    )
    back_rows = lax.all_to_all(
        d_blocks.reshape(-1, capacity, model_width), "fsdp", split_axis=0, concat_axis=0, tiled=True
    )
    d_normed_two = trans_times(dispatch, back_rows.reshape(-1, model_width))
    gate_mean = jnp.sum(gate_values * d_gates, axis=1, keepdims=True)
    d_picked = gate_values * (d_gates - gate_mean)
    d_logits = jnp.sum(jnp.where(choose, d_picked[:, :, None], 0.0), axis=1).astype(jnp.bfloat16)
    grad_router = trans_times(normed_two, d_logits)
    d_normed_two = d_normed_two + times_trans(d_logits, weight_router)
    unused_two, norm_pull_two = jax.vjp(rms_norm, mixed_rows, gain_two.astype(jnp.float32))
    d_mixed_norm, grad_gain_two = norm_pull_two(d_normed_two)
    d_mixed = grad_rows + d_mixed_norm
    d_branch = d_mixed.astype(jnp.bfloat16)
    grad_out_weight = trans_times(attended, d_branch)
    d_attended = (
        times_trans(d_branch, weight_out)
        .astype(jnp.bfloat16)
        .reshape(row_count, head_count, head_size)
    )
    attn_probs = jnp.exp(score_of() - log_total)
    d_probs = jnp.einsum("ihd,jhd->hij", d_attended, values_all, preferred_element_type=jnp.float32)
    d_values = jnp.einsum(
        "hij,ihd->jhd",
        attn_probs.astype(jnp.bfloat16),
        d_attended,
        preferred_element_type=jnp.float32,
    )
    row_delta = jnp.sum(attn_probs * d_probs, axis=-1, keepdims=True)
    d_score = (attn_probs * (d_probs - row_delta)).astype(jnp.bfloat16)
    d_queries = (
        jnp.einsum("hij,jhd->ihd", d_score, keys_all, preferred_element_type=jnp.float32)
        * score_scale
    )
    d_keys = (
        jnp.einsum("hij,ihd->jhd", d_score, queries, preferred_element_type=jnp.float32)
        * score_scale
    )
    d_packed = jnp.concatenate(
        [
            d_queries.reshape(row_count, model_width),
            d_keys.reshape(row_count, model_width),
            d_values.reshape(row_count, model_width),
        ],
        axis=1,
    ).astype(jnp.bfloat16)
    unused_bias, toeplitz_pull = jax.vjp(lambda spread: toeplitz(spread, row_count), per_distance)
    d_distance = toeplitz_pull(d_score.astype(jnp.float32))[0]
    bias_local = jnp.dot(d_distance, onehot_dist, precision=highest)
    bias_grad = lax.psum(bias_local, ("fsdp", "rep"))
    grad_qkv = trans_times(normed_one, d_packed)
    d_normed_one = times_trans(d_packed, weight_qkv)
    unused_one, norm_pull_one = jax.vjp(rms_norm, inputs, gain_one.astype(jnp.float32))
    d_inputs_norm, grad_gain_one = norm_pull_one(d_normed_one)
    token_grad = d_mixed + d_inputs_norm
    owned = (
        lax.psum_scatter(grad_gain_one, ("fsdp", "rep"), scatter_dimension=0, tiled=True),
        lax.psum_scatter(grad_qkv, ("fsdp", "rep"), scatter_dimension=0, tiled=True),
        lax.psum_scatter(grad_out_weight, ("fsdp", "rep"), scatter_dimension=0, tiled=True),
        lax.psum_scatter(grad_gain_two, ("fsdp", "rep"), scatter_dimension=0, tiled=True),
        lax.psum_scatter(grad_router, ("fsdp", "rep"), scatter_dimension=0, tiled=True),
    )
    return (
        output.astype(jnp.bfloat16),
        token_grad,
        owned[0],
        owned[1],
        owned[2],
        owned[3],
        owned[4],
        owned_in[None],
        owned_out[None],
        bias_grad,
    )


def solution(mesh):
    return jax.shard_map(
        shards,
        mesh=mesh,
        in_specs=(
            P(("fsdp", "rep"), None),
            P(("fsdp", "rep")),
            P(("fsdp", "rep"), None),
            P(("fsdp", "rep"), None),
            P(("fsdp", "rep")),
            P(("fsdp", "rep"), None),
            P("fsdp", "rep", None),
            P("fsdp", "rep", None),
            P(),
            P(("fsdp", "rep"), None),
            P(),
            P(("fsdp", "rep"), None),
            P(("fsdp", "rep"), None),
        ),
        out_specs=(
            P(("fsdp", "rep"), None),
            P(("fsdp", "rep"), None),
            P(("fsdp", "rep")),
            P(("fsdp", "rep"), None),
            P(("fsdp", "rep"), None),
            P(("fsdp", "rep")),
            P(("fsdp", "rep"), None),
            P("fsdp", "rep", None),
            P("fsdp", "rep", None),
            P(),
        ),
        check_vma=False,
    )
```

profile of v0, /device:TPU:0, one launch (start us, length us, event | category | flops | bytes accessed | tf_op | source)
XLA Modules:
  0.0 1044.6 jit_solution(6855606829698658241)
XLA Ops:
  12.9 42.0 %all-reduce.11 = (bf16[768]{0:T(1024)(128)(2,1)S(1)}, bf16[768]{0:T(1024)(128)(2,1)S(1)}) all-reduce(bf16[768]{0:T(1024)(128)(2,1)S(1)} %dynamic-update-slice, bf16[768]{0:T(1024)(128)(2,1)S(1)} %dynamic-update-slice.1), channel_id=1, replica_groups=mesh['fsdp'=8,'rep'=4] {'fsdp','rep'}, use_global_device_ids=true, to_apply=%add.5 | all-reduce | flops 1536 | bytes 6144
  57.6 11.7 %tile.4 = f32[12,512,1024]{2,1,0:T(8,128)} broadcast(f32[12,1024]{1,0:T(8,128)S(1)} %concatenate.19), dimensions={0,2} | broadcast | bytes 25214976 | tf_op jit(solution)/shard_map/tile | solution.py:60
  69.3 11.0 %pad.18 = f32[16,512,1024]{2,1,0:T(8,128)S(1)} pad(f32[12,512,1024]{2,1,0:T(8,128)} %tile.4, f32[]{:T(128)} %constant.39.clone.1), padding=0_4x0_0x0_0 | pad | bytes 58720260
  80.3 39.8 %copy.128 = f32[2,8,512,1024]{3,1,2,0:T(8,128)} copy(f32[2,8,512,1024]{3,2,1,0:T(8,128)S(1)} %bitcast.166) | data formatting | bytes 67108864
  120.0 25.9 %slice.55 = f32[12,523776]{1,0:T(8,128)} slice(f32[12,524288]{1,0:T(8,128)} %bitcast.168), slice={[0:12], [511:524287]} | slice | bytes 50282496 | tf_op jit(solution)/shard_map/slice | solution.py:62
  146.0 42.7 %reshape.297 = f32[12,512,1023]{2,1,0:T(8,128)} reshape(f32[12,523776]{1,0:T(8,128)} %slice.55) | data formatting | bytes 50282496 | tf_op jit(solution)/shard_map/reshape | solution.py:63
  188.7 10.7 %slice.56 = f32[12,512,512]{2,1,0:T(8,128)} slice(f32[12,512,1023]{2,1,0:T(8,128)} %reshape.297), slice={[0:12], [0:512], [0:512]} | slice | bytes 25165824 | tf_op jit(solution)/shard_map/slice | solution.py:63
  199.5 12.7 %copy.126 = f32[12,512,512]{1,2,0:T(8,128)} copy(f32[12,512,512]{2,1,0:T(8,128)} %slice.56) | data formatting | bytes 25165824
  215.9 4.1 convolution_convert_fusion.1
  221.0 6.8 fusion.134
  242.3 6.1 all-to-all-start
  248.5 68.8 %all-to-all-done = bf16[8,256,768]{2,1,0:T(8,128)(2,1)} async-done(((bf16[8,256,768]{2,1,0:T(8,128)(2,1)}), bf16[8,256,768]{2,1,0:T(8,128)(2,1)}, u32[]{:S(2)}, u32[]{:S(2)}) %all-to-all-start) | async-done | bytes 3145760 | tf_op jit(solution)/shard_map/all_to_all | solution.py:156
  319.2 40.8 %while.25 = (s32[]{:T(128)}, bf16[4,512,768]{2,1,0:T(8,128)(2,1)}, bf16[4,512,768]{2,1,0:T(8,128)(2,1)}, bf16[768,3072]{1,0:T(8,128)(2,1)}, bf16[3072,768]{1,0:T(8,128)(2,1)}, /*index=5*/s32[]{:T(128)}) while((s32[]{:T(128)}, bf16[4,512,768]{2,1,0:T(8,128)(2,1)}, bf16[4,512,768]{2,1,0:T(8,128)(2,1)}, bf16[768,3072]{1,0:T(8,128)(2,1)}, ...), condition=%wide.region_13.14_spmd, body=%wide.region_12.13_spmd.sunk | while | flops 4846387200 | bytes 11011149 | solution.py:172
  319.2 10.2 fusion.193
  329.4 10.2 fusion.193
  339.6 10.2 fusion.193
  349.8 10.2 fusion.193
  360.0 4.6 all-to-all-start.1
  364.6 86.0 %all-gather = bf16[32,24,8]{1,2,0:T(8,128)(2,1)S(1)} all-gather(bf16[1,24,8]{1,2,0:T(8,128)(2,1)S(1)} %bitcast.200), channel_id=1, replica_groups=mesh['fsdp'=8,'rep'=4] {'fsdp','rep'}, dimensions={0}, use_global_device_ids=true | all-gather | bytes 12672 | tf_op jit(solution)/shard_map/all_gather | solution.py:101
  451.2 4.0 fusion.64
  455.2 5.7 fusion.94
  463.7 4.0 add_convert_fusion
  467.7 12.5 %all-to-all-start.2 = ((bf16[8,256,768]{2,1,0:T(8,128)(2,1)}), bf16[8,256,768]{2,1,0:T(8,128)(2,1)}, u32[]{:S(2)}, u32[]{:S(2)}) async-start(bf16[8,256,768]{2,1,0:T(8,128)(2,1)} %bitcast.23), calls=%async_computation.2 | async-start | bytes 6291456 | tf_op jit(solution)/shard_map/all_to_all | solution.py:208
  480.2 72.2 %all-to-all-done.2 = bf16[8,256,768]{2,1,0:T(8,128)(2,1)} async-done(((bf16[8,256,768]{2,1,0:T(8,128)(2,1)}), bf16[8,256,768]{2,1,0:T(8,128)(2,1)}, u32[]{:S(2)}, u32[]{:S(2)}) %all-to-all-start.2) | async-done | bytes 3145760 | tf_op jit(solution)/shard_map/all_to_all | solution.py:208
  554.3 151.1 %while.26 = (s32[]{:T(128)}, f32[768,3072]{1,0:T(8,128)}, f32[3072,768]{1,0:T(8,128)}, bf16[4,512,768]{2,1,0:T(8,128)(2,1)}, bf16[4,512,768]{2,1,0:T(8,128)(2,1)...) while((s32[]{:T(128)}, f32[768,3072]{1,0:T(8,128)}, ...), condition=%wide.region_15.16_spmd.clone, body=%wide.region_14.15_spmd.clone.sunk | while | flops 12141330432 | bytes 243007840 | solution.py:225
  554.5 4.8 fusion.203
  561.9 8.2 fusion.204
  570.2 7.4 select_add_fusion.4
  579.2 7.1 select_add_fusion.5
  586.4 3.8 fusion.205
  590.2 4.8 fusion.203
  597.6 8.2 fusion.204
  605.9 8.8 select_add_fusion.4
  617.6 7.1 select_add_fusion.5
  628.6 4.8 fusion.203
  636.0 8.2 fusion.204
  644.3 8.8 select_add_fusion.4
  656.0 7.1 select_add_fusion.5
  663.2 3.8 fusion.205
  667.0 4.8 fusion.203
  674.4 8.2 fusion.204
  682.7 8.8 select_add_fusion.4
  694.5 7.1 select_add_fusion.5
  701.6 3.8 fusion.205
  705.4 6.2 convert_element_type.127
  711.9 7.5 convert_element_type.126
  719.5 4.6 all-to-all-start.3
  724.5 70.8 %all-to-all-done.3 = bf16[8,256,768]{2,1,0:T(8,128)(2,1)} async-done(((bf16[8,256,768]{2,1,0:T(8,128)(2,1)}), bf16[8,256,768]{2,1,0:T(8,128)(2,1)}, u32[]{:S(2)}, u32[]{:S(2)}) %all-to-all-start.3) | async-done | bytes 3145760 | tf_op jit(solution)/shard_map/all_to_all | solution.py:236
  795.3 4.0 fusion.70
  807.5 8.0 multiply_reduce_fusion
  816.2 5.3 multiply_convert_fusion.2
  821.4 8.7 copy.127
  830.1 9.0 pad.11.clone
  839.2 35.3 %reshape.312 = bf16[12,523776]{1,0:T(8,128)(2,1)} reshape(bf16[12,512,1023]{2,1,0:T(8,128)(2,1)} %pad.11.clone) | data formatting | bytes 25141248 | tf_op jit(solution)/shard_map/transpose(jvp())/reshape | solution.py:63
  874.5 4.9 multiply_convert_fusion.3
  879.4 4.4 multiply_convert_fusion.4
  883.8 6.7 fusion.99
  891.4 5.1 fusion.103
  896.6 10.2 pad_convert_fusion
  906.8 35.7 %copy.130 = f32[2,8,512,1024]{3,2,1,0:T(8,128)} copy(f32[2,8,512,1024]{3,1,2,0:T(8,128)S(1)} %bitcast.167) | data formatting | bytes 67108864
  942.5 9.7 slice_reduce_fusion
  953.0 6.2 fusion.88
  959.2 40.2 %all-reduce.10 = (f32[768]{0:T(1024)S(1)}, f32[768]{0:T(1024)S(1)}, f32[768,8]{0,1:T(8,128)S(1)}, f32[12,32]{1,0:T(8,128)}) all-reduce(f32[768]{0:T(1024)S(1)} %get-tuple-element.114, f32[768]{0:T(1024)S(1)} %get-tuple-element.112, f32[768,8]{0,1:T(8,128)S(1)} %fusion.136, ...), channel_id=2, replica_groups=mesh['fsdp'=8,'rep'=4] {'fsdp','rep'}, use_global_device_ids=true, to_apply=%region_24.25.clone | all-reduce | flops 8064 | bytes 64512
  1010.2 27.4 %reduce-scatter.6.cloned.1.call-done = f32[24,2304]{1,0:T(8,128)} async-done(((f32[768,2304]{1,0:T(8,128)}), f32[24,2304]{1,0:T(8,128)}) %reduce-scatter.6.cloned.1.call-update) | async-done | bytes 221200 | tf_op jit(solution)/shard_map/reduce_scatter | solution.py:292
  (298 shorter events, 80.5 us)
Async XLA Ops:
  7.2 49.3 %copy-start = (f32[12,32]{1,0:T(8,128)S(1)}, f32[12,32]{1,0:T(8,128)}, u32[]{:S(2)}) copy-start(f32[12,32]{1,0:T(8,128)} %param.25) | copy-start | bytes 4612
  7.2 47.7 %copy-start.21 = (bf16[512,768]{1,0:T(8,128)(2,1)S(1)}, bf16[512,768]{1,0:T(8,128)(2,1)}, u32[]{:S(2)}) copy-start(bf16[512,768]{1,0:T(8,128)(2,1)} %param.17) | copy-start | bytes 2359300
  7.2 48.0 %copy-start.61 = (s32[384]{0:T(512)S(1)}, s32[384]{0:T(512)}, u32[]{:S(2)}) copy-start(s32[384]{0:T(512)} %param.27) | copy-start | bytes 4612
  7.2 208.6 %all-gather.6.cloned.1.call-start = ((), (), s32[]{:S(2)}) async-start(), calls=%async_computation.8 | async-start | bytes 3649536 | tf_op jit(solution)/shard_map/all_gather | solution.py:98
  7.9 226.8 %all-gather.8.cloned.1.call-start = ((), (), s32[]{:S(2)}) async-start(), calls=%async_computation.9 | async-start | bytes 1216512 | tf_op jit(solution)/shard_map/all_gather | solution.py:99
  8.7 239.8 %all-gather.10.cloned.1.call-start = ((), (), s32[]{:S(2)}) async-start(), calls=%async_computation.10 | async-start | bytes 5898240 | tf_op jit(solution)/shard_map/all_gather | solution.py:105
  9.4 239.1 %all-gather.12.cloned.1.call-start = ((), (), s32[]{:S(2)}) async-start(), calls=%async_computation.11 | async-start | bytes 5898240 | tf_op jit(solution)/shard_map/all_gather | solution.py:106
  54.9 160.9 %copy-start.45 = (f32[768]{0:T(1024)}, f32[768]{0:T(1024)S(1)}, u32[]{:S(2)}) copy-start(f32[768]{0:T(1024)S(1)} %convert_element_type.103) | copy-start | bytes 9220
  55.2 160.7 %copy-start.47 = (f32[512]{0:T(512)}, f32[512]{0:T(512)S(1)}, u32[]{:S(2)}) copy-start(f32[512]{0:T(512)S(1)} %fusion.126) | copy-start | bytes 6148
  56.5 12.8 %copy-start.62 = (s32[512]{0:T(512)}, s32[512]{0:T(512)S(1)}, u32[]{:S(2)}) copy-start(s32[512]{0:T(512)S(1)} %concatenate.17) | copy-start | bytes 6148
  199.5 12.7 %copy-start.70 = (s32[1,4]{1,0:T(1,128)S(1)}, s32[1,4]{1,0:T(1,128)}, u32[]{:S(2)}) copy-start(s32[1,4]{1,0:T(1,128)} %param.26) | copy-start | bytes 52
  199.5 16.3 %copy-start.37 = (s32[512,2]{0,1:T(2,128)S(1)}, s32[512,2]{0,1:T(2,128)}, u32[]{:S(2)}) copy-start(s32[512,2]{0,1:T(2,128)} %param.28) | copy-start | bytes 12292
  212.6 24.6 %copy-start.35 = (f32[768]{0:T(1024)}, f32[768]{0:T(1024)S(1)}, u32[]{:S(2)}) copy-start(f32[768]{0:T(1024)S(1)} %convert_element_type.110) | copy-start | bytes 9220
  215.8 245.7 %copy-start.66 = (s32[512,1]{0,1:T(1,128)}, s32[512,1]{0,1:T(1,128)S(1)}, u32[]{:S(2)}) copy-start(s32[512,1]{0,1:T(1,128)S(1)} %get-tuple-element.160) | copy-start | bytes 6148
  215.8 247.8 %copy-start.64 = (s32[512,1]{0,1:T(1,128)}, s32[512,1]{0,1:T(1,128)S(1)}, u32[]{:S(2)}) copy-start(s32[512,1]{0,1:T(1,128)S(1)} %get-tuple-element.159) | copy-start | bytes 6148
  220.4 9.3 copy-start.13
  220.7 7.1 copy-start.15
  221.0 6.8 copy-start.9
  237.2 5.2 copy-start.58
  238.5 212.2 %copy-start.17 = (bf16[512,768]{1,0:T(8,128)(2,1)}, bf16[512,768]{1,0:T(8,128)(2,1)S(1)}, u32[]{:S(2)}) copy-start(bf16[512,768]{1,0:T(8,128)(2,1)S(1)} %multiply_convert_fusion.5) | copy-start | bytes 2359300
  242.3 75.0 %all-to-all-start = ((bf16[8,256,768]{2,1,0:T(8,128)(2,1)}), bf16[8,256,768]{2,1,0:T(8,128)(2,1)}, u32[]{:S(2)}, u32[]{:S(2)}) async-start(bf16[8,256,768]{2,1,0:T(8,128)(2,1)} %bitcast.183), calls=%async_computation | async-start | bytes 6291456 | tf_op jit(solution)/shard_map/all_to_all | solution.py:156
  360.0 91.2 %all-to-all-start.1 = ((bf16[8,256,768]{2,1,0:T(8,128)(2,1)}), bf16[8,256,768]{2,1,0:T(8,128)(2,1)}, u32[]{:S(2)}, u32[]{:S(2)}) async-start(bf16[8,256,768]{2,1,0:T(8,128)(2,1)} %bitcast.20), calls=%async_computation.1 | async-start | bytes 6291456 | tf_op jit(solution)/shard_map/all_to_all | solution.py:173
  455.2 5.7 copy-start.24
  467.7 84.8 %all-to-all-start.2 = ((bf16[8,256,768]{2,1,0:T(8,128)(2,1)}), bf16[8,256,768]{2,1,0:T(8,128)(2,1)}, u32[]{:S(2)}, u32[]{:S(2)}) async-start(bf16[8,256,768]{2,1,0:T(8,128)(2,1)} %bitcast.23), calls=%async_computation.2 | async-start | bytes 6291456 | tf_op jit(solution)/shard_map/all_to_all | solution.py:208
  480.2 524.2 %reduce-scatter.12.cloned.1.call-start = ((), (), s32[]{:S(2)}) async-start(), calls=%async_computation.15 | async-start | bytes 5898240 | tf_op jit(solution)/shard_map/reduce_scatter | solution.py:232
  554.5 7.4 copy-start.68
  570.2 7.4 copy-start.4
  570.2 9.0 copy-start.11
  570.2 16.1 %slice-start.3 = ((s8[4718592]{0:T(1024)(128)(4,1)}), s8[4194304]{0:T(1024)(128)(4,1)S(1)}, s32[]{:S(2)}) async-start(s8[4718592]{0:T(1024)(128)(4,1)} %bitcast.170), calls=%async_computation.19 | async-start | bytes 8388608 | tf_op jit(solution)/shard_map/while
  579.2 7.1 slice-start.4
  590.2 7.4 copy-start.68
  605.9 8.8 copy-start.4
  605.9 11.8 %copy-start.11 = (f32[3072,768]{1,0:T(8,128)S(1)}, f32[3072,768]{1,0:T(8,128)}, u32[]{:S(2)}) copy-start(f32[3072,768]{1,0:T(8,128)} %get-tuple-element.280) | copy-start | bytes 28311556 | tf_op jit(solution)/shard_map/while
  605.9 18.9 %slice-start.3 = ((s8[4718592]{0:T(1024)(128)(4,1)}), s8[4194304]{0:T(1024)(128)(4,1)S(1)}, s32[]{:S(2)}) async-start(s8[4718592]{0:T(1024)(128)(4,1)} %bitcast.170), calls=%async_computation.19 | async-start | bytes 8388608 | tf_op jit(solution)/shard_map/while
  617.6 7.2 slice-start.4
  628.6 7.4 copy-start.68
  644.2 8.8 copy-start.4
  644.2 11.8 %copy-start.11 = (f32[3072,768]{1,0:T(8,128)S(1)}, f32[3072,768]{1,0:T(8,128)}, u32[]{:S(2)}) copy-start(f32[3072,768]{1,0:T(8,128)} %get-tuple-element.280) | copy-start | bytes 28311556 | tf_op jit(solution)/shard_map/while
  644.3 18.9 %slice-start.3 = ((s8[4718592]{0:T(1024)(128)(4,1)}), s8[4194304]{0:T(1024)(128)(4,1)S(1)}, s32[]{:S(2)}) async-start(s8[4718592]{0:T(1024)(128)(4,1)} %bitcast.170), calls=%async_computation.19 | async-start | bytes 8388608 | tf_op jit(solution)/shard_map/while
  656.0 7.2 slice-start.4
  667.0 7.4 copy-start.68
  682.7 8.8 copy-start.4
  682.7 11.8 %copy-start.11 = (f32[3072,768]{1,0:T(8,128)S(1)}, f32[3072,768]{1,0:T(8,128)}, u32[]{:S(2)}) copy-start(f32[3072,768]{1,0:T(8,128)} %get-tuple-element.280) | copy-start | bytes 28311556 | tf_op jit(solution)/shard_map/while
  682.7 18.9 %slice-start.3 = ((s8[4718592]{0:T(1024)(128)(4,1)}), s8[4194304]{0:T(1024)(128)(4,1)S(1)}, s32[]{:S(2)}) async-start(s8[4718592]{0:T(1024)(128)(4,1)} %bitcast.170), calls=%async_computation.19 | async-start | bytes 8388608 | tf_op jit(solution)/shard_map/while
  694.5 7.2 slice-start.4
  711.7 295.5 %reduce-scatter.10.cloned.1.call-start = ((), (), s32[]{:S(2)}) async-start(), calls=%async_computation.14 | async-start | bytes 5898240 | tf_op jit(solution)/shard_map/reduce_scatter | solution.py:229
  719.5 75.8 %copy-start.65 = (s32[512,1]{0,1:T(1,128)S(1)}, s32[512,1]{0,1:T(1,128)}, u32[]{:S(2)}) copy-start(s32[512,1]{0,1:T(1,128)} %copy-done.64) | copy-start | bytes 6148
  719.5 75.8 %copy-start.67 = (s32[512,1]{0,1:T(1,128)S(1)}, s32[512,1]{0,1:T(1,128)}, u32[]{:S(2)}) copy-start(s32[512,1]{0,1:T(1,128)} %copy-done.66) | copy-start | bytes 6148
  719.5 75.8 %all-to-all-start.3 = ((bf16[8,256,768]{2,1,0:T(8,128)(2,1)}), bf16[8,256,768]{2,1,0:T(8,128)(2,1)}, u32[]{:S(2)}, u32[]{:S(2)}) async-start(bf16[8,256,768]{2,1,0:T(8,128)(2,1)} %bitcast.25), calls=%async_computation.3 | async-start | bytes 6291456 | tf_op jit(solution)/shard_map/all_to_all | solution.py:236
  724.1 286.0 %reduce-scatter.8.cloned.1.call-start = ((), (), s32[]{:S(2)}) async-start(), calls=%async_computation.13 | async-start | bytes 2433024 | tf_op jit(solution)/shard_map/reduce_scatter | solution.py:293
  807.4 230.2 %reduce-scatter.6.cloned.1.call-start = ((), (), s32[]{:S(2)}) async-start(), calls=%async_computation.12 | async-start | bytes 7299072 | tf_op jit(solution)/shard_map/reduce_scatter | solution.py:292
  807.5 8.0 slice-start
  807.5 8.0 slice-start.1
  807.5 8.7 slice-start.2
  839.2 35.3 %copy-start.16 = (bf16[512,768]{0,1:T(8,128)(2,1)S(1)}, bf16[512,768]{0,1:T(8,128)(2,1)}, u32[]{:S(2)}) copy-start(bf16[512,768]{0,1:T(8,128)(2,1)} %copy-done.15) | copy-start | bytes 2359300
  874.5 4.9 copy-start.10
  879.4 11.2 %copy-start.32 = (bf16[12,64,512]{2,1,0:T(8,128)(2,1)}, bf16[12,64,512]{2,1,0:T(8,128)(2,1)S(1)}, u32[]{:S(2)}) copy-start(bf16[12,64,512]{2,1,0:T(8,128)(2,1)S(1)} %multiply_convert_fusion.3) | copy-start | bytes 2359300
  883.8 7.7 copy-start.23
  883.8 7.7 copy-start.46
  883.8 7.6 copy-start.48
  942.5 10.2 copy-start.63
  953.0 48.2 %copy-start.44 = (f32[512]{0:T(512)S(1)}, f32[512]{0:T(512)}, u32[]{:S(2)}) copy-start(f32[512]{0:T(512)} %copy-done.43) | copy-start | bytes 6148
  953.0 48.2 %copy-start.8 = (f32[512,768]{1,0:T(8,128)S(1)}, f32[512,768]{1,0:T(8,128)}, u32[]{:S(2)}) copy-start(f32[512,768]{1,0:T(8,128)} %copy-done.7) | copy-start | bytes 4718596
  1001.2 36.3 %copy-start.1 = (f32[12,32]{1,0:T(8,128)S(1)}, f32[12,32]{1,0:T(8,128)}, u32[]{:S(2)}) copy-start(f32[12,32]{1,0:T(8,128)} %param.25) | copy-start | bytes 4612
  (45 other events, 137.6 us)
Sparse Core Ops, SparseCore 0:
  11.0 62.8 all-gather.5
  76.8 52.9 all-gather.7
  131.3 36.3 all-gather.9
  169.1 37.4 all-gather.11
  711.8 44.9 reduce-scatter.11
  759.4 47.8 reduce-scatter.9
  813.1 99.0 reduce-scatter.7
  919.4 118.1 reduce-scatter.5
where the time goes:
time: 1060 us; the launch traced here: 1040 us
  local copies, waits for them, and re-layouts  285 us (27%)
  matrix products  250 us (24%)
  waiting for transfers between devices  242 us (23%)
  blocking collectives  168 us (16%)
  other arithmetic  55.4 us (5%)
  starting transfers between devices  28.3 us (3%)
  between operations  15.6 us (1%)
    unnamed x154, local copies, waits for them, and re-layouts  120 us
    all_gather x1, blocking collectives, shards(): lax.all_gather(router_weight, ('fsdp', 'rep'), axis=0, tiled=True)  86 us
    dot_general x14, matrix products, trans_times(): lax.dot_general(left_side, right_side, (((0,), (0,)), ((), ())), preferre...  83.5 us
    unnamed x2, blocking collectives  82.2 us
    reshape x2, local copies, waits for them, and re-layouts, toeplitz(): return window.reshape(head_count, row_count, width)[:, :, :row_count]  78 us
    all_to_all x1, waiting for transfers between devices, shards(): lax.all_to_all(slot_grad, 'fsdp', split_axis=0, concat_axis=0, tiled=True)  72.2 us
    all_to_all x1, waiting for transfers between devices, shards(): lax.all_to_all(d_blocks.reshape(-1, capacity, model_width), 'fsdp', split...  70.8 us
    all_to_all x1, waiting for transfers between devices, shards(): lax.all_to_all(sending.reshape(experts, capacity, model_width), 'fsdp', s...  68.8 us
  transfers between devices with their start and end apart: 12, of which 4 were waited for; matrix products, arithmetic and copies ran while one was open for 35% of the time, Pallas kernels for 0%

commit v1 on v0

v1 whole, which is shorter than its diff:
```python
import functools

import jax
import jax.numpy as jnp
from jax import lax
from jax.experimental import pallas as pl
from jax.experimental.pallas import tpu as pltpu
from jax.sharding import PartitionSpec as P

EPSILON = 1e-06
MASKED = -1e30
GELU_COEF = 0.7978845608028654
TILE = 128
LANES = 128
VMEM_BYTES = 56 * 1024 * 1024


def rms_norm(values, gain_vector):
    return (
        values
        * lax.rsqrt(jnp.mean(values * values, axis=-1, keepdims=True) + EPSILON)
        * gain_vector
    )


def times(left_side, right_side):
    return lax.dot_general(
        left_side, right_side, (((1,), (0,)), ((), ())), preferred_element_type=jnp.float32
    )


def times_trans(left_side, right_side):
    return lax.dot_general(
        left_side, right_side, (((1,), (1,)), ((), ())), preferred_element_type=jnp.float32
    )


def trans_times(left_side, right_side):
    return lax.dot_general(
        left_side, right_side, (((0,), (0,)), ((), ())), preferred_element_type=jnp.float32
    )


def sequence_starts(lengths, row_count):
    seq_ends = jnp.cumsum(lengths, dtype=jnp.int32)
    places = jnp.arange(row_count, dtype=jnp.int32)
    passed = places[:, None] >= seq_ends[None, :]
    return jnp.max(jnp.where(passed, seq_ends[None, :], 0), axis=1, keepdims=True)


def distance_onehot(bucket_map, row_count, buckets):
    longest = bucket_map.shape[0]
    distance = row_count - TILE - jnp.arange(row_count, dtype=jnp.int32)
    place = jnp.arange(longest, dtype=jnp.int32)
    at_distance = jnp.sum(
        jnp.where(distance[:, None] == place[None, :], bucket_map[None, :] + 1, 0), axis=1
    )
    return (at_distance[:, None] == 1 + jnp.arange(buckets, dtype=jnp.int32)[None, :]).astype(
        jnp.float32
    )


def head_lanes(block, which, head_size):
    lane = lax.broadcasted_iota(jnp.int32, block.shape, 1)
    inside = (lane >= which * head_size) & (lane < (which + 1) * head_size)
    return jnp.where(inside, block, jnp.zeros_like(block))


def bias_strip(base_ref, head, row_count):
    row = base_ref[pl.ds(head, 1), :]
    spread = jnp.broadcast_to(row, (TILE, row_count))
    return pltpu.roll(spread, 0, 1, stride=1, stride_axis=0)


def tile_probs(query_tile, keys, strip, starts, tile, scale):
    row_count = strip.shape[1]
    width = TILE * (tile + 1)
    score = times_trans(query_tile, keys[:width]) * scale + strip[:, row_count - width :]
    place = lax.broadcasted_iota(jnp.int32, score.shape, 1)
    row = lax.broadcasted_iota(jnp.int32, score.shape, 0) + TILE * tile
    score = jnp.where((place <= row) & (place >= starts), score, MASKED)
    exponent = jnp.exp(score - jnp.max(score, axis=1, keepdims=True))
    return exponent * (1.0 / jnp.sum(exponent, axis=1, keepdims=True))


def lane_block(first):
    return pl.ds(pl.multiple_of(first, LANES), LANES)


def attention_kernel(head_size, base_ref, starts_ref, packed_ref, attended_ref):
    row_count, width = attended_ref.shape
    per_block = LANES // head_size
    scale = head_size ** (-0.5)

    @pl.loop(0, width // LANES)
    def _(block):
        queries = packed_ref[:, lane_block(block * LANES)]
        keys = packed_ref[:, lane_block(width + block * LANES)]
        values = packed_ref[:, lane_block(2 * width + block * LANES)]
        strips = [bias_strip(base_ref, block * per_block + own, row_count) for own in range(per_block)]
        for tile in range(row_count // TILE):
            rows = slice(tile * TILE, (tile + 1) * TILE)
            starts = starts_ref[rows, :]
            total = jnp.zeros((TILE, LANES), jnp.float32)
            for own in range(per_block):
                probs = tile_probs(
                    head_lanes(queries[rows], own, head_size), keys, strips[own], starts, tile, scale
                ).astype(jnp.bfloat16)
                total += times(probs, head_lanes(values[: probs.shape[1]], own, head_size))
            attended_ref[rows, lane_block(block * LANES)] = total.astype(jnp.bfloat16)


def attention(base, starts, packed, head_size):
    row_count = packed.shape[0]
    width = packed.shape[1] // 3
    return pl.pallas_call(
        functools.partial(attention_kernel, head_size),
        out_shape=jax.ShapeDtypeStruct((row_count, width), jnp.bfloat16),
        compiler_params=pltpu.CompilerParams(vmem_limit_bytes=VMEM_BYTES),
        cost_estimate=pl.CostEstimate(
            flops=8 * row_count * row_count * width,
            bytes_accessed=8 * row_count * width,
            transcendentals=row_count * row_count * width // head_size,
        ),
        name="attention",
    )(base, starts, packed)


def attention_pull_kernel(
    head_size,
    base_ref,
    starts_ref,
    packed_ref,
    grad_ref,
    d_packed_ref,
    d_base_ref,
    d_keys_ref,
    d_values_ref,
    d_strip_ref,
):
    row_count, width = grad_ref.shape
    per_block = LANES // head_size
    scale = head_size ** (-0.5)

    @pl.loop(0, width // LANES)
    def _(block):
        queries = packed_ref[:, lane_block(block * LANES)]
        keys = packed_ref[:, lane_block(width + block * LANES)]
        values = packed_ref[:, lane_block(2 * width + block * LANES)]
        grads = grad_ref[:, lane_block(block * LANES)]
        strips = [bias_strip(base_ref, block * per_block + own, row_count) for own in range(per_block)]
        d_keys_ref[...] = jnp.zeros_like(d_keys_ref)
        d_values_ref[...] = jnp.zeros_like(d_values_ref)
        d_strip_ref[...] = jnp.zeros_like(d_strip_ref)
        for tile in range(row_count // TILE):
            rows = slice(tile * TILE, (tile + 1) * TILE)
            reach = TILE * (tile + 1)
            starts = starts_ref[rows, :]
            d_queries = jnp.zeros((TILE, LANES), jnp.float32)
            for own in range(per_block):
                own_queries = head_lanes(queries[rows], own, head_size)
                own_grads = head_lanes(grads[rows], own, head_size)
                probs = tile_probs(own_queries, keys, strips[own], starts, tile, scale)
                d_probs = times_trans(own_grads, values[:reach])
                row_delta = jnp.sum(probs * d_probs, axis=1, keepdims=True)
                d_score = (probs * (d_probs - row_delta)).astype(jnp.bfloat16)
                d_strip_ref[own, :, row_count - reach :] += d_score.astype(jnp.float32)
                d_queries += times(d_score, head_lanes(keys[:reach], own, head_size))
                d_keys_ref[:reach, :] += trans_times(d_score, own_queries)
                d_values_ref[:reach, :] += trans_times(probs.astype(jnp.bfloat16), own_grads)
            d_packed_ref[rows, lane_block(block * LANES)] = (d_queries * scale).astype(jnp.bfloat16)
        d_packed_ref[:, lane_block(width + block * LANES)] = (d_keys_ref[...] * scale).astype(
            jnp.bfloat16
        )
        d_packed_ref[:, lane_block(2 * width + block * LANES)] = d_values_ref[...].astype(
            jnp.bfloat16
        )
        for own in range(per_block):
            folded = d_strip_ref[own]
            half = TILE // 2
            while half >= 8:
                folded = folded[:half] + pltpu.roll(folded[half:], row_count - half, 1)
                half //= 2
            row = lax.broadcasted_iota(jnp.int32, folded.shape, 0)
            for bit in (4, 2, 1):
                folded = jnp.where(
                    (row & bit) != 0, pltpu.roll(folded, row_count - bit, 1), folded
                )
            d_base_ref[pl.ds(block * per_block + own, 1), :] = jnp.sum(
                folded, axis=0, keepdims=True
            )


def attention_pull(base, starts, packed, grads, head_size):
    row_count, width = grads.shape
    return pl.pallas_call(
        functools.partial(attention_pull_kernel, head_size),
        out_shape=(
            jax.ShapeDtypeStruct(packed.shape, jnp.bfloat16),
            jax.ShapeDtypeStruct(base.shape, jnp.float32),
        ),
        scratch_shapes=[
            pltpu.VMEM((row_count, LANES), jnp.float32),
            pltpu.VMEM((row_count, LANES), jnp.float32),
            pltpu.VMEM((LANES // head_size, TILE, row_count), jnp.float32),
        ],
        compiler_params=pltpu.CompilerParams(vmem_limit_bytes=VMEM_BYTES),
        cost_estimate=pl.CostEstimate(
            flops=20 * row_count * row_count * width,
            bytes_accessed=14 * row_count * width,
            transcendentals=row_count * row_count * width // head_size,
        ),
        name="attention_pull",
    )(base, starts, packed, grads)


def gelu_parts(values):
    inner = GELU_COEF * (values + 0.044715 * values * values * values)
    bend = jnp.tanh(inner)
    slope = 0.5 * (1.0 + bend) + 0.5 * values * (1.0 - bend * bend) * (
        GELU_COEF * (1.0 + 3.0 * 0.044715 * values * values)
    )
    return 0.5 * values * (1.0 + bend), slope


def expert_rows_kernel(
    chunk,
    own_ref,
    rows_ref,
    grads_ref,
    other_ref,
    router_ref,
    in_ref,
    out_ref,
    produced_ref,
    active_ref,
    d_hidden_ref,
    slot_grad_ref,
    row_grad_ref,
    d_gate_ref,
    produced_sum,
    row_sum,
):
    hidden_width = in_ref.shape[1]
    rows = rows_ref[...]
    logits = times(rows, router_ref[...])
    column = lax.broadcasted_iota(jnp.int32, logits.shape, 1)
    own_logit = jnp.sum(jnp.where(column == own_ref[0], logits, 0.0), axis=1, keepdims=True)
    other_logit = jnp.sum(jnp.where(column == other_ref[...], logits, 0.0), axis=1, keepdims=True)
    peak = jnp.maximum(own_logit, other_logit)
    own_part = jnp.exp(own_logit - peak)
    gate = own_part / (own_part + jnp.exp(other_logit - peak))
    grads = grads_ref[...].astype(jnp.float32)
    slot_grad_ref[...] = (gate * grads).astype(jnp.bfloat16)
    for step in range(hidden_width // chunk):
        columns = slice(step * chunk, (step + 1) * chunk)
        hidden = times(rows_ref[...], in_ref[:, columns])
        active, slope = gelu_parts(hidden)
        active = active.astype(jnp.bfloat16)
        active_ref[:, columns] = active
        d_active = times_trans(slot_grad_ref[...], out_ref[columns, :])
        d_hidden = (slope * d_active).astype(jnp.bfloat16)
        d_hidden_ref[:, columns] = d_hidden
        produced = times(active, out_ref[columns, :])
        back = times_trans(d_hidden, in_ref[:, columns])
        if step == 0:
            produced_sum[...] = produced
            row_sum[...] = back
        else:
            produced_sum[...] += produced
            row_sum[...] += back
    result = produced_sum[...].astype(jnp.bfloat16)
    produced_ref[...] = result
    row_grad_ref[...] = row_sum[...].astype(jnp.bfloat16)
    d_gate_ref[...] = jnp.sum(result.astype(jnp.float32) * grads, axis=1, keepdims=True)


def expert_rows(own, rows, grads, other, router, weight_in, weight_out):
    row_count, width = rows.shape
    hidden_width = weight_in.shape[1]
    block = min(512, row_count)
    chunk = min(768, hidden_width)

    def by_rows(columns):
        return pl.BlockSpec((block, columns), lambda i: (i, 0))

    def whole(shape):
        return pl.BlockSpec(shape, lambda i: (0, 0), pipeline_mode=pl.Buffered(1))

    def like(columns, dtype=jnp.bfloat16):
        return jax.ShapeDtypeStruct((row_count, columns), dtype)

    return pl.pallas_call(
        functools.partial(expert_rows_kernel, chunk),
        grid=(row_count // block,),
        in_specs=[
            pl.BlockSpec(memory_space=pltpu.SMEM),
            by_rows(width),
            by_rows(width),
            by_rows(1),
            whole(router.shape),
            whole(weight_in.shape),
            whole(weight_out.shape),
        ],
        out_specs=(
            by_rows(width),
            by_rows(hidden_width),
            by_rows(hidden_width),
            by_rows(width),
            by_rows(width),
            by_rows(1),
        ),
        out_shape=(
            like(width),
            like(hidden_width),
            like(hidden_width),
            like(width),
            like(width),
            like(1, jnp.float32),
        ),
        scratch_shapes=[
            pltpu.VMEM((block, width), jnp.float32),
            pltpu.VMEM((block, width), jnp.float32),
        ],
        compiler_params=pltpu.CompilerParams(vmem_limit_bytes=VMEM_BYTES),
        cost_estimate=pl.CostEstimate(
            flops=8 * row_count * width * hidden_width,
            bytes_accessed=4 * row_count * (hidden_width + 3 * width) + 4 * width * hidden_width,
            transcendentals=row_count * hidden_width,
        ),
        name="expert_rows",
    )(own, rows, grads, other, router, weight_in, weight_out)


def slot_position(device_ids, experts):
    flat_ids = device_ids.reshape(-1)
    chosen = (flat_ids[:, None] == jnp.arange(experts, dtype=jnp.int32)[None, :]).astype(jnp.int32)
    before = jnp.cumsum(chosen, axis=0, dtype=jnp.int32) - chosen
    position = jnp.sum(before * chosen, axis=1, dtype=jnp.int32)
    return position.reshape(device_ids.shape)


def partner(size, step):
    return [(index, index ^ step) for index in range(size)]


def swap_blocks(blocks, axis, size):
    if size > 8:
        order = lax.axis_index(axis) ^ jnp.arange(size, dtype=jnp.int32)
        placed = jnp.take(jnp.stack(blocks), order, axis=0)
        landed = lax.all_to_all(placed, axis, split_axis=0, concat_axis=0, tiled=True)
        landed = jnp.take(landed, order, axis=0)
        return [landed[step] for step in range(size)]
    return [blocks[0]] + [
        lax.ppermute(blocks[step], axis, partner(size, step)) for step in range(1, size)
    ]


def gather_rep(shard, size):
    near = lax.ppermute(shard, "rep", partner(size, 1))
    far = lax.ppermute(shard, "rep", partner(size, 2))
    far_near = lax.ppermute(far, "rep", partner(size, 1))
    return place_rep([shard, near, far, far_near], lax.axis_index("rep"))


def place_rep(pieces, me):
    height, width = pieces[0].shape
    whole = jnp.zeros((len(pieces) * height, width), pieces[0].dtype)
    for step, piece in enumerate(pieces):
        whole = lax.dynamic_update_slice(whole, piece, ((me ^ step) * height, 0))
    return whole


def scatter_rep(piece_of, size):
    me = lax.axis_index("rep")
    near = lax.ppermute(piece_of(me ^ 1).astype(jnp.bfloat16), "rep", partner(size, 1))
    far_near = lax.ppermute(piece_of(me ^ 3).astype(jnp.bfloat16), "rep", partner(size, 1))
    far = (piece_of(me ^ 2) + far_near.astype(jnp.float32)).astype(jnp.bfloat16)
    far = lax.ppermute(far, "rep", partner(size, 2))
    return piece_of(me) + near.astype(jnp.float32) + far.astype(jnp.float32)


def shards(
    fsdp,
    rep,
    tokens,
    attn_gain,
    qkv_weight,
    out_weight,
    ffn_gain,
    router_weight,
    expert_in,
    expert_out,
    bias_table,
    seq_lengths,
    bucket_map,
    expert_ids,
    cotangent,
):
    both = ("fsdp", "rep")
    row_count, model_width = tokens.shape
    head_count, buckets = bias_table.shape
    head_size = model_width // head_count
    experts = router_weight.shape[1]
    capacity = 4 * row_count // experts
    highest = lax.Precision.HIGHEST
    own_rows = qkv_weight.shape[0]
    extra = -(-(experts + 2) // LANES) * LANES
    me = lax.axis_index("fsdp")

    small = jnp.concatenate(
        [
            router_weight,
            attn_gain[:, None],
            ffn_gain[:, None],
            jnp.zeros((own_rows, extra - experts - 2), jnp.bfloat16),
        ],
        axis=1,
    )
    first_part = lax.all_gather(
        jnp.concatenate([qkv_weight, small], axis=1), both, axis=0, tiled=True
    )
    weight_out = lax.all_gather(out_weight, both, axis=0, tiled=True)
    weight_in = gather_rep(expert_in[0], rep)
    weight_back = gather_rep(expert_out[0], rep)

    position = slot_position(expert_ids, experts)
    slot_ids = (expert_ids ^ me) * capacity + position
    slot_rows = jnp.arange(experts * capacity, dtype=jnp.int32)
    in_first = slot_rows[:, None] == slot_ids[None, :, 0]
    in_second = slot_rows[:, None] == slot_ids[None, :, 1]
    first_map = in_first.astype(jnp.bfloat16)
    second_map = in_second.astype(jnp.bfloat16)
    dispatch = first_map + second_map
    others = jnp.sum(
        jnp.where(in_first, expert_ids[None, :, 1], 0)
        + jnp.where(in_second, expert_ids[None, :, 0], 0),
        axis=1,
    )

    def to_blocks(rows):
        return [rows[step * capacity : (step + 1) * capacity] for step in range(experts)]

    slot_others = jnp.concatenate(swap_blocks(to_blocks(others), "fsdp", fsdp))[:, None]
    sent_grads = times(dispatch, cotangent).astype(jnp.bfloat16)
    slot_dy = jnp.concatenate(swap_blocks(to_blocks(sent_grads), "fsdp", fsdp))

    weight_qkv = first_part[:, : qkv_weight.shape[1]]
    small = first_part[:, qkv_weight.shape[1] :]
    weight_router = small[:, :experts]
    gain_one = small[:, experts].astype(jnp.float32)
    gain_two = small[:, experts + 1].astype(jnp.float32)

    onehot = distance_onehot(bucket_map, row_count, buckets)
    base = lax.dot_general(bias_table, onehot, (((1,), (1,)), ((), ())), precision=highest)
    starts = sequence_starts(seq_lengths[0], row_count)
    inputs = tokens.astype(jnp.float32)
    normed_one = rms_norm(inputs, gain_one).astype(jnp.bfloat16)
    packed = times(normed_one, weight_qkv).astype(jnp.bfloat16)
    attended = attention(base, starts, packed, head_size)
    mixed_rows = inputs + times(attended, weight_out)
    normed_two = rms_norm(mixed_rows, gain_two).astype(jnp.bfloat16)

    sending = times(dispatch, normed_two).astype(jnp.bfloat16)
    arrived = jnp.concatenate(swap_blocks(to_blocks(sending), "fsdp", fsdp))
    produced, active, d_hidden, slot_grad, row_grads, slot_d_gates = expert_rows(
        me[None].astype(jnp.int32), arrived, slot_dy, slot_others, small, weight_in, weight_back
    )
    back_rows = jnp.concatenate(swap_blocks(to_blocks(row_grads), "fsdp", fsdp))
    back_gates = jnp.concatenate(swap_blocks(to_blocks(slot_d_gates[:, 0]), "fsdp", fsdp))
    returned = jnp.concatenate(swap_blocks(to_blocks(produced), "fsdp", fsdp))

    in_rows = expert_in.shape[1]
    out_rows = expert_out.shape[1]
    owned_in = scatter_rep(
        lambda who: trans_times(
            lax.dynamic_slice_in_dim(arrived, who * in_rows, in_rows, 1), d_hidden
        ),
        rep,
    )
    owned_out = scatter_rep(
        lambda who: trans_times(
            lax.dynamic_slice_in_dim(active, who * out_rows, out_rows, 1), slot_grad
        ),
        rep,
    )

    logits = times(normed_two, weight_router)
    choose = expert_ids[:, :, None] == jnp.arange(experts, dtype=jnp.int32)[None, None, :]
    picked = jnp.sum(jnp.where(choose, logits[:, None, :], 0.0), axis=2)
    gate_exp = jnp.exp(picked - jnp.max(picked, axis=1, keepdims=True))
    gate_values = gate_exp / jnp.sum(gate_exp, axis=1, keepdims=True)
    d_gates = jnp.stack(
        [
            jnp.sum(jnp.where(in_first, back_gates[:, None], 0.0), axis=0),
            jnp.sum(jnp.where(in_second, back_gates[:, None], 0.0), axis=0),
        ],
        axis=1,
    )
    gate_mean = jnp.sum(gate_values * d_gates, axis=1, keepdims=True)
    d_picked = gate_values * (d_gates - gate_mean)
    d_logits = jnp.sum(jnp.where(choose, d_picked[:, :, None], 0.0), axis=1).astype(jnp.bfloat16)
    d_normed_two = trans_times(dispatch, back_rows) + times_trans(d_logits, weight_router)
    grad_router = trans_times(normed_two, d_logits)
    unused_two, norm_pull_two = jax.vjp(rms_norm, mixed_rows, gain_two)
    d_mixed_norm, grad_gain_two = norm_pull_two(d_normed_two)
    d_mixed = cotangent.astype(jnp.float32) + d_mixed_norm
    d_branch = d_mixed.astype(jnp.bfloat16)
    grad_out_weight = trans_times(attended, d_branch)
    owned_early = lax.psum_scatter(
        jnp.concatenate(
            [
                grad_out_weight,
                grad_router,
                grad_gain_two[:, None],
                jnp.zeros((model_width, extra - experts - 1), jnp.float32),
            ],
            axis=1,
        ),
        both,
        scatter_dimension=0,
        tiled=True,
    )
    d_attended = times_trans(d_branch, weight_out).astype(jnp.bfloat16)
    d_packed, d_base = attention_pull(base, starts, packed, d_attended, head_size)
    bias_grad = lax.psum(jnp.dot(d_base, onehot, precision=highest), both)
    grad_qkv = trans_times(normed_one, d_packed)
    d_normed_one = times_trans(d_packed, weight_qkv)
    unused_one, norm_pull_one = jax.vjp(rms_norm, inputs, gain_one)
    d_inputs_norm, grad_gain_one = norm_pull_one(d_normed_one)
    token_grad = d_mixed + d_inputs_norm
    owned_late = lax.psum_scatter(
        jnp.concatenate(
            [
                grad_qkv,
                grad_gain_one[:, None],
                jnp.zeros((model_width, LANES - 1), jnp.float32),
            ],
            axis=1,
        ),
        both,
        scatter_dimension=0,
        tiled=True,
    )
    first_out = trans_times(first_map, returned)
    second_out = trans_times(second_map, returned)
    output = mixed_rows + gate_values[:, 0:1] * first_out + gate_values[:, 1:2] * second_out
    qkv_width = qkv_weight.shape[1]
    return (
        output.astype(jnp.bfloat16),
        token_grad,
        owned_late[:, qkv_width],
        owned_late[:, :qkv_width],
        owned_early[:, :model_width],
        owned_early[:, model_width + experts],
        owned_early[:, model_width : model_width + experts],
        owned_in[None],
        owned_out[None],
        bias_grad,
    )


def solution(mesh):
    return jax.shard_map(
        functools.partial(shards, mesh.shape["fsdp"], mesh.shape["rep"]),
        mesh=mesh,
        in_specs=(
            P(("fsdp", "rep"), None),
            P(("fsdp", "rep")),
            P(("fsdp", "rep"), None),
            P(("fsdp", "rep"), None),
            P(("fsdp", "rep")),
            P(("fsdp", "rep"), None),
            P("fsdp", "rep", None),
            P("fsdp", "rep", None),
            P(),
            P(("fsdp", "rep"), None),
            P(),
            P(("fsdp", "rep"), None),
            P(("fsdp", "rep"), None),
        ),
        out_specs=(
            P(("fsdp", "rep"), None),
            P(("fsdp", "rep"), None),
            P(("fsdp", "rep")),
            P(("fsdp", "rep"), None),
            P(("fsdp", "rep"), None),
            P(("fsdp", "rep")),
            P(("fsdp", "rep"), None),
            P("fsdp", "rep", None),
            P("fsdp", "rep", None),
            P(),
        ),
        check_vma=False,
    )
```

time: 1060 us -> 771 us (0.73)
  local copies, waits for them, and re-layouts: 285 us -> 89.1 us
  matrix products: 250 us -> 91.6 us
  Pallas kernels: 0 us -> 97.2 us
  starting transfers between devices: 28.3 us -> 115 us
  blocking collectives: 168 us -> 109 us
  other arithmetic: 55.4 us -> 17 us
  waiting for transfers between devices: 242 us -> 231 us
    all_to_all x4 -> x0, waiting for transfers between devices: 212 us -> none  [the longest x1 72.2 us: shards(): lax.all_to_all(slot_grad, 'fsdp', split_axis=0, concat_axis=0, tiled=True)]
    ppermute x0 -> x54, waiting for transfers between devices: none -> 188 us  [the longest x42 188 us: swap_blocks(): lax.ppermute(blocks[step], axis, partner(size, step))]
    ppermute x0 -> x54, starting transfers between devices: none -> 114 us  [the longest x42 104 us: swap_blocks(): lax.ppermute(blocks[step], axis, partner(size, step))]
    psum x0 -> x1, blocking collectives: none -> 109 us  [shards(): bias_grad = lax.psum(jnp.dot(d_base, onehot, precision=highest), both)]
    pallas_call x0 -> x3, Pallas kernels: none -> 97.2 us  [the longest x1 54.3 us: expert_rows(): pl.pallas_call(functools.partial(expert_rows_kernel, chunk), grid=(row_co...]
    dot_general x22 -> x7, matrix products: 110 us -> 16.4 us  [the longest x5 14.5 us: times(): lax.dot_general(left_side, right_side, (((1,), (0,)), ((), ())), preferre...]
    all_gather x1 -> x0, blocking collectives: 86 us -> none  [shards(): lax.all_gather(router_weight, ('fsdp', 'rep'), axis=0, tiled=True)]
    unnamed x154 -> x162, local copies, waits for them, and re-layouts: 120 us -> 34.7 us
  transfers between devices with their start and end apart: 12 -> 57, of which waited for: 4 -> 20; matrix products, arithmetic and copies ran while one was open for 35% -> 21% of each run, Pallas kernels for 0% -> 6%
where the time goes in v1:
time: 771 us; the launch traced here: 765 us
  waiting for transfers between devices  231 us (30%)
  starting transfers between devices  115 us (15%)
  blocking collectives  109 us (14%)
  Pallas kernels  97.2 us (13%)
  matrix products  91.6 us (12%)
  local copies, waits for them, and re-layouts  89.1 us (12%)
  other arithmetic  17 us (2%)
  between operations  14.9 us (2%)
    ppermute x42, waiting for transfers between devices, swap_blocks(): lax.ppermute(blocks[step], axis, partner(size, step))  188 us
    psum x1, blocking collectives, shards(): bias_grad = lax.psum(jnp.dot(d_base, onehot, precision=highest), both)  109 us
    ppermute x42, starting transfers between devices, swap_blocks(): lax.ppermute(blocks[step], axis, partner(size, step))  104 us
    dot_general x14, matrix products, trans_times(): lax.dot_general(left_side, right_side, (((0,), (0,)), ((), ())), preferre...  69.2 us
    pallas_call x1, Pallas kernels, expert_rows(): pl.pallas_call(functools.partial(expert_rows_kernel, chunk), grid=(row_co...  54.3 us
    unnamed x4, waiting for transfers between devices  42.8 us
    unnamed x162, local copies, waits for them, and re-layouts  34.7 us
    pallas_call x1, Pallas kernels, attention_pull(): pl.pallas_call(functools.partial(attention_pull_kernel, head_size), out_s...  29.2 us
  transfers between devices with their start and end apart: 57, of which 20 were waited for; matrix products, arithmetic and copies ran while one was open for 21% of the time, Pallas kernels for 6%

profile of v1, /device:TPU:0, one launch (start us, length us, event | category | flops | bytes accessed | tf_op | source)
XLA Modules:
  0.0 764.7 jit_solution(8611340091063905483)
XLA Ops:
  12.4 2.3 reduce-window.19
  18.8 2.9 collective-permute-start.14
  23.4 3.3 convolution_convert_fusion.3
  33.6 2.4 broadcast_in_dim.175
  37.1 2.8 broadcast_in_dim.174
  44.0 2.6 collective-permute-start.17
  47.6 2.5 collective-permute-start.19
  50.0 2.3 collective-permute-start.20
  53.5 2.5 collective-permute-start.10
  61.2 13.9 %collective-permute-done.9 = bf16[256,768]{1,0:T(8,128)(2,1)S(1)} collective-permute-done((bf16[256,768]{1,0:T(8,128)(2,1)}, bf16[256,768]{1,0:T(8,128)(2,1)S(1)}, u32[]{:S(2)}, u32[]{:S(2)}) %collective-permute-start.9) | collective-permute-done | bytes 393248 | tf_op jit(solution)/shard_map/ppermute | solution.py:355
  75.1 22.2 %collective-permute-done.10 = bf16[256,768]{1,0:T(8,128)(2,1)S(1)} collective-permute-done((bf16[256,768]{1,0:T(8,128)(2,1)}, bf16[256,768]{1,0:T(8,128)(2,1)S(1)}, u32[]{:S(2)}, u32[]{:S(2)}) %collective-permute-start.10) | collective-permute-done | bytes 393248 | tf_op jit(solution)/shard_map/ppermute | solution.py:355
  99.4 11.4 %collective-permute-done.11 = bf16[256,768]{1,0:T(8,128)(2,1)S(1)} collective-permute-done((bf16[256,768]{1,0:T(8,128)(2,1)}, bf16[256,768]{1,0:T(8,128)(2,1)S(1)}, u32[]{:S(2)}, u32[]{:S(2)}) %collective-permute-start.11) | collective-permute-done | bytes 393248 | tf_op jit(solution)/shard_map/ppermute | solution.py:355
  125.3 5.4 collective-permute-done.13
  131.5 2.4 constant_dynamic-update-slice_fusion.46
  133.9 2.4 constant_dynamic-update-slice_fusion.45
  136.3 2.3 constant_dynamic-update-slice_fusion.50
  138.6 2.4 constant_dynamic-update-slice_fusion.49
  144.6 5.5 convolution_convert_fusion.packed_ref
  150.1 13.7 %attention.1 = bf16[512,768]{1,0:T(8,128)(2,1)} custom-call(f32[12,512]{1,0:T(8,128)} %convolution_bitcast_fusion.base_ref, s32[512,1]{1,0:T(8,128)} %copy.74.starts_ref, bf16[512,2304]{1,0:T(8,128)(2,1)} %convolution_convert_fusion.packed_ref), custom_call_target="tpu_custom_call" | custom-call | flops 1610612736 | bytes 3145728 | tf_op jit(solution)/shard_map/attention/pallas_call | solution.py:116
  163.8 2.4 multiply_reduce_fusion.2
  166.9 2.1 convolution_convert_fusion.4
  171.2 6.6 collective-permute-start.1
  178.0 2.4 collective-permute-start.3
  189.6 12.4 %collective-permute-done.1 = bf16[256,768]{1,0:T(8,128)(2,1)} collective-permute-done((bf16[256,768]{1,0:T(8,128)(2,1)}, bf16[256,768]{1,0:T(8,128)(2,1)}, u32[]{:S(2)}, u32[]{:S(2)}) %collective-permute-start.1) | collective-permute-done | bytes 393248 | tf_op jit(solution)/shard_map/ppermute | solution.py:355
  202.0 2.2 collective-permute-start.6
  211.3 22.8 %collective-permute-done.4 = bf16[256,768]{1,0:T(8,128)(2,1)} collective-permute-done((bf16[256,768]{1,0:T(8,128)(2,1)}, bf16[256,768]{1,0:T(8,128)(2,1)}, u32[]{:S(2)}, u32[]{:S(2)}) %collective-permute-start.4) | collective-permute-done | bytes 393248 | tf_op jit(solution)/shard_map/ppermute | solution.py:355
  237.4 54.3 %expert_rows.1 = (bf16[2048,768]{1,0:T(8,128)(2,1)}, bf16[2048,3072]{1,0:T(8,128)(2,1)}, bf16[2048,3072]{1,0:T(8,128)(2,1)}, bf16[2048,768]{1,0:T(8,128)(2,1)}, ...) custom-call(s32[1]{0:T(128)} %bitcast.8.own_ref, bf16[2048,768]{1,0:T(8,128)(2,1)} %constant_dynamic-update-slice_fusion.rows_ref, ...), custom_call_target="tpu_custom_call" | custom-call | flops 38654705664 | bytes 53477376 | tf_op jit(solution)/shard_map/expert_rows/pallas_call | solution.py:293
  291.7 6.7 fusion.43
  298.5 5.8 fusion.46
  304.3 3.8 convolution_convert_fusion.1
  308.2 3.8 convolution_convert_fusion.2
  313.1 11.0 %collective-permute-start.35 = (bf16[256,768]{1,0:T(8,128)(2,1)S(1)}, bf16[256,768]{1,0:T(8,128)(2,1)S(1)}, u32[]{:S(2)}, u32[]{:S(2)}) collective-permute-start(bf16[256,768]{1,0:T(8,128)(2,1)S(1)} %get-tuple-element.103), channel_id=1, source_target_pairs={{0,8},{4,12},{8,0},{12,4},{16,24},{20,28},{24,16},{28,20},{1,9},{5... | collective-permute-start | bytes 1179656 | tf_op jit(solution)/shard_map/ppermute | solution.py:355
  328.3 6.1 collective-permute-start.42
  334.5 7.6 collective-permute-done.42
  344.0 2.5 collective-permute-done.43
  348.3 2.7 collective-permute-done.44
  351.0 2.5 collective-permute-start.45
  353.5 2.8 collective-permute-done.45
  357.8 3.9 collective-permute-done.46
  361.7 2.3 collective-permute-start.47
  364.0 4.1 collective-permute-done.47
  370.6 3.2 collective-permute-start.38
  375.9 2.5 collective-permute-start.40
  378.5 29.5 %collective-permute-done.37 = bf16[256,768]{1,0:T(8,128)(2,1)S(1)} collective-permute-done((bf16[256,768]{1,0:T(8,128)(2,1)S(1)}, bf16[256,768]{1,0:T(8,128)(2,1)S(1)}, u32[]{:S(2)}, u32[]{:S(2)}) %collective-permute-start.37) | collective-permute-done | bytes 393248 | tf_op jit(solution)/shard_map/ppermute | solution.py:355
  408.7 7.8 %collective-permute-done.38 = bf16[256,768]{1,0:T(8,128)(2,1)S(1)} collective-permute-done((bf16[256,768]{1,0:T(8,128)(2,1)S(1)}, bf16[256,768]{1,0:T(8,128)(2,1)S(1)}, u32[]{:S(2)}, u32[]{:S(2)}) %collective-permute-start.38) | collective-permute-done | bytes 393248 | tf_op jit(solution)/shard_map/ppermute | solution.py:355
  416.6 8.9 %collective-permute-start.29 = (bf16[256,768]{1,0:T(8,128)(2,1)}, bf16[256,768]{1,0:T(8,128)(2,1)}, u32[]{:S(2)}, u32[]{:S(2)}) collective-permute-start(bf16[256,768]{1,0:T(8,128)(2,1)} %get-tuple-element.110), channel_id=1, source_target_pairs={{0,12},{4,8},{8,4},{12,0},{16,28},{20,24},{24,20},{28,16},{1,13},{... | collective-permute-start | bytes 1179656 | tf_op jit(solution)/shard_map/ppermute | solution.py:355
  425.6 13.6 %collective-permute-start.30 = (bf16[256,768]{1,0:T(8,128)(2,1)}, bf16[256,768]{1,0:T(8,128)(2,1)}, u32[]{:S(2)}, u32[]{:S(2)}) collective-permute-start(bf16[256,768]{1,0:T(8,128)(2,1)} %get-tuple-element.109), channel_id=1, source_target_pairs={{0,16},{4,20},{8,24},{12,28},{16,0},{20,4},{24,8},{28,12},{1,17},{... | collective-permute-start | bytes 1179656 | tf_op jit(solution)/shard_map/ppermute | solution.py:355
  439.3 2.4 multiply_reduce_fusion
  445.4 29.2 %attention_pull.1 = (bf16[512,2304]{1,0:T(8,128)(2,1)}, f32[12,512]{1,0:T(8,128)}) custom-call(f32[12,512]{1,0:T(8,128)} %convolution_bitcast_fusion.base_ref, s32[512,1]{1,0:T(8,128)} %copy.74.starts_ref, bf16[512,2304]{1,0:T(8,128)(2,1)} %convolution_convert_fusion.packed_ref, bf16[512,768]{1,0:T(8,128)(2,1)} %convolution_convert_fusion.5.grad_ref), custom_call_target="tpu_custom_call" | custom-call | flops 4026531840 | bytes 5505024 | tf_op jit(solution)/shard_map/attention_pull/pallas_call | solution.py:196
  474.6 6.8 fusion.62
  481.4 3.9 fusion.34
  488.1 8.8 %concatenate.38 = f32[768,2432]{1,0:T(8,128)} concatenate(f32[768,2304]{1,0:T(8,128)} %fusion.62, f32[768,1]{1,0:T(8,128)S(1)} %broadcast_in_dim.187, f32[768,127]{1,0:T(8,128)S(1)} %broadcast_in_dim.182), dimensions={1} | concatenate | bytes 14942208 | tf_op jit(solution)/shard_map/concatenate | solution.py:533
  508.0 28.1 %collective-permute-done.31 = bf16[256,768]{1,0:T(8,128)(2,1)S(1)} collective-permute-done((bf16[256,768]{1,0:T(8,128)(2,1)}, bf16[256,768]{1,0:T(8,128)(2,1)S(1)}, u32[]{:S(2)}, u32[]{:S(2)}) %collective-permute-start.31) | collective-permute-done | bytes 393248 | tf_op jit(solution)/shard_map/ppermute | solution.py:355
  540.6 8.1 %collective-permute-done.33 = bf16[256,768]{1,0:T(8,128)(2,1)S(1)} collective-permute-done((bf16[256,768]{1,0:T(8,128)(2,1)S(1)}, bf16[256,768]{1,0:T(8,128)(2,1)S(1)}, u32[]{:S(2)}, u32[]{:S(2)}) %collective-permute-start.33) | collective-permute-done | bytes 393248 | tf_op jit(solution)/shard_map/ppermute | solution.py:355
  549.6 4.1 fusion.2
  553.7 5.1 add_convert_fusion.1
  558.8 5.7 add_convert_fusion
  564.5 6.9 collective-permute-start.53
  571.5 5.2 fusion.6
  576.7 108.7 %psum.7 = f32[12,32]{1,0:T(8,128)} all-reduce(f32[12,32]{1,0:T(8,128)} %fusion.59), channel_id=1, replica_groups=mesh['fsdp'=8,'rep'=4] {'fsdp','rep'}, use_global_device_ids=true, to_apply=%region_22.23 | all-reduce | flops 384 | bytes 3072 | tf_op jit(solution)/shard_map/psum | solution.py:526
  685.4 3.1 fusion.36
  688.6 6.8 add_bitcast_fusion
  695.4 12.0 %fusion.5 = f32[1,192,3072]{2,1,0:T(8,128)} fusion(bf16[2048,3072]{1,0:T(8,128)(2,1)} %get-tuple-element.22, bf16[192,3072]{1,0:T(8,128)(2,1)} %collective-permute-done.50, bf16[192,3072]{1,0:T(8,128)(2,1)} %collective-permute-done.48, bf16[2048,768]{1,0:T(8,128)(2,1)} %constant_dynamic-update-slice_fusion.rows_ref, s32[]{:T(128)S(6)} %select_n.67), kind=kOutput, calls=%fused_computation.13 | convolution fusion | flops 2418278400 | bytes 18350084 | tf_op jit(solution)/shard_map/dot_general | solution.py:39
  707.4 42.8 %all-reduce.5.cloned.1.call-done = (f32[768,2432]{1,0:T(8,128)}, f32[768,896]{0,1:T(8,128)}) async-done(((f32[768,2432]{1,0:T(8,128)}, f32[768,896]{0,1:T(8,128)}), (f32[768,2432]{1,0:T(8,128)}, f32[768,896]{0,1:T(8,128)})) %all-reduce.5.cloned.1.call-update) | async-done | bytes 10223632
  (324 shorter events, 120.4 us)
Async XLA Ops:
  7.2 136.1 %all-gather.3.cloned.1.call-start = ((), (), s32[]{:S(2)}) async-start(), calls=%async_computation | async-start | bytes 3852288 | tf_op jit(solution)/shard_map/all_gather | solution.py:420
  11.2 152.7 %all-gather.5.cloned.1.call-start = ((), (), s32[]{:S(2)}) async-start(), calls=%async_computation.1 | async-start | bytes 1216512 | tf_op jit(solution)/shard_map/all_gather | solution.py:423
  18.8 25.2 %collective-permute-start.14 = (s32[256]{0:T(256)}, s32[256]{0:T(256)}, u32[]{:S(2)}, u32[]{:S(2)}) collective-permute-start(s32[256]{0:T(256)} %get-tuple-element.136), channel_id=1, source_target_pairs={{0,4},{4,0},{8,12},{12,8},{16,20},{20,16},{24,28},{28,24},{1,5},{5... | collective-permute-start | bytes 3080 | tf_op jit(solution)/shard_map/ppermute | solution.py:355
  21.8 24.8 %collective-permute-start.15 = (s32[256]{0:T(256)}, s32[256]{0:T(256)}, u32[]{:S(2)}, u32[]{:S(2)}) collective-permute-start(s32[256]{0:T(256)} %get-tuple-element.135), channel_id=1, source_target_pairs={{0,8},{4,12},{8,0},{12,4},{16,24},{20,28},{24,16},{28,20},{1,9},{5... | collective-permute-start | bytes 3080 | tf_op jit(solution)/shard_map/ppermute | solution.py:355
  23.3 24.2 %collective-permute-start.16 = (s32[256]{0:T(256)}, s32[256]{0:T(256)}, u32[]{:S(2)}, u32[]{:S(2)}) collective-permute-start(s32[256]{0:T(256)} %get-tuple-element.134), channel_id=1, source_target_pairs={{0,12},{4,8},{8,4},{12,0},{16,28},{20,24},{24,20},{28,16},{1,13},{... | collective-permute-start | bytes 3080 | tf_op jit(solution)/shard_map/ppermute | solution.py:355
  28.2 30.6 %collective-permute-start.7 = (bf16[256,768]{1,0:T(8,128)(2,1)}, bf16[256,768]{1,0:T(8,128)(2,1)}, u32[]{:S(2)}, u32[]{:S(2)}) collective-permute-start(bf16[256,768]{1,0:T(8,128)(2,1)} %get-tuple-element.120), channel_id=1, source_target_pairs={{0,4},{4,0},{8,12},{12,8},{16,20},{20,16},{24,28},{28,24},{1,5},{5... | collective-permute-start | bytes 1179656 | tf_op jit(solution)/shard_map/ppermute | solution.py:355
  30.1 29.9 %collective-permute-start.8 = (bf16[256,768]{1,0:T(8,128)(2,1)}, bf16[256,768]{1,0:T(8,128)(2,1)}, u32[]{:S(2)}, u32[]{:S(2)}) collective-permute-start(bf16[256,768]{1,0:T(8,128)(2,1)} %get-tuple-element.119), channel_id=1, source_target_pairs={{0,8},{4,12},{8,0},{12,4},{16,24},{20,28},{24,16},{28,20},{1,9},{5... | collective-permute-start | bytes 1179656 | tf_op jit(solution)/shard_map/ppermute | solution.py:355
  31.7 718.4 %all-reduce.5.cloned.1.call-start = ((), (), s32[]{:S(2)}) async-start(), calls=%async_computation.2 | async-start | bytes 20447232
  44.0 6.0 collective-permute-start.17
  46.6 5.7 collective-permute-start.18
  47.6 5.9 collective-permute-start.19
  50.0 6.6 collective-permute-start.20
  52.3 22.7 %collective-permute-start.9 = (bf16[256,768]{1,0:T(8,128)(2,1)}, bf16[256,768]{1,0:T(8,128)(2,1)S(1)}, u32[]{:S(2)}, u32[]{:S(2)}) collective-permute-start(bf16[256,768]{1,0:T(8,128)(2,1)} %get-tuple-element.118), channel_id=1, source_target_pairs={{0,12},{4,8},{8,4},{12,0},{16,28},{20,24},{24,20},{28,16},{1,13},{... | collective-permute-start | bytes 1179656 | tf_op jit(solution)/shard_map/ppermute | solution.py:355
  53.5 43.8 %collective-permute-start.10 = (bf16[256,768]{1,0:T(8,128)(2,1)}, bf16[256,768]{1,0:T(8,128)(2,1)S(1)}, u32[]{:S(2)}, u32[]{:S(2)}) collective-permute-start(bf16[256,768]{1,0:T(8,128)(2,1)} %get-tuple-element.117), channel_id=1, source_target_pairs={{0,16},{4,20},{8,24},{12,28},{16,0},{20,4},{24,8},{28,12},{1,17},{... | collective-permute-start | bytes 1179656 | tf_op jit(solution)/shard_map/ppermute | solution.py:355
  56.7 66.3 %collective-permute-start.25 = (bf16[768,768]{1,0:T(8,128)(2,1)S(1)}, bf16[768,768]{1,0:T(8,128)(2,1)}, u32[]{:S(2)}, u32[]{:S(2)}) collective-permute-start(bf16[768,768]{1,0:T(8,128)(2,1)S(1)} %bitcast.75), channel_id=1, source_target_pairs={{0,2},{1,3},{2,0},{3,1},{4,6},{5,7},{6,4},{7,5},{8,10},{9,11},{10,... | collective-permute-start | bytes 3538952 | tf_op jit(solution)/shard_map/ppermute | solution.py:361
  58.9 51.9 %collective-permute-start.11 = (bf16[256,768]{1,0:T(8,128)(2,1)}, bf16[256,768]{1,0:T(8,128)(2,1)S(1)}, u32[]{:S(2)}, u32[]{:S(2)}) collective-permute-start(bf16[256,768]{1,0:T(8,128)(2,1)} %get-tuple-element.116), channel_id=1, source_target_pairs={{0,20},{4,16},{8,28},{12,24},{16,4},{20,0},{24,12},{28,8},{1,21},{... | collective-permute-start | bytes 1179656 | tf_op jit(solution)/shard_map/ppermute | solution.py:355
  60.0 64.8 %collective-permute-start.22 = (bf16[192,3072]{1,0:T(8,128)(2,1)S(1)}, bf16[192,3072]{1,0:T(8,128)(2,1)}, u32[]{:S(2)}, u32[]{:S(2)}) collective-permute-start(bf16[192,3072]{1,0:T(8,128)(2,1)S(1)} %bitcast.77), channel_id=1, source_target_pairs={{0,2},{1,3},{2,0},{3,1},{4,6},{5,7},{6,4},{7,5},{8,10},{9,11},{10,... | collective-permute-start | bytes 3538952 | tf_op jit(solution)/shard_map/ppermute | solution.py:361
  75.1 56.4 %collective-permute-start.24 = (bf16[768,768]{1,0:T(8,128)(2,1)S(1)}, bf16[768,768]{1,0:T(8,128)(2,1)}, u32[]{:S(2)}, u32[]{:S(2)}) collective-permute-start(bf16[768,768]{1,0:T(8,128)(2,1)S(1)} %bitcast.76), channel_id=1, source_target_pairs={{0,1},{1,0},{2,3},{3,2},{4,5},{5,4},{6,7},{7,6},{8,9},{9,8},{10,11... | collective-permute-start | bytes 3538952 | tf_op jit(solution)/shard_map/ppermute | solution.py:360
  97.3 19.2 %collective-permute-start.12 = (bf16[256,768]{1,0:T(8,128)(2,1)}, bf16[256,768]{1,0:T(8,128)(2,1)}, u32[]{:S(2)}, u32[]{:S(2)}) collective-permute-start(bf16[256,768]{1,0:T(8,128)(2,1)} %get-tuple-element.115), channel_id=1, source_target_pairs={{0,24},{4,28},{8,16},{12,20},{16,8},{20,12},{24,0},{28,4},{1,25},{... | collective-permute-start | bytes 1179656 | tf_op jit(solution)/shard_map/ppermute | solution.py:355
  110.8 25.4 %collective-permute-start.21 = (bf16[192,3072]{1,0:T(8,128)(2,1)S(1)}, bf16[192,3072]{1,0:T(8,128)(2,1)}, u32[]{:S(2)}, u32[]{:S(2)}) collective-permute-start(bf16[192,3072]{1,0:T(8,128)(2,1)S(1)} %bitcast.78), channel_id=1, source_target_pairs={{0,1},{1,0},{2,3},{3,2},{4,5},{5,4},{6,7},{7,6},{8,9},{9,8},{10,11... | collective-permute-start | bytes 3538952 | tf_op jit(solution)/shard_map/ppermute | solution.py:360
  116.5 14.2 %collective-permute-start.13 = (bf16[256,768]{1,0:T(8,128)(2,1)S(1)}, bf16[256,768]{1,0:T(8,128)(2,1)S(1)}, u32[]{:S(2)}, u32[]{:S(2)}) collective-permute-start(bf16[256,768]{1,0:T(8,128)(2,1)S(1)} %get-tuple-element.114), channel_id=1, source_target_pairs={{0,28},{4,24},{8,20},{12,16},{16,12},{20,8},{24,4},{28,0},{1,29},{... | collective-permute-start | bytes 1179656 | tf_op jit(solution)/shard_map/ppermute | solution.py:355
  123.0 18.0 %collective-permute-start.26 = (bf16[768,768]{1,0:T(8,128)(2,1)}, bf16[768,768]{1,0:T(8,128)(2,1)S(1)}, u32[]{:S(2)}, u32[]{:S(2)}) collective-permute-start(bf16[768,768]{1,0:T(8,128)(2,1)} %collective-permute-done.25), channel_id=1, source_target_pairs={{0,1},{1,0},{2,3},{3,2},{4,5},{5,4},{6,7},{7,6},{8,9},{9,8},{10,11... | collective-permute-start | bytes 3538952 | tf_op jit(solution)/shard_map/ppermute | solution.py:362
  124.8 17.3 %collective-permute-start.23 = (bf16[192,3072]{1,0:T(8,128)(2,1)}, bf16[192,3072]{1,0:T(8,128)(2,1)S(1)}, u32[]{:S(2)}, u32[]{:S(2)}) collective-permute-start(bf16[192,3072]{1,0:T(8,128)(2,1)} %collective-permute-done.22), channel_id=1, source_target_pairs={{0,1},{1,0},{2,3},{3,2},{4,5},{5,4},{6,7},{7,6},{8,9},{9,8},{10,11... | collective-permute-start | bytes 3538952 | tf_op jit(solution)/shard_map/ppermute | solution.py:362
  166.3 273.0 %copy-start.4 = (f32[512,768]{1,0:T(8,128)}, f32[512,768]{1,0:T(8,128)S(1)}, u32[]{:S(2)}) copy-start(f32[512,768]{1,0:T(8,128)S(1)} %get-tuple-element.143) | copy-start | bytes 4718596
  170.6 15.2 %collective-permute-start = (bf16[256,768]{1,0:T(8,128)(2,1)}, bf16[256,768]{1,0:T(8,128)(2,1)}, u32[]{:S(2)}, u32[]{:S(2)}) collective-permute-start(bf16[256,768]{1,0:T(8,128)(2,1)} %get-tuple-element.128), channel_id=1, source_target_pairs={{0,4},{4,0},{8,12},{12,8},{16,20},{20,16},{24,28},{28,24},{1,5},{5... | collective-permute-start | bytes 1179656 | tf_op jit(solution)/shard_map/ppermute | solution.py:355
  171.2 30.8 %collective-permute-start.1 = (bf16[256,768]{1,0:T(8,128)(2,1)}, bf16[256,768]{1,0:T(8,128)(2,1)}, u32[]{:S(2)}, u32[]{:S(2)}) collective-permute-start(bf16[256,768]{1,0:T(8,128)(2,1)} %get-tuple-element.127), channel_id=1, source_target_pairs={{0,8},{4,12},{8,0},{12,4},{16,24},{20,28},{24,16},{28,20},{1,9},{5... | collective-permute-start | bytes 1179656 | tf_op jit(solution)/shard_map/ppermute | solution.py:355
  177.8 30.0 %collective-permute-start.2 = (bf16[256,768]{1,0:T(8,128)(2,1)}, bf16[256,768]{1,0:T(8,128)(2,1)}, u32[]{:S(2)}, u32[]{:S(2)}) collective-permute-start(bf16[256,768]{1,0:T(8,128)(2,1)} %get-tuple-element.126), channel_id=1, source_target_pairs={{0,12},{4,8},{8,4},{12,0},{16,28},{20,24},{24,20},{28,16},{1,13},{... | collective-permute-start | bytes 1179656 | tf_op jit(solution)/shard_map/ppermute | solution.py:355
  178.0 31.5 %collective-permute-start.3 = (bf16[256,768]{1,0:T(8,128)(2,1)}, bf16[256,768]{1,0:T(8,128)(2,1)}, u32[]{:S(2)}, u32[]{:S(2)}) collective-permute-start(bf16[256,768]{1,0:T(8,128)(2,1)} %get-tuple-element.125), channel_id=1, source_target_pairs={{0,16},{4,20},{8,24},{12,28},{16,0},{20,4},{24,8},{28,12},{1,17},{... | collective-permute-start | bytes 1179656 | tf_op jit(solution)/shard_map/ppermute | solution.py:355
  180.4 53.7 %collective-permute-start.4 = (bf16[256,768]{1,0:T(8,128)(2,1)}, bf16[256,768]{1,0:T(8,128)(2,1)}, u32[]{:S(2)}, u32[]{:S(2)}) collective-permute-start(bf16[256,768]{1,0:T(8,128)(2,1)} %get-tuple-element.124), channel_id=1, source_target_pairs={{0,20},{4,16},{8,28},{12,24},{16,4},{20,0},{24,12},{28,8},{1,21},{... | collective-permute-start | bytes 1179656 | tf_op jit(solution)/shard_map/ppermute | solution.py:355
  185.8 50.1 %collective-permute-start.5 = (bf16[256,768]{1,0:T(8,128)(2,1)}, bf16[256,768]{1,0:T(8,128)(2,1)S(1)}, u32[]{:S(2)}, u32[]{:S(2)}) collective-permute-start(bf16[256,768]{1,0:T(8,128)(2,1)} %get-tuple-element.123), channel_id=1, source_target_pairs={{0,24},{4,28},{8,16},{12,20},{16,8},{20,12},{24,0},{28,4},{1,25},{... | collective-permute-start | bytes 1179656 | tf_op jit(solution)/shard_map/ppermute | solution.py:355
  202.0 34.7 %collective-permute-start.6 = (bf16[256,768]{1,0:T(8,128)(2,1)S(1)}, bf16[256,768]{1,0:T(8,128)(2,1)S(1)}, u32[]{:S(2)}, u32[]{:S(2)}) collective-permute-start(bf16[256,768]{1,0:T(8,128)(2,1)S(1)} %get-tuple-element.122), channel_id=1, source_target_pairs={{0,28},{4,24},{8,20},{12,16},{16,12},{20,8},{24,4},{28,0},{1,29},{... | collective-permute-start | bytes 1179656 | tf_op jit(solution)/shard_map/ppermute | solution.py:355
  312.0 376.6 %collective-permute-start.51 = (bf16[768,768]{1,0:T(8,128)(2,1)}, bf16[768,768]{1,0:T(8,128)(2,1)}, u32[]{:S(2)}, u32[]{:S(2)}) collective-permute-start(bf16[768,768]{1,0:T(8,128)(2,1)} %fusion.43), channel_id=1, source_target_pairs={{0,1},{1,0},{2,3},{3,2},{4,5},{5,4},{6,7},{7,6},{8,9},{9,8},{10,11... | collective-permute-start | bytes 3538952 | tf_op jit(solution)/shard_map/ppermute | solution.py:376
  312.2 58.4 %collective-permute-start.34 = (bf16[256,768]{1,0:T(8,128)(2,1)S(1)}, bf16[256,768]{1,0:T(8,128)(2,1)S(1)}, u32[]{:S(2)}, u32[]{:S(2)}) collective-permute-start(bf16[256,768]{1,0:T(8,128)(2,1)S(1)} %get-tuple-element.104), channel_id=1, source_target_pairs={{0,4},{4,0},{8,12},{12,8},{16,20},{20,16},{24,28},{28,24},{1,5},{5... | collective-permute-start | bytes 1179656 | tf_op jit(solution)/shard_map/ppermute | solution.py:355
  313.1 60.7 %collective-permute-start.35 = (bf16[256,768]{1,0:T(8,128)(2,1)S(1)}, bf16[256,768]{1,0:T(8,128)(2,1)S(1)}, u32[]{:S(2)}, u32[]{:S(2)}) collective-permute-start(bf16[256,768]{1,0:T(8,128)(2,1)S(1)} %get-tuple-element.103), channel_id=1, source_target_pairs={{0,8},{4,12},{8,0},{12,4},{16,24},{20,28},{24,16},{28,20},{1,9},{5... | collective-permute-start | bytes 1179656 | tf_op jit(solution)/shard_map/ppermute | solution.py:355
  324.1 51.8 %collective-permute-start.36 = (bf16[256,768]{1,0:T(8,128)(2,1)S(1)}, bf16[256,768]{1,0:T(8,128)(2,1)S(1)}, u32[]{:S(2)}, u32[]{:S(2)}) collective-permute-start(bf16[256,768]{1,0:T(8,128)(2,1)S(1)} %get-tuple-element.102), channel_id=1, source_target_pairs={{0,12},{4,8},{8,4},{12,0},{16,28},{20,24},{24,20},{28,16},{1,13},{... | collective-permute-start | bytes 1179656 | tf_op jit(solution)/shard_map/ppermute | solution.py:355
  324.7 3.6 collective-permute-start.41
  326.0 43.3 %copy-start.29 = (f32[512]{0:T(512)S(1)}, f32[512]{0:T(512)}, u32[]{:S(2)}) copy-start(f32[512]{0:T(512)} %reduce_max.19) | copy-start | bytes 6148
  326.0 43.4 %copy-start.23 = (bf16[768,2432]{1,0:T(8,128)(2,1)S(1)}, bf16[768,2432]{1,0:T(8,128)(2,1)}, u32[]{:S(2)}) copy-start(bf16[768,2432]{1,0:T(8,128)(2,1)} %all-gather.3.cloned.1.call-done) | copy-start | bytes 11206660
  328.3 13.7 %collective-permute-start.42 = (f32[256]{0:T(256)S(1)}, f32[256]{0:T(256)S(1)}, u32[]{:S(2)}, u32[]{:S(2)}) collective-permute-start(f32[256]{0:T(256)S(1)} %get-tuple-element.87), channel_id=1, source_target_pairs={{0,8},{4,12},{8,0},{12,4},{16,24},{20,28},{24,16},{28,20},{1,9},{5... | collective-permute-start | bytes 3080 | tf_op jit(solution)/shard_map/ppermute | solution.py:355
  342.0 4.5 collective-permute-start.43
  346.5 4.5 collective-permute-start.44
  351.0 5.4 collective-permute-start.45
  356.3 5.4 collective-permute-start.46
  361.7 6.4 collective-permute-start.47
  368.1 39.9 %collective-permute-start.37 = (bf16[256,768]{1,0:T(8,128)(2,1)S(1)}, bf16[256,768]{1,0:T(8,128)(2,1)S(1)}, u32[]{:S(2)}, u32[]{:S(2)}) collective-permute-start(bf16[256,768]{1,0:T(8,128)(2,1)S(1)} %get-tuple-element.101), channel_id=1, source_target_pairs={{0,16},{4,20},{8,24},{12,28},{16,0},{20,4},{24,8},{28,12},{1,17},{... | collective-permute-start | bytes 1179656 | tf_op jit(solution)/shard_map/ppermute | solution.py:355
  369.8 69.4 %copy-start.26 = (f32[768]{0:T(1024)S(1)}, f32[768]{0:T(1024)}, u32[]{:S(2)}) copy-start(f32[768]{0:T(1024)} %copy-done.25) | copy-start | bytes 9220
  369.8 69.4 %copy-start.31 = (f32[512]{0:T(512)S(1)}, f32[512]{0:T(512)}, u32[]{:S(2)}) copy-start(f32[512]{0:T(512)} %copy-done.30) | copy-start | bytes 6148
  370.6 45.9 %collective-permute-start.38 = (bf16[256,768]{1,0:T(8,128)(2,1)S(1)}, bf16[256,768]{1,0:T(8,128)(2,1)S(1)}, u32[]{:S(2)}, u32[]{:S(2)}) collective-permute-start(bf16[256,768]{1,0:T(8,128)(2,1)S(1)} %get-tuple-element.100), channel_id=1, source_target_pairs={{0,20},{4,16},{8,28},{12,24},{16,4},{20,0},{24,12},{28,8},{1,21},{... | collective-permute-start | bytes 1179656 | tf_op jit(solution)/shard_map/ppermute | solution.py:355
  373.8 42.8 %collective-permute-start.39 = (bf16[256,768]{1,0:T(8,128)(2,1)S(1)}, bf16[256,768]{1,0:T(8,128)(2,1)S(1)}, u32[]{:S(2)}, u32[]{:S(2)}) collective-permute-start(bf16[256,768]{1,0:T(8,128)(2,1)S(1)} %get-tuple-element.99), channel_id=1, source_target_pairs={{0,24},{4,28},{8,16},{12,20},{16,8},{20,12},{24,0},{28,4},{1,25},{... | collective-permute-start | bytes 1179656 | tf_op jit(solution)/shard_map/ppermute | solution.py:355
  375.9 49.6 %collective-permute-start.40 = (bf16[256,768]{1,0:T(8,128)(2,1)S(1)}, bf16[256,768]{1,0:T(8,128)(2,1)S(1)}, u32[]{:S(2)}, u32[]{:S(2)}) collective-permute-start(bf16[256,768]{1,0:T(8,128)(2,1)S(1)} %get-tuple-element.98), channel_id=1, source_target_pairs={{0,28},{4,24},{8,20},{12,16},{16,12},{20,8},{24,4},{28,0},{1,29},{... | collective-permute-start | bytes 1179656 | tf_op jit(solution)/shard_map/ppermute | solution.py:355
  408.0 89.0 %collective-permute-start.27 = (bf16[256,768]{1,0:T(8,128)(2,1)}, bf16[256,768]{1,0:T(8,128)(2,1)}, u32[]{:S(2)}, u32[]{:S(2)}) collective-permute-start(bf16[256,768]{1,0:T(8,128)(2,1)} %get-tuple-element.112), channel_id=1, source_target_pairs={{0,4},{4,0},{8,12},{12,8},{16,20},{20,16},{24,28},{28,24},{1,5},{5... | collective-permute-start | bytes 1179656 | tf_op jit(solution)/shard_map/ppermute | solution.py:355
  416.6 83.8 %collective-permute-start.28 = (bf16[256,768]{1,0:T(8,128)(2,1)}, bf16[256,768]{1,0:T(8,128)(2,1)}, u32[]{:S(2)}, u32[]{:S(2)}) collective-permute-start(bf16[256,768]{1,0:T(8,128)(2,1)} %get-tuple-element.111), channel_id=1, source_target_pairs={{0,8},{4,12},{8,0},{12,4},{16,24},{20,28},{24,16},{28,20},{1,9},{5... | collective-permute-start | bytes 1179656 | tf_op jit(solution)/shard_map/ppermute | solution.py:355
  416.6 85.5 %collective-permute-start.29 = (bf16[256,768]{1,0:T(8,128)(2,1)}, bf16[256,768]{1,0:T(8,128)(2,1)}, u32[]{:S(2)}, u32[]{:S(2)}) collective-permute-start(bf16[256,768]{1,0:T(8,128)(2,1)} %get-tuple-element.110), channel_id=1, source_target_pairs={{0,12},{4,8},{8,4},{12,0},{16,28},{20,24},{24,20},{28,16},{1,13},{... | collective-permute-start | bytes 1179656 | tf_op jit(solution)/shard_map/ppermute | solution.py:355
  425.6 78.9 %collective-permute-start.30 = (bf16[256,768]{1,0:T(8,128)(2,1)}, bf16[256,768]{1,0:T(8,128)(2,1)}, u32[]{:S(2)}, u32[]{:S(2)}) collective-permute-start(bf16[256,768]{1,0:T(8,128)(2,1)} %get-tuple-element.109), channel_id=1, source_target_pairs={{0,16},{4,20},{8,24},{12,28},{16,0},{20,4},{24,8},{28,12},{1,17},{... | collective-permute-start | bytes 1179656 | tf_op jit(solution)/shard_map/ppermute | solution.py:355
  497.0 52.5 %copy-start.43 = (s32[512]{0:T(512)S(1)}, s32[512]{0:T(512)}, u32[]{:S(2)}) copy-start(s32[512]{0:T(512)} %copy-done.40) | copy-start | bytes 6148
  497.0 39.0 %collective-permute-start.31 = (bf16[256,768]{1,0:T(8,128)(2,1)}, bf16[256,768]{1,0:T(8,128)(2,1)S(1)}, u32[]{:S(2)}, u32[]{:S(2)}) collective-permute-start(bf16[256,768]{1,0:T(8,128)(2,1)} %get-tuple-element.108), channel_id=1, source_target_pairs={{0,20},{4,16},{8,28},{12,24},{16,4},{20,0},{24,12},{28,8},{1,21},{... | collective-permute-start | bytes 1179656 | tf_op jit(solution)/shard_map/ppermute | solution.py:355
  500.3 58.5 %collective-permute-start.52 = (bf16[768,768]{1,0:T(8,128)(2,1)}, bf16[768,768]{1,0:T(8,128)(2,1)S(1)}, u32[]{:S(2)}, u32[]{:S(2)}) collective-permute-start(bf16[768,768]{1,0:T(8,128)(2,1)} %fusion.46), channel_id=1, source_target_pairs={{0,1},{1,0},{2,3},{3,2},{4,5},{5,4},{6,7},{7,6},{8,9},{9,8},{10,11... | collective-permute-start | bytes 3538952 | tf_op jit(solution)/shard_map/ppermute | solution.py:377
  502.1 69.3 %collective-permute-start.49 = (bf16[192,3072]{1,0:T(8,128)(2,1)}, bf16[192,3072]{1,0:T(8,128)(2,1)S(1)}, u32[]{:S(2)}, u32[]{:S(2)}) collective-permute-start(bf16[192,3072]{1,0:T(8,128)(2,1)} %convolution_convert_fusion.1), channel_id=1, source_target_pairs={{0,1},{1,0},{2,3},{3,2},{4,5},{5,4},{6,7},{7,6},{8,9},{9,8},{10,11... | collective-permute-start | bytes 3538952 | tf_op jit(solution)/shard_map/ppermute | solution.py:377
  504.5 35.4 %collective-permute-start.32 = (bf16[256,768]{1,0:T(8,128)(2,1)}, bf16[256,768]{1,0:T(8,128)(2,1)S(1)}, u32[]{:S(2)}, u32[]{:S(2)}) collective-permute-start(bf16[256,768]{1,0:T(8,128)(2,1)} %get-tuple-element.107), channel_id=1, source_target_pairs={{0,24},{4,28},{8,16},{12,20},{16,8},{20,12},{24,0},{28,4},{1,25},{... | collective-permute-start | bytes 1179656 | tf_op jit(solution)/shard_map/ppermute | solution.py:355
  536.1 12.7 %collective-permute-start.33 = (bf16[256,768]{1,0:T(8,128)(2,1)S(1)}, bf16[256,768]{1,0:T(8,128)(2,1)S(1)}, u32[]{:S(2)}, u32[]{:S(2)}) collective-permute-start(bf16[256,768]{1,0:T(8,128)(2,1)S(1)} %copy-done.18), channel_id=1, source_target_pairs={{0,28},{4,24},{8,20},{12,16},{16,12},{20,8},{24,4},{28,0},{1,29},{... | collective-permute-start | bytes 1179656 | tf_op jit(solution)/shard_map/ppermute | solution.py:355
  539.9 155.5 %collective-permute-start.48 = (bf16[192,3072]{1,0:T(8,128)(2,1)S(1)}, bf16[192,3072]{1,0:T(8,128)(2,1)}, u32[]{:S(2)}, u32[]{:S(2)}) collective-permute-start(bf16[192,3072]{1,0:T(8,128)(2,1)S(1)} %copy-done.12), channel_id=1, source_target_pairs={{0,1},{1,0},{2,3},{3,2},{4,5},{5,4},{6,7},{7,6},{8,9},{9,8},{10,11... | collective-permute-start | bytes 3538952 | tf_op jit(solution)/shard_map/ppermute | solution.py:376
  564.5 124.0 %collective-permute-start.53 = (bf16[768,768]{1,0:T(8,128)(2,1)}, bf16[768,768]{1,0:T(8,128)(2,1)}, u32[]{:S(2)}, u32[]{:S(2)}) collective-permute-start(bf16[768,768]{1,0:T(8,128)(2,1)} %add_convert_fusion), channel_id=1, source_target_pairs={{0,2},{1,3},{2,0},{3,1},{4,6},{5,7},{6,4},{7,5},{8,10},{9,11},{10,... | collective-permute-start | bytes 3538952 | tf_op jit(solution)/shard_map/ppermute | solution.py:379
  576.7 118.7 %collective-permute-start.50 = (bf16[192,3072]{1,0:T(8,128)(2,1)}, bf16[192,3072]{1,0:T(8,128)(2,1)}, u32[]{:S(2)}, u32[]{:S(2)}) collective-permute-start(bf16[192,3072]{1,0:T(8,128)(2,1)} %fusion.6), channel_id=1, source_target_pairs={{0,2},{1,3},{2,0},{3,1},{4,6},{5,7},{6,4},{7,5},{8,10},{9,11},{10,... | collective-permute-start | bytes 3538952 | tf_op jit(solution)/shard_map/ppermute | solution.py:379
  695.4 62.6 %copy-start.1 = (f32[12,32]{1,0:T(8,128)S(1)}, f32[12,32]{1,0:T(8,128)}, u32[]{:S(2)}) copy-start(f32[12,32]{1,0:T(8,128)} %param.21) | copy-start | bytes 4612
  (54 other events, 689.3 us)
Sparse Core Ops, SparseCore 0:
  11.4 85.7 all-gather.2
  100.2 55.8 all-gather.4
  497.1 253.0 all-reduce.4

commit v2 on v1

v2 whole, which is shorter than its diff:
```python
import functools

import jax
import jax.numpy as jnp
from jax import lax
from jax.experimental import pallas as pl
from jax.experimental.pallas import tpu as pltpu
from jax.sharding import PartitionSpec as P

EPSILON = 1e-06
MASKED = -1e30
GELU_COEF = 0.7978845608028654
TILE = 128
LANES = 128
PARTS = 2
TAIL = 16
VMEM_BYTES = 56 * 1024 * 1024


def rms_norm(values, gain_vector):
    return (
        values
        * lax.rsqrt(jnp.mean(values * values, axis=-1, keepdims=True) + EPSILON)
        * gain_vector
    )


def times(left_side, right_side):
    return lax.dot_general(
        left_side, right_side, (((1,), (0,)), ((), ())), preferred_element_type=jnp.float32
    )


def times_trans(left_side, right_side):
    return lax.dot_general(
        left_side, right_side, (((1,), (1,)), ((), ())), preferred_element_type=jnp.float32
    )


def trans_times(left_side, right_side):
    return lax.dot_general(
        left_side, right_side, (((0,), (0,)), ((), ())), preferred_element_type=jnp.float32
    )


def sequence_starts(lengths, row_count):
    seq_ends = jnp.cumsum(lengths, dtype=jnp.int32)
    places = jnp.arange(row_count, dtype=jnp.int32)
    passed = places[:, None] >= seq_ends[None, :]
    return jnp.max(jnp.where(passed, seq_ends[None, :], 0), axis=1, keepdims=True)


def distance_onehot(bucket_map, row_count, buckets):
    longest = bucket_map.shape[0]
    distance = row_count - TILE - jnp.arange(row_count, dtype=jnp.int32)
    place = jnp.arange(longest, dtype=jnp.int32)
    at_distance = jnp.sum(
        jnp.where(distance[:, None] == place[None, :], bucket_map[None, :] + 1, 0), axis=1
    )
    return (at_distance[:, None] == 1 + jnp.arange(buckets, dtype=jnp.int32)[None, :]).astype(
        jnp.float32
    )


def head_lanes(block, which, head_size):
    lane = lax.broadcasted_iota(jnp.int32, block.shape, 1)
    inside = (lane >= which * head_size) & (lane < (which + 1) * head_size)
    return jnp.where(inside, block, jnp.zeros_like(block))


def bias_strip(base_ref, head, row_count):
    row = base_ref[pl.ds(head, 1), :]
    spread = jnp.broadcast_to(row, (TILE, row_count))
    return pltpu.roll(spread, 0, 1, stride=1, stride_axis=0)


def tile_probs(query_tile, keys, strip, starts, tile, scale):
    row_count = strip.shape[1]
    width = TILE * (tile + 1)
    score = times_trans(query_tile, keys[:width]) * scale + strip[:, row_count - width :]
    place = lax.broadcasted_iota(jnp.int32, score.shape, 1)
    row = lax.broadcasted_iota(jnp.int32, score.shape, 0) + TILE * tile
    score = jnp.where((place <= row) & (place >= starts), score, MASKED)
    exponent = jnp.exp(score - jnp.max(score, axis=1, keepdims=True))
    return exponent * (1.0 / jnp.sum(exponent, axis=1, keepdims=True))


def lane_block(first):
    return pl.ds(pl.multiple_of(first, LANES), LANES)


def attention_kernel(head_size, base_ref, starts_ref, packed_ref, attended_ref):
    row_count, width = attended_ref.shape
    per_block = LANES // head_size
    scale = head_size ** (-0.5)

    @pl.loop(0, width // LANES)
    def _(block):
        queries = packed_ref[:, lane_block(block * LANES)]
        keys = packed_ref[:, lane_block(width + block * LANES)]
        values = packed_ref[:, lane_block(2 * width + block * LANES)]
        strips = [bias_strip(base_ref, block * per_block + own, row_count) for own in range(per_block)]
        for tile in range(row_count // TILE):
            rows = slice(tile * TILE, (tile + 1) * TILE)
            starts = starts_ref[rows, :]
            total = jnp.zeros((TILE, LANES), jnp.float32)
            for own in range(per_block):
                probs = tile_probs(
                    head_lanes(queries[rows], own, head_size), keys, strips[own], starts, tile, scale
                ).astype(jnp.bfloat16)
                total += times(probs, head_lanes(values[: probs.shape[1]], own, head_size))
            attended_ref[rows, lane_block(block * LANES)] = total.astype(jnp.bfloat16)


def attention(base, starts, packed, head_size):
    row_count = packed.shape[0]
    width = packed.shape[1] // 3
    return pl.pallas_call(
        functools.partial(attention_kernel, head_size),
        out_shape=jax.ShapeDtypeStruct((row_count, width), jnp.bfloat16),
        compiler_params=pltpu.CompilerParams(vmem_limit_bytes=VMEM_BYTES),
        cost_estimate=pl.CostEstimate(flops=1000, bytes_accessed=1000, transcendentals=0),
        name="attention",
    )(base, starts, packed)


def attention_pull_kernel(
    head_size,
    base_ref,
    starts_ref,
    packed_ref,
    grad_ref,
    kept_rows_ref,
    sent_rows_ref,
    d_packed_ref,
    d_base_ref,
    keep_ref,
    send_ref,
    d_keys_ref,
    d_values_ref,
    d_strip_ref,
):
    row_count, width = grad_ref.shape
    per_block = LANES // head_size
    scale = head_size ** (-0.5)

    @pl.loop(0, width // LANES)
    def _(block):
        queries = packed_ref[:, lane_block(block * LANES)]
        keys = packed_ref[:, lane_block(width + block * LANES)]
        values = packed_ref[:, lane_block(2 * width + block * LANES)]
        grads = grad_ref[:, lane_block(block * LANES)]
        strips = [bias_strip(base_ref, block * per_block + own, row_count) for own in range(per_block)]
        d_keys_ref[...] = jnp.zeros_like(d_keys_ref)
        d_values_ref[...] = jnp.zeros_like(d_values_ref)
        d_strip_ref[...] = jnp.zeros_like(d_strip_ref)
        for tile in range(row_count // TILE):
            rows = slice(tile * TILE, (tile + 1) * TILE)
            reach = TILE * (tile + 1)
            starts = starts_ref[rows, :]
            d_queries = jnp.zeros((TILE, LANES), jnp.float32)
            for own in range(per_block):
                own_queries = head_lanes(queries[rows], own, head_size)
                own_grads = head_lanes(grads[rows], own, head_size)
                probs = tile_probs(own_queries, keys, strips[own], starts, tile, scale)
                d_probs = times_trans(own_grads, values[:reach])
                row_delta = jnp.sum(probs * d_probs, axis=1, keepdims=True)
                d_score = (probs * (d_probs - row_delta)).astype(jnp.bfloat16)
                d_strip_ref[own, :, row_count - reach :] += d_score.astype(jnp.float32)
                d_queries += times(d_score, head_lanes(keys[:reach], own, head_size))
                d_keys_ref[:reach, :] += trans_times(d_score, own_queries)
                d_values_ref[:reach, :] += trans_times(probs.astype(jnp.bfloat16), own_grads)
            d_packed_ref[rows, lane_block(block * LANES)] = (d_queries * scale).astype(jnp.bfloat16)
        d_packed_ref[:, lane_block(width + block * LANES)] = (d_keys_ref[...] * scale).astype(
            jnp.bfloat16
        )
        d_packed_ref[:, lane_block(2 * width + block * LANES)] = d_values_ref[...].astype(
            jnp.bfloat16
        )
        for own in range(per_block):
            folded = d_strip_ref[own]
            half = TILE // 2
            while half >= 8:
                folded = folded[:half] + pltpu.roll(folded[half:], row_count - half, 1)
                half //= 2
            row = lax.broadcasted_iota(jnp.int32, folded.shape, 0)
            for bit in (4, 2, 1):
                folded = jnp.where(
                    (row & bit) != 0, pltpu.roll(folded, row_count - bit, 1), folded
                )
            d_base_ref[pl.ds(block * per_block + own, 1), :] = jnp.sum(
                folded, axis=0, keepdims=True
            )

    for start in range(0, 3 * width, width):
        columns = slice(start, start + width)
        send_ref[:, columns] = trans_times(sent_rows_ref[...], d_packed_ref[:, columns]).astype(
            jnp.bfloat16
        )
        keep_ref[:, columns] = trans_times(kept_rows_ref[...], d_packed_ref[:, columns])


def attention_pull(base, starts, packed, grads, rows, head_size):
    row_count, width = grads.shape
    half = rows[0].shape[1]
    return pl.pallas_call(
        functools.partial(attention_pull_kernel, head_size),
        out_shape=(
            jax.ShapeDtypeStruct(packed.shape, jnp.bfloat16),
            jax.ShapeDtypeStruct(base.shape, jnp.float32),
            jax.ShapeDtypeStruct((half, packed.shape[1]), jnp.float32),
            jax.ShapeDtypeStruct((half, packed.shape[1]), jnp.bfloat16),
        ),
        scratch_shapes=[
            pltpu.VMEM((row_count, LANES), jnp.float32),
            pltpu.VMEM((row_count, LANES), jnp.float32),
            pltpu.VMEM((LANES // head_size, TILE, row_count), jnp.float32),
        ],
        compiler_params=pltpu.CompilerParams(vmem_limit_bytes=VMEM_BYTES),
        cost_estimate=pl.CostEstimate(flops=1000, bytes_accessed=1000, transcendentals=0),
        name="attention_pull",
    )(base, starts, packed, grads, *rows)


def gelu_parts(values):
    inner = GELU_COEF * (values + 0.044715 * values * values * values)
    bend = jnp.tanh(inner)
    slope = 0.5 * (1.0 + bend) + 0.5 * values * (1.0 - bend * bend) * (
        GELU_COEF * (1.0 + 3.0 * 0.044715 * values * values)
    )
    return 0.5 * values * (1.0 + bend), slope


def vmem():
    return pl.BlockSpec(memory_space=pltpu.VMEM)


def two_gates(logits, first_ids, second_ids):
    column = lax.broadcasted_iota(jnp.int32, logits.shape, 1)
    first = jnp.sum(jnp.where(column == first_ids, logits, 0.0), axis=1, keepdims=True)
    second = jnp.sum(jnp.where(column == second_ids, logits, 0.0), axis=1, keepdims=True)
    peak = jnp.maximum(first, second)
    first, second = jnp.exp(first - peak), jnp.exp(second - peak)
    return first / (first + second), second / (first + second)


def project_kernel(column, tokens_ref, *refs):
    first_refs, second_refs = refs[0:2], refs[2:4]
    packed_ref, normed_refs = refs[4], refs[5:7]
    row_count, half = normed_refs[0].shape
    cut = first_refs[0].shape[1]
    rest = packed_ref.shape[1] - cut
    inputs = tokens_ref[...].astype(jnp.float32)
    inverse = lax.rsqrt(jnp.mean(inputs * inputs, axis=1, keepdims=True) + EPSILON)
    for which in range(2):
        small = second_refs[which][:, rest:].astype(jnp.float32)
        gain = jnp.transpose(small)[column : column + 1, :]
        normed = (inputs[:, which * half : (which + 1) * half] * inverse * gain).astype(
            jnp.bfloat16
        )
        normed_refs[which][...] = normed
    both = jnp.concatenate([normed_refs[0][...], normed_refs[1][...]], axis=1)
    for refs_of, start, width in ((first_refs, 0, cut), (second_refs, cut, rest)):
        weights = jnp.concatenate([refs_of[0][:, :width], refs_of[1][:, :width]], axis=0)
        packed_ref[:, start : start + width] = times(both, weights).astype(jnp.bfloat16)


def project(tokens_rel, first, second, column, qkv_width):
    row_count, width = tokens_rel.shape
    half = jax.ShapeDtypeStruct((row_count, width // 2), jnp.bfloat16)
    return pl.pallas_call(
        functools.partial(project_kernel, column),
        out_shape=(jax.ShapeDtypeStruct((row_count, qkv_width), jnp.bfloat16), half, half),
        compiler_params=pltpu.CompilerParams(vmem_limit_bytes=VMEM_BYTES),
        cost_estimate=pl.CostEstimate(flops=1000, bytes_accessed=1000, transcendentals=0),
        name="project",
    )(tokens_rel, *first, *second)


def slot_rows_of(ids_ref, rows, first_place, count):
    place = first_place + lax.broadcasted_iota(jnp.int32, (count, rows.shape[0]), 0)
    inside = (place == ids_ref[0:1, :]) | (place == ids_ref[1:2, :])
    return times(jnp.where(inside, 1.0, 0.0).astype(jnp.bfloat16), rows).astype(jnp.bfloat16)


def fill_blocks(ids_ref, rows, block_refs):
    experts, count, _ = block_refs[0].shape
    for part, block_ref in enumerate(block_refs):
        for expert in range(experts):
            place = (expert * len(block_refs) + part) * count
            block_ref[expert] = slot_rows_of(ids_ref, rows, place, count)


def spread_kernel(ids_ref, rows_ref, block_ref):
    fill_blocks(ids_ref, rows_ref[...], [block_ref])


def spread(slot_ids, rows, experts, capacity):
    row_count, width = rows.shape
    return pl.pallas_call(
        spread_kernel,
        out_shape=jax.ShapeDtypeStruct((experts, capacity, width), jnp.bfloat16),
        compiler_params=pltpu.CompilerParams(vmem_limit_bytes=VMEM_BYTES),
        cost_estimate=pl.CostEstimate(flops=1000, bytes_accessed=1000, transcendentals=0),
        name="spread",
    )(slot_ids, rows)


def mix_kernel(
    ids_ref, tokens_ref, attended_ref, out_ref, gain_ref, mixed_ref, normed_ref, *block_refs
):
    mixed = tokens_ref[...].astype(jnp.float32) + times(attended_ref[...], out_ref[...])
    mixed_ref[...] = mixed
    inverse = lax.rsqrt(jnp.mean(mixed * mixed, axis=1, keepdims=True) + EPSILON)
    normed_ref[...] = (mixed * inverse * gain_ref[...]).astype(jnp.bfloat16)
    fill_blocks(ids_ref, normed_ref[...], block_refs)


def mix(slot_ids, tokens, attended, weight_out, gain, experts, capacity):
    row_count, width = tokens.shape
    block = jax.ShapeDtypeStruct((experts, capacity // PARTS, width), jnp.bfloat16)
    return pl.pallas_call(
        mix_kernel,
        out_shape=(
            jax.ShapeDtypeStruct((row_count, width), jnp.float32),
            jax.ShapeDtypeStruct((row_count, width), jnp.bfloat16),
        )
        + (block,) * PARTS,
        compiler_params=pltpu.CompilerParams(vmem_limit_bytes=VMEM_BYTES),
        cost_estimate=pl.CostEstimate(flops=1000, bytes_accessed=1000, transcendentals=0),
        name="mix",
    )(slot_ids, tokens, attended, weight_out, gain)


def expert_kernel(
    place_ref,
    rows_ref,
    grads_ref,
    other_ref,
    router_ref,
    in_ref,
    out_ref,
    *refs,
):
    payload_ref, produced_ref, rows_all, slot_grad_all, active_ref, d_hidden_ref = refs[-10:-4]
    rows, slot_grad, produced_sum, row_sum = refs[-4:]
    sources, capacity, width = rows_ref.shape
    count = sources * capacity
    step = pl.program_id(0)

    @pl.when(step == 0)
    def _():
        rows[...] = rows_ref[...].reshape(count, width)
        logits = times(rows[...], router_ref[...])
        own_ids = jnp.full((count, 1), place_ref[0], jnp.int32)
        gate, unused_gate = two_gates(logits, own_ids, other_ref[...])
        grads = grads_ref[...].reshape(count, width).astype(jnp.float32)
        slot_grad[...] = (gate * grads).astype(jnp.bfloat16)
        rows_all[...] = rows[...]
        slot_grad_all[...] = slot_grad[...]
        produced_sum[...] = jnp.zeros_like(produced_sum)
        row_sum[...] = jnp.zeros_like(row_sum)

    hidden = times(rows[...], in_ref[...])
    active, slope = gelu_parts(hidden)
    active = active.astype(jnp.bfloat16)
    active_ref[...] = active
    d_active = times_trans(slot_grad[...], out_ref[...])
    d_hidden = (slope * d_active).astype(jnp.bfloat16)
    d_hidden_ref[...] = d_hidden
    produced_sum[...] += times(active, out_ref[...])
    row_sum[...] += times_trans(d_hidden, in_ref[...])

    @pl.when(step == pl.num_programs(0) - 1)
    def _():
        for source in range(sources):
            own = slice(source * capacity, (source + 1) * capacity)
            result = produced_sum[own, :].astype(jnp.bfloat16)
            produced_ref[source] = result
            payload_ref[source, :capacity, :] = row_sum[own, :].astype(jnp.bfloat16)
            d_gate = jnp.sum(
                result.astype(jnp.float32) * grads_ref[source].astype(jnp.float32),
                axis=1,
                keepdims=True,
            )
            across = jnp.transpose(jnp.broadcast_to(d_gate, (capacity, LANES)))[:TAIL, :]
            high = across.astype(jnp.bfloat16).astype(jnp.float32)
            row = lax.broadcasted_iota(jnp.int32, across.shape, 0)
            tail = jnp.where(row == 0, high, jnp.where(row == 1, across - high, 0.0))
            payload_ref[source, capacity:, :] = jnp.zeros((TAIL, width), jnp.bfloat16)
            payload_ref[source, capacity:, :capacity] = tail.astype(jnp.bfloat16)


def expert_rows(place, part, rows, grads, other, router, weight_in, weight_out, earlier):
    sources, capacity, width = rows.shape
    hidden_width = weight_in.shape[1]
    chunk = hidden_width // 4
    count = sources * capacity

    def whole(shape):
        return pl.BlockSpec(shape, lambda i, place: (0,) * len(shape))

    def part_of(*shape):
        return pl.BlockSpec(shape, lambda i, place: (0, part, 0))

    def part_block(columns):
        return pl.BlockSpec((count, columns), lambda i, place: (part, 0))

    def part_chunk():
        return pl.BlockSpec((count, chunk), lambda i, place: (part, i))

    def full(*shape):
        return jax.ShapeDtypeStruct(shape, jnp.bfloat16)

    total = PARTS * count
    operands = (rows, grads, other, router, weight_in, weight_out)
    in_specs = [
        whole(rows.shape),
        part_of(sources, capacity, width),
        whole(other.shape),
        whole(router.shape),
        pl.BlockSpec((width, chunk), lambda i, place: (0, i)),
        pl.BlockSpec((chunk, width), lambda i, place: (i, 0)),
    ]
    aliases = {}
    if earlier is not None:
        aliases = {1 + len(operands) + which: 1 + which for which in range(5)}
        operands = operands + tuple(earlier)
        in_specs = in_specs + [pl.BlockSpec(memory_space=pl.ANY)] * 5
    results = pl.pallas_call(
        expert_kernel,
        grid_spec=pltpu.PrefetchScalarGridSpec(
            num_scalar_prefetch=1,
            grid=(4,),
            in_specs=in_specs,
            out_specs=[
                whole((sources, capacity + TAIL, width)),
                part_of(sources, capacity, width),
                part_block(width),
                part_block(width),
                part_chunk(),
                part_chunk(),
            ],
            scratch_shapes=[
                pltpu.VMEM((count, width), jnp.bfloat16),
                pltpu.VMEM((count, width), jnp.bfloat16),
                pltpu.VMEM((count, width), jnp.float32),
                pltpu.VMEM((count, width), jnp.float32),
            ],
        ),
        out_shape=[
            full(sources, capacity + TAIL, width),
            full(sources, PARTS * capacity, width),
            full(total, width),
            full(total, width),
            full(total, hidden_width),
            full(total, hidden_width),
        ],
        input_output_aliases=aliases,
        compiler_params=pltpu.CompilerParams(vmem_limit_bytes=VMEM_BYTES),
        cost_estimate=pl.CostEstimate(
            flops=8 * count * width * hidden_width,
            bytes_accessed=4 * count * (hidden_width + 4 * width) + 4 * width * hidden_width,
            transcendentals=count * hidden_width,
        ),
        name="expert_rows",
    )(place, *operands)
    return results[0], results[1:]


def collect_kernel(
    slots_ref,
    experts_ref,
    places_ref,
    normed_ref,
    mixed_ref,
    cotangent_ref,
    router_ref,
    gain_ref,
    out_ref,
    pick_ref,
    attended_ref,
    normed_rel_ref,
    *refs,
):
    payload_refs = refs[:-5]
    d_mixed_ref, d_attended_ref, gates_ref, keep_ref, send_ref = refs[-5:]
    row_count, width = mixed_ref.shape
    experts, capacity = payload_refs[0].shape[0], payload_refs[0].shape[1] - TAIL
    first_slots, second_slots = slots_ref[:, 0:1], slots_ref[:, 1:2]
    first_grad = jnp.zeros((row_count, 1), jnp.float32)
    second_grad = jnp.zeros((row_count, 1), jnp.float32)
    d_normed = jnp.zeros((row_count, width), jnp.float32)
    for part, payload_ref in enumerate(payload_refs):
        places = places_ref[part : part + 1, :]
        select = jnp.where((places == first_slots) | (places == second_slots), 1.0, 0.0)
        rows = payload_ref[...].reshape(experts * (capacity + TAIL), width)
        d_normed += times(select.astype(jnp.bfloat16), rows)
        for expert in range(experts):
            first_place = (expert * len(payload_refs) + part) * capacity
            place = first_place + lax.broadcasted_iota(jnp.int32, (row_count, capacity), 1)
            tail = payload_ref[expert, capacity:, :capacity].astype(jnp.float32)
            d_gate = tail[0:1, :] + tail[1:2, :]
            first_grad += jnp.sum(
                jnp.where(place == first_slots, d_gate, 0.0), axis=1, keepdims=True
            )
            second_grad += jnp.sum(
                jnp.where(place == second_slots, d_gate, 0.0), axis=1, keepdims=True
            )
    logits = times(normed_ref[...], router_ref[...])
    first_ids, second_ids = experts_ref[:, 0:1], experts_ref[:, 1:2]
    first_gate, second_gate = two_gates(logits, first_ids, second_ids)
    mean = first_gate * first_grad + second_gate * second_grad
    column = lax.broadcasted_iota(jnp.int32, logits.shape, 1)
    d_logits = jnp.where(
        column == first_ids,
        first_gate * (first_grad - mean),
        jnp.where(column == second_ids, second_gate * (second_grad - mean), 0.0),
    ).astype(jnp.bfloat16)
    gates_ref[:, 0:1] = first_gate
    gates_ref[:, 1:2] = second_gate
    d_normed = d_normed + times_trans(d_logits, router_ref[...])
    mixed = mixed_ref[...]
    inverse = lax.rsqrt(jnp.mean(mixed * mixed, axis=1, keepdims=True) + EPSILON)
    d_gain = jnp.sum(d_normed * mixed * inverse, axis=0, keepdims=True)
    scaled = d_normed * gain_ref[...]
    pulled = jnp.mean(scaled * mixed, axis=1, keepdims=True) * inverse * inverse
    d_mixed = cotangent_ref[...].astype(jnp.float32) + inverse * (scaled - mixed * pulled)
    d_mixed_ref[...] = d_mixed
    d_branch = d_mixed.astype(jnp.bfloat16)
    d_attended_ref[...] = times_trans(d_branch, out_ref[...]).astype(jnp.bfloat16)
    small = trans_times(normed_rel_ref[...], d_logits)
    column = lax.broadcasted_iota(jnp.int32, small.shape, 1)
    gain_column = jnp.sum(
        pick_ref[...].astype(jnp.float32) * d_gain, axis=1, keepdims=True
    )
    small = jnp.where(column == small.shape[1] - 1, gain_column, small)
    half = width // 2
    keep_ref[:, width:] = small[:half]
    send_ref[:, width:] = small[half:].astype(jnp.bfloat16)
    keep_ref[:, :width] = trans_times(attended_ref[:, :half], d_branch)
    send_ref[:, :width] = trans_times(attended_ref[:, half:], d_branch).astype(jnp.bfloat16)


def collect(
    slots,
    experts,
    normed,
    mixed,
    cotangent,
    router,
    gain,
    weight_out,
    pick,
    attended_rel,
    normed_rel,
    payloads,
):
    row_count, width = mixed.shape
    sources, tall, _ = payloads[0].shape
    inside = jnp.arange(tall, dtype=jnp.int32)
    places = jnp.stack(
        [
            jnp.where(
                inside[None, :] < tall - TAIL,
                (jnp.arange(sources, dtype=jnp.int32)[:, None] * len(payloads) + part)
                * (tall - TAIL)
                + inside[None, :],
                -1,
            ).reshape(-1)
            for part in range(len(payloads))
        ]
    )
    columns = width + router.shape[1]
    return pl.pallas_call(
        collect_kernel,
        out_shape=(
            jax.ShapeDtypeStruct((row_count, width), jnp.float32),
            jax.ShapeDtypeStruct((row_count, width), jnp.bfloat16),
            jax.ShapeDtypeStruct((row_count, 2), jnp.float32),
            jax.ShapeDtypeStruct((width // 2, columns), jnp.float32),
            jax.ShapeDtypeStruct((width // 2, columns), jnp.bfloat16),
        ),
        compiler_params=pltpu.CompilerParams(vmem_limit_bytes=VMEM_BYTES),
        cost_estimate=pl.CostEstimate(flops=1000, bytes_accessed=1000, transcendentals=0),
        name="collect",
    )(
        slots,
        experts,
        places,
        normed,
        mixed,
        cotangent,
        router,
        gain,
        weight_out,
        pick,
        attended_rel,
        normed_rel,
        *payloads,
    )


def finish_kernel(slots_ref, gates_ref, mixed_ref, produced_ref, output_ref):
    row_count, width = mixed_ref.shape
    experts, capacity, _ = produced_ref.shape
    produced = produced_ref[...].reshape(experts * capacity, width)
    place = lax.broadcasted_iota(jnp.int32, (row_count, experts * capacity), 1)
    total = mixed_ref[...]
    for which in range(2):
        select = jnp.where(place == slots_ref[:, which : which + 1], 1.0, 0.0)
        found = times(select.astype(jnp.bfloat16), produced)
        total = total + gates_ref[:, which : which + 1] * found
    output_ref[...] = total.astype(jnp.bfloat16)


def finish(slots, gates, mixed, produced):
    row_count, width = mixed.shape
    return pl.pallas_call(
        finish_kernel,
        out_shape=jax.ShapeDtypeStruct((row_count, width), jnp.bfloat16),
        compiler_params=pltpu.CompilerParams(vmem_limit_bytes=VMEM_BYTES),
        cost_estimate=pl.CostEstimate(flops=1000, bytes_accessed=1000, transcendentals=0),
        name="finish",
    )(slots, gates, mixed, produced)


def slot_position(device_ids, experts):
    flat_ids = device_ids.reshape(-1)
    chosen = (flat_ids[:, None] == jnp.arange(experts, dtype=jnp.int32)[None, :]).astype(jnp.int32)
    before = jnp.cumsum(chosen, axis=0, dtype=jnp.int32) - chosen
    position = jnp.sum(before * chosen, axis=1, dtype=jnp.int32)
    return position.reshape(device_ids.shape)


def swap(rows, axis, size, step):
    return lax.ppermute(rows, axis, [(index, index ^ step) for index in range(size)])


def after(values, *earlier):
    return lax.optimization_barrier((values,) + earlier)[0]


def trade(blocks):
    return lax.all_to_all(blocks, "fsdp", split_axis=0, concat_axis=0, tiled=True)


class Ring:
    def __init__(self, fsdp, rep, own_rows):
        self.fsdp, self.rep, self.own_rows = fsdp, rep, own_rows
        self.relative = fsdp == 8 and rep == 4
        self.half = own_rows * fsdp * rep // 2

    def order(self, which):
        row = jnp.arange(self.half, dtype=jnp.int32)
        if not self.relative:
            return row + which * self.half
        group = row // self.own_rows
        mask = which + 8 * (group & 1) + 16 * ((group >> 1) & 1) + 2 * ((group >> 2) & 1)
        mask = mask + 4 * ((group >> 3) & 1)
        device = lax.axis_index("fsdp") * self.rep + lax.axis_index("rep")
        return (device ^ mask) * self.own_rows + row % self.own_rows

    def hop(self, rows, bit):
        return swap(rows, "rep", 4, bit) if bit < 4 else swap(rows, "fsdp", 8, bit // 4)

    def line(self, shard):
        if not self.relative:
            return shard
        return jnp.concatenate([shard] + [self.hop(shard, bit) for bit in (8, 16, 24)])

    def gather(self, line, cut):
        if not self.relative:
            whole = lax.all_gather(line, ("fsdp", "rep"), axis=0, tiled=True)
            halves = (whole[: self.half], whole[self.half :])
            return tuple(h[:, :cut] for h in halves), tuple(h[:, cut:] for h in halves)
        parts = []
        for columns, early, late in ((line[:, :cut], 2, 4), (line[:, cut:], 4, 2)):
            one = self.hop(columns, early)
            two = self.hop(columns, late)
            both = self.hop(one, late)
            by_y, by_x = (one, two) if early == 2 else (two, one)
            parts.append(jnp.concatenate([columns, by_y, by_x, both]))
        return tuple((part, self.hop(part, 1)) for part in parts)

    def group(self, rows):
        if not self.relative:
            return lax.all_gather(rows, "fsdp", axis=0)
        rows = rows[None]
        for bit in (4, 8, 16):
            rows = jnp.concatenate([rows, self.hop(rows, bit)])
        return rows

    def by_source(self, rows):
        if not self.relative:
            return rows
        order = lax.axis_index("fsdp") ^ jnp.arange(self.fsdp, dtype=jnp.int32)
        return jnp.take(rows, order, axis=0)

    def scatter(self, keep, send, earlier):
        if not self.relative:
            whole = jnp.concatenate([keep, send.astype(jnp.float32)])
            return lax.psum_scatter(whole, ("fsdp", "rep"), scatter_dimension=0, tiled=True)
        low = jnp.bfloat16
        total = keep + self.hop(send, 1).astype(jnp.float32)
        cut = -(-total.shape[1] // 256) * 128
        results = []
        quarter = self.half // 4
        for columns, first in ((total[:, :cut], 4), (total[:, cut:], 2)):
            if first == 4:
                kept, sent = columns[: 2 * quarter], columns[2 * quarter :]
            else:
                kept = jnp.concatenate([columns[:quarter], columns[2 * quarter : 3 * quarter]])
                sent = jnp.concatenate([columns[quarter : 2 * quarter], columns[3 * quarter :]])
            columns = kept + self.hop(sent.astype(low), first).astype(jnp.float32)
            for bit in (6 - first, 16, 8):
                if bit == 16:
                    columns = after(columns, earlier)
                middle = columns.shape[0] // 2
                got = self.hop(columns[middle:].astype(low), bit)
                columns = columns[:middle] + got.astype(jnp.float32)
            results.append(columns)
        return jnp.concatenate(results, axis=1)

    def total(self, values, earlier):
        if not self.relative:
            return lax.psum(values, ("fsdp", "rep"))
        for bit in (1, 2, 4, 8, 16):
            if bit == 8:
                values = after(values, earlier)
            values = values + self.hop(values, bit)
        return values

    def own(self, values):
        device = lax.axis_index("fsdp") * self.rep + lax.axis_index("rep")
        return lax.dynamic_slice_in_dim(values, device * self.own_rows, self.own_rows, 0)


def scatter_rep(piece_of, size):
    me = lax.axis_index("rep")
    low = jnp.bfloat16
    far_near = swap(piece_of(me ^ 3).astype(low), "rep", size, 1)
    near = swap(piece_of(me ^ 1).astype(low), "rep", size, 1)
    far = (piece_of(me ^ 2) + far_near.astype(jnp.float32)).astype(low)
    far = swap(far, "rep", size, 2)
    return piece_of(me) + near.astype(jnp.float32), far


def add_late(near_sum, far, earlier):
    near_sum, far = lax.optimization_barrier((near_sum, far, earlier))[:2]
    return near_sum + far.astype(jnp.float32)


def shards(
    fsdp,
    rep,
    tokens,
    attn_gain,
    qkv_weight,
    out_weight,
    ffn_gain,
    router_weight,
    expert_in,
    expert_out,
    bias_table,
    seq_lengths,
    bucket_map,
    expert_ids,
    cotangent,
):
    row_count, model_width = tokens.shape
    head_count, buckets = bias_table.shape
    head_size = model_width // head_count
    experts = router_weight.shape[1]
    capacity = 4 * row_count // experts
    highest = lax.Precision.HIGHEST
    own_rows, qkv_width = qkv_weight.shape
    extra = -(-(experts + 2) // LANES) * LANES
    me = lax.axis_index("fsdp")
    ring = Ring(fsdp, rep, own_rows)
    cut = qkv_width // 2

    small = jnp.concatenate(
        [
            router_weight,
            attn_gain[:, None],
            ffn_gain[:, None],
            jnp.zeros((own_rows, extra - experts - 2), jnp.bfloat16),
        ],
        axis=1,
    )
    line_qkv = ring.line(jnp.concatenate([qkv_weight, small], axis=1))
    first, second = ring.gather(line_qkv, cut)
    weight_out = lax.all_gather(out_weight, ("fsdp", "rep"), axis=0, tiled=True)

    position = slot_position(expert_ids, experts)
    slot_ids = expert_ids * capacity + position
    group_ids = ring.group(expert_ids)
    to_me = group_ids == me
    named = jnp.any(to_me, axis=2)
    other_ids = jnp.where(to_me[:, :, 0], group_ids[:, :, 1], group_ids[:, :, 0])
    places = jnp.where(named, jnp.cumsum(named, axis=1, dtype=jnp.int32) - 1, -1)
    slot_others = jnp.sum(
        jnp.where(
            places[:, None, :] == jnp.arange(capacity, dtype=jnp.int32)[None, :, None],
            other_ids[:, None, :],
            0,
        ),
        axis=2,
    )
    slot_others = ring.by_source(slot_others)
    slot_ids_across = slot_ids.T

    feature = jnp.arange(model_width, dtype=jnp.int32)
    picks = [
        (ring.order(which)[:, None] == feature[None, :]).astype(jnp.bfloat16) for which in range(2)
    ]
    pick = jnp.concatenate(picks)
    tokens_rel = times_trans(tokens, pick).astype(jnp.bfloat16)
    onehot = distance_onehot(bucket_map, row_count, buckets)
    base = lax.dot_general(bias_table, onehot, (((1,), (1,)), ((), ())), precision=highest)
    starts = sequence_starts(seq_lengths[0], row_count)

    sent_dy = spread(slot_ids_across, cotangent, experts, capacity)
    slot_dy = trade(after(sent_dy, line_qkv))
    weight_in = lax.all_gather(expert_in, "rep", axis=1, tiled=True)[0]
    weight_back = lax.all_gather(expert_out, "rep", axis=1, tiled=True)[0]

    def natural(halves):
        joined = trans_times(pick, jnp.concatenate(halves))
        return joined.astype(jnp.bfloat16)

    packed, *normed_halves = project(tokens_rel, first, second, experts, qkv_width)
    small = natural([half[:, qkv_width - cut :] for half in second])
    gains = small.T.astype(jnp.float32)
    gain_one, gain_two = gains[experts : experts + 1], gains[experts + 1 : experts + 2]
    attended = attention(base, starts, packed, head_size)
    mixed, normed_two, *sending = mix(
        slot_ids_across, tokens, attended, weight_out, gain_two, experts, capacity
    )
    place = me[None].astype(jnp.int32)
    size = capacity // PARTS
    arrived = [trade(after(sending[0], slot_dy))]
    arrived.append(trade(after(sending[1], arrived[0])))
    payloads, kept = [], None
    for part in range(PARTS):
        payload, kept = expert_rows(
            place,
            part,
            arrived[part],
            slot_dy,
            slot_others[:, part * size : (part + 1) * size].reshape(-1, 1),
            small,
            weight_in,
            weight_back,
            kept,
        )
        payloads.append(payload)
    produced, rows_all, slot_grad, active, d_hidden = kept
    payloads[0] = trade(payloads[0])
    payloads[1] = trade(after(payloads[1], payloads[0]))
    rows_all, slot_grad, active, d_hidden = lax.optimization_barrier(
        (rows_all, slot_grad, active, d_hidden, payloads[0])
    )[:4]
    returned = trade(after(produced, payloads[1]))

    in_rows = expert_in.shape[1]
    out_rows = expert_out.shape[1]
    owned_in = scatter_rep(
        lambda who: trans_times(
            lax.dynamic_slice_in_dim(rows_all, who * in_rows, in_rows, 1), d_hidden
        ),
        rep,
    )
    owned_out = scatter_rep(
        lambda who: trans_times(
            lax.dynamic_slice_in_dim(active, who * out_rows, out_rows, 1), slot_grad
        ),
        rep,
    )

    attended_rel = times_trans(attended, pick).astype(jnp.bfloat16)
    normed_rel = times_trans(normed_two, pick).astype(jnp.bfloat16)
    d_mixed, d_attended, gates, *out_pieces = collect(
        slot_ids,
        expert_ids,
        normed_two,
        mixed,
        cotangent,
        small,
        gain_two,
        weight_out,
        pick,
        attended_rel,
        normed_rel,
        payloads,
    )
    owned_out_weight = ring.scatter(*out_pieces, returned)
    early = owned_out_weight[:, model_width:]
    d_packed, d_base, *qkv_pieces = attention_pull(
        base, starts, packed, d_attended, normed_halves, head_size
    )
    owned_qkv = ring.scatter(*qkv_pieces, returned)
    weight_qkv = jnp.concatenate(
        [natural(first), natural([half[:, : qkv_width - cut] for half in second])], axis=1
    )
    d_normed_one = times_trans(d_packed, weight_qkv)
    inputs = tokens.astype(jnp.float32)
    unused_one, norm_pull_one = jax.vjp(rms_norm, inputs, gain_one)
    d_inputs_norm, d_gain_one = norm_pull_one(d_normed_one)
    token_grad = d_mixed + d_inputs_norm
    bias_local = jnp.dot(d_base, onehot, precision=highest)
    late = jnp.concatenate([d_gain_one.reshape(-1), bias_local.reshape(-1)])
    late = ring.total(late, returned)
    output = finish(slot_ids, gates, mixed, returned)
    return (
        output,
        token_grad,
        ring.own(late[:model_width]),
        owned_qkv,
        owned_out_weight[:, :model_width],
        early[:, -1],
        early[:, :experts],
        add_late(*owned_in, d_packed)[None],
        add_late(*owned_out, d_packed)[None],
        late[model_width:].reshape(bias_table.shape),
    )


def solution(mesh):
    return jax.shard_map(
        functools.partial(shards, mesh.shape["fsdp"], mesh.shape["rep"]),
        mesh=mesh,
        in_specs=(
            P(("fsdp", "rep"), None),
            P(("fsdp", "rep")),
            P(("fsdp", "rep"), None),
            P(("fsdp", "rep"), None),
            P(("fsdp", "rep")),
            P(("fsdp", "rep"), None),
            P("fsdp", "rep", None),
            P("fsdp", "rep", None),
            P(),
            P(("fsdp", "rep"), None),
            P(),
            P(("fsdp", "rep"), None),
            P(("fsdp", "rep"), None),
        ),
        out_specs=(
            P(("fsdp", "rep"), None),
            P(("fsdp", "rep"), None),
            P(("fsdp", "rep")),
            P(("fsdp", "rep"), None),
            P(("fsdp", "rep"), None),
            P(("fsdp", "rep")),
            P(("fsdp", "rep"), None),
            P("fsdp", "rep", None),
            P("fsdp", "rep", None),
            P(),
        ),
        check_vma=False,
    )
```

time: 771 us -> 459 us (0.60)
  waiting for transfers between devices: 231 us -> 100 us
  blocking collectives: 109 us -> 0 us
  local copies, waits for them, and re-layouts: 89.1 us -> 28.7 us
  Pallas kernels: 97.2 us -> 142 us
  matrix products: 91.6 us -> 56.1 us
  starting transfers between devices: 115 us -> 86 us
  other arithmetic: 17 us -> 26.8 us
    psum x1 -> x0, blocking collectives: 109 us -> none  [shards(): bias_grad = lax.psum(jnp.dot(d_base, onehot, precision=highest), both)]
    ppermute x54 -> x43, waiting for transfers between devices: 188 us -> 93.2 us  [swap(): lax.ppermute(rows, axis, [(index, index ^ step) for index in range(size)])]
    ppermute x54 -> x43, starting transfers between devices: 114 us -> 54.4 us  [swap(): lax.ppermute(rows, axis, [(index, index ^ step) for index in range(size)])]
    unnamed x4 -> x3, waiting for transfers between devices: 42.8 us -> 1.39 us
    pallas_call x1 -> x7, Pallas kernels: 54.3 us -> 95.2 us  [the longest x2 59.6 us: expert_rows(): pl.pallas_call(expert_kernel, grid_spec=pltpu.PrefetchScalarGridSpec(num_...]
    all_to_all x0 -> x6, starting transfers between devices: none -> 30.9 us  [trade(): lax.all_to_all(blocks, 'fsdp', split_axis=0, concat_axis=0, tiled=True)]
    dot_general x14 -> x11, matrix products: 69.2 us -> 43.7 us  [trans_times(): lax.dot_general(left_side, right_side, (((0,), (0,)), ((), ())), preferre...]
    unnamed x162 -> x102, local copies, waits for them, and re-layouts: 34.7 us -> 10.5 us
  transfers between devices with their start and end apart: 57 -> 52, of which waited for: 20 -> 19; matrix products, arithmetic and copies ran while one was open for 21% -> 24% of each run, Pallas kernels for 6% -> 31%
where the time goes in v2:
time: 459 us; the launch traced here: 454 us
  Pallas kernels  142 us (31%)
  waiting for transfers between devices  100 us (22%)
  starting transfers between devices  86 us (19%)
  matrix products  56.1 us (12%)
  local copies, waits for them, and re-layouts  28.7 us (6%)
  other arithmetic  26.8 us (6%)
  between operations  15 us (3%)
    ppermute x43, waiting for transfers between devices, swap(): lax.ppermute(rows, axis, [(index, index ^ step) for index in range(size)])  93.2 us
    pallas_call x2, Pallas kernels, expert_rows(): pl.pallas_call(expert_kernel, grid_spec=pltpu.PrefetchScalarGridSpec(num_...  59.6 us
    ppermute x43, starting transfers between devices, swap(): lax.ppermute(rows, axis, [(index, index ^ step) for index in range(size)])  54.4 us
    dot_general x11, matrix products, trans_times(): lax.dot_general(left_side, right_side, (((0,), (0,)), ((), ())), preferre...  43.7 us
    pallas_call x1, Pallas kernels, attention_pull(): pl.pallas_call(functools.partial(attention_pull_kernel, head_size), out_s...  32.5 us
    all_to_all x6, starting transfers between devices, trade(): lax.all_to_all(blocks, 'fsdp', split_axis=0, concat_axis=0, tiled=True)  30.9 us
    pallas_call x1, Pallas kernels, attention(): pl.pallas_call(functools.partial(attention_kernel, head_size), out_shape=...  13.8 us
    pallas_call x1, Pallas kernels, collect(): pl.pallas_call(collect_kernel, out_shape=(jax.ShapeDtypeStruct((row_count...  11.3 us
  transfers between devices with their start and end apart: 52, of which 19 were waited for; matrix products, arithmetic and copies ran while one was open for 24% of the time, Pallas kernels for 31%

profile of v2, /device:TPU:0, one launch (start us, length us, event | category | flops | bytes accessed | tf_op | source)
XLA Modules:
  0.0 454.4 jit_solution(3873621190255710031)
XLA Ops:
  11.9 5.1 %collective-permute-start.2 = (bf16[24,2432]{1,0:T(8,128)(2,1)S(1)}, bf16[24,2432]{1,0:T(8,128)(2,1)S(1)}, u32[]{:S(2)}, u32[]{:S(2)}) collective-permute-start(bf16[24,2432]{1,0:T(8,128)(2,1)S(1)} %concatenate.66), channel_id=1, source_target_pairs={{0,24},{4,28},{8,16},{12,20},{16,8},{20,12},{24,0},{28,4},{1,25},{... | collective-permute-start | bytes 350216 | tf_op jit(solution)/shard_map/ppermute | solution.py:637
  18.7 2.3 reduce-window.21
  22.8 4.6 %spread.1 = bf16[8,256,768]{2,1,0:T(8,128)(2,1)} custom-call(s32[2,512]{1,0:T(2,128)} %copy.87.ids_ref, bf16[512,768]{1,0:T(8,128)(2,1)} %cotangent_ref.1), custom_call_target="tpu_custom_call" | custom-call | flops 1000 | bytes 1000 | tf_op jit(solution)/shard_map/spread/pallas_call | solution.py:300
  27.5 6.0 %all-to-all-start = ((bf16[8,256,768]{2,1,0:T(8,128)(2,1)}), bf16[8,256,768]{2,1,0:T(8,128)(2,1)}, u32[]{:S(2)}, u32[]{:S(2)}) async-start(bf16[8,256,768]{2,1,0:T(8,128)(2,1)} %spread.1), calls=%async_computation | async-start | bytes 6291456 | tf_op jit(solution)/shard_map/all_to_all | solution.py:645
  34.0 2.0 collective-permute-start.11
  36.9 1.6 collective-permute-start.7
  38.4 27.7 %collective-permute-done.8 = bf16[96,1280]{1,0:T(8,128)(2,1)S(1)} collective-permute-done((bf16[96,1280]{1,0:T(8,128)(2,1)S(1)}, bf16[96,1280]{1,0:T(8,128)(2,1)S(1)}, u32[]{:S(2)}, u32[]{:S(2)}) %collective-permute-start.8) | collective-permute-done | bytes 245792 | tf_op jit(solution)/shard_map/ppermute | solution.py:637
  69.8 2.5 collective-permute-start.4
  72.3 4.8 %collective-permute-done.3 = bf16[96,1152]{1,0:T(8,128)(2,1)S(1)} collective-permute-done((bf16[96,1152]{1,0:T(8,128)(2,1)S(1)}, bf16[96,1152]{1,0:T(8,128)(2,1)S(1)}, u32[]{:S(2)}, u32[]{:S(2)}) %collective-permute-start.3) | collective-permute-done | bytes 221216 | tf_op jit(solution)/shard_map/ppermute | solution.py:637
  77.1 2.7 collective-permute-start.5
  80.0 7.6 %collective-permute-done.4 = bf16[96,1152]{1,0:T(8,128)(2,1)S(1)} collective-permute-done((bf16[96,1152]{1,0:T(8,128)(2,1)S(1)}, bf16[96,1152]{1,0:T(8,128)(2,1)S(1)}, u32[]{:S(2)}, u32[]{:S(2)}) %collective-permute-start.4) | collective-permute-done | bytes 221216 | tf_op jit(solution)/shard_map/ppermute | solution.py:637
  87.6 3.6 collective-permute-done.5
  94.1 1.7 fusion.26.tokens_ref
  96.8 6.1 %project.1 = (bf16[512,2304]{1,0:T(8,128)(2,1)}, bf16[512,384]{1,0:T(8,128)(2,1)}, bf16[512,384]{1,0:T(8,128)(2,1)}) custom-call(bf16[512,768]{1,0:T(8,128)(2,1)} %fusion.26.tokens_ref, bf16[384,1152]{1,0:T(8,128)(2,1)} %pad_maximum_fusion.1.refs_0_, bf16[384,1152]{1,0:T(8,128)(2,1)} %collective-permute-done.6.refs_1_, bf16[384,1280]{1,0:T(8,128)(2,1)} %copy-done.4, ...), custom_call_target="tpu_custom_call" | custom-call | flops 1000 | bytes 1000 | tf_op jit(solution)/shard_map/project/pallas_call | solution.py:271
  102.9 13.8 %attention.1.attended_ref = bf16[512,768]{1,0:T(8,128)(2,1)} custom-call(f32[12,512]{1,0:T(8,128)} %convolution_bitcast_fusion.base_ref, s32[512,1]{1,0:T(8,128)} %copy.86.starts_ref, bf16[512,2304]{1,0:T(8,128)(2,1)} %get-tuple-element.56.packed_ref), custom_call_target="tpu_custom_call" | custom-call | flops 1000 | bytes 1000 | tf_op jit(solution)/shard_map/attention/pallas_call | solution.py:118
  118.3 6.7 %mix.1 = (f32[512,768]{1,0:T(8,128)}, bf16[512,768]{1,0:T(8,128)(2,1)}, bf16[8,128,768]{2,1,0:T(8,128)(2,1)}, bf16[8,128,768]{2,1,0:T(8,128)(2,1)}) custom-call(s32[2,512]{1,0:T(2,128)} %copy.87.ids_ref, bf16[512,768]{1,0:T(8,128)(2,1)} %tokens_ref.1, bf16[512,768]{1,0:T(8,128)(2,1)} %attention.1.attended_ref, ...), custom_call_target="tpu_custom_call" | custom-call | flops 1000 | bytes 1000 | tf_op jit(solution)/shard_map/mix/pallas_call | solution.py:322
  125.0 3.7 all-to-all-start.1
  131.8 2.0 collective-permute-start.12
  133.8 22.8 %collective-permute-done.12 = s32[2,512,2]{1,2,0:T(2,128)S(1)} collective-permute-done((s32[2,512,2]{1,2,0:T(2,128)S(1)}, s32[2,512,2]{1,2,0:T(2,128)S(1)}, u32[]{:S(2)}, u32[]{:S(2)}) %collective-permute-start.12) | collective-permute-done | bytes 8224 | tf_op jit(solution)/shard_map/ppermute | solution.py:637
  156.6 3.4 collective-permute-start.13
  160.0 7.4 %collective-permute-done.13 = s32[4,512,2]{1,2,0:T(2,128)S(1)} collective-permute-done((s32[4,512,2]{1,2,0:T(2,128)S(1)}, s32[4,512,2]{1,2,0:T(2,128)S(1)}, u32[]{:S(2)}, u32[]{:S(2)}) %collective-permute-start.13) | collective-permute-done | bytes 16416 | tf_op jit(solution)/shard_map/ppermute | solution.py:637
  170.1 4.5 all-to-all-start.3
  176.7 1.6 constant_dynamic-update-slice_fusion.3
  178.4 1.6 constant_dynamic-update-slice_fusion.2
  180.0 1.6 constant_dynamic-update-slice_fusion.1
  182.5 4.1 all-gather.8.cloned.1.call-done
  186.6 29.8 %expert_rows.2 = (bf16[8,144,768]{2,1,0:T(8,128)(2,1)}, bf16[8,256,768]{2,1,0:T(8,128)(2,1)}, bf16[2048,768]{1,0:T(8,128)(2,1)}, bf16[2048,768]{1,0:T(8,128)(2,1...) custom-call(s32[1]{0:T(128)} %bitcast.10.place_ref, bf16[8,128,768]{2,1,0:T(8,128)(2,1)} %copy-done.20, ...), custom_call_target="tpu_custom_call" | custom-call | flops 19327352832 | bytes 34603008 | tf_op jit(solution)/shard_map/expert_rows/pallas_call | solution.py:430
  216.4 5.8 %all-to-all-start.2 = ((bf16[8,144,768]{2,1,0:T(8,128)(2,1)}), bf16[8,144,768]{2,1,0:T(8,128)(2,1)S(1)}, u32[]{:S(2)}, u32[]{:S(2)}) async-start(bf16[8,144,768]{2,1,0:T(8,128)(2,1)} %get-tuple-element.62), calls=%async_computation.2 | async-start | bytes 3538944 | tf_op jit(solution)/shard_map/all_to_all | solution.py:645
  222.2 2.1 constant_dynamic-update-slice_fusion
  224.4 4.5 convolution_convert_fusion.3
  228.9 3.0 convolution_convert_fusion.2
  231.9 1.7 convolution_convert_fusion.5.attended_ref
  233.6 1.7 convolution_convert_fusion.4.normed_rel_ref
  235.3 29.8 %expert_rows.3 = (bf16[8,144,768]{2,1,0:T(8,128)(2,1)}, bf16[8,256,768]{2,1,0:T(8,128)(2,1)}, bf16[2048,768]{1,0:T(8,128)(2,1)}, bf16[2048,768]{1,0:T(8,128)(2,1...) custom-call(s32[1]{0:T(128)} %bitcast.10.place_ref, ...), custom_call_target="tpu_custom_call", output_to_operand_aliasing={{1}: (7, {}), {2}: (8, {}), {3}: (9, {}), {4}: (10, {}), {5... | custom-call | flops 19327352832 | bytes 34603008 | tf_op jit(solution)/shard_map/expert_rows/pallas_call | solution.py:430
  265.2 6.4 %all-to-all-start.4 = ((bf16[8,144,768]{2,1,0:T(8,128)(2,1)}), bf16[8,144,768]{2,1,0:T(8,128)(2,1)S(1)}, u32[]{:S(2)}, u32[]{:S(2)}) async-start(bf16[8,144,768]{2,1,0:T(8,128)(2,1)} %get-tuple-element.71), calls=%async_computation.4 | async-start | bytes 3538944 | tf_op jit(solution)/shard_map/all_to_all | solution.py:645
  271.6 5.7 %fusion.23 = bf16[768,768]{1,0:T(8,128)(2,1)S(1)} fusion(bf16[2048,768]{1,0:T(8,128)(2,1)} %get-tuple-element.99, bf16[2048,3072]{1,0:T(8,128)(2,1)} %get-tuple-element.98, s32[]{:T(128)S(6)} %select_n.161), kind=kOutput, calls=%fused_computation.41 | convolution fusion | flops 2416508928 | bytes 7471108 | tf_op jit(solution)/shard_map/dot_general | solution.py:41
  277.3 4.7 %fusion.20 = bf16[768,768]{1,0:T(8,128)(2,1)S(1)} fusion(bf16[2048,768]{1,0:T(8,128)(2,1)S(1)} %copy-done.43, bf16[2048,3072]{1,0:T(8,128)(2,1)} %get-tuple-element.98, s32[]{:T(128)S(6)} %select_n.159), kind=kOutput, calls=%fused_computation.40 | convolution fusion | flops 2416508928 | bytes 7471108 | tf_op jit(solution)/shard_map/dot_general | solution.py:41
  282.6 2.8 convolution_convert_fusion
  285.6 2.7 convolution_convert_fusion.1
  288.8 5.8 %add_convert_fusion = bf16[768,768]{1,0:T(8,128)(2,1)} fusion(bf16[768,768]{1,0:T(8,128)(2,1)S(1)} %collective-permute-done.41, bf16[2048,768]{1,0:T(8,128)(2,1)S(1)} %copy-done.43, bf16[2048,3072]{1,0:T(8,128)(2,1)} %get-tuple-element.98, s32[]{:T(128)S(6)} %select_n.160), kind=kOutput, calls=%fused_computation.26 | convolution fusion | flops 2417688576 | bytes 8650756 | tf_op jit(solution)/shard_map/dot_general | solution.py:41
  295.3 3.8 add_convert_fusion.1
  300.4 4.1 convert_add_fusion.2
  304.6 6.0 %convert_add_fusion.1 = f32[768,768]{1,0:T(8,128)} fusion(bf16[768,768]{1,0:T(8,128)(2,1)S(1)} %collective-permute-done.40, bf16[2048,768]{1,0:T(8,128)(2,1)S(1)} %copy-done.43, bf16[2048,3072]{1,0:T(8,128)(2,1)} %get-tuple-element.98, s32[]{:T(128)S(6)} %select_n.158), kind=kOutput, calls=%fused_computation.27 | convolution fusion | flops 2417098752 | bytes 9830404 | tf_op jit(solution)/shard_map/dot_general | solution.py:41
  310.6 1.6 all-to-all-done.4.refs_1_
  313.5 4.6 %all-to-all-start.5 = ((bf16[8,256,768]{2,1,0:T(8,128)(2,1)}), bf16[8,256,768]{2,1,0:T(8,128)(2,1)S(1)}, u32[]{:S(2)}, u32[]{:S(2)}) async-start(bf16[8,256,768]{2,1,0:T(8,128)(2,1)} %get-tuple-element.74), calls=%async_computation.5 | async-start | bytes 6291456 | tf_op jit(solution)/shard_map/all_to_all | solution.py:645
  318.1 11.3 %collect.1 = (f32[512,768]{1,0:T(8,128)}, bf16[512,768]{1,0:T(8,128)(2,1)}, f32[512,2]{1,0:T(8,128)}, f32[384,896]{1,0:T(8,128)}, bf16[384,896]{1,0:T(8,128)(2,1)}) custom-call(s32[512,2]{1,0:T(8,128)} %copy-done.12, s32[512,2]{1,0:T(8,128)} %copy-done.13, s32[2,1152]{1,0:T(2,128)} %pad_add_fusion.3.places_ref, ...), custom_call_target="tpu_custom_call" | custom-call | flops 1000 | bytes 1000 | tf_op jit(solution)/shard_map/collect/pallas_call | solution.py:575
  329.5 32.5 %attention_pull.1 = (bf16[512,2304]{1,0:T(8,128)(2,1)}, f32[12,512]{1,0:T(8,128)}, f32[384,2304]{1,0:T(8,128)}, bf16[384,2304]{1,0:T(8,128)(2,1)}) custom-call(f32[12,512]{1,0:T(8,128)} %convolution_bitcast_fusion.base_ref, s32[512,1]{1,0:T(8,128)} %copy.86.starts_ref, bf16[512,2304]{1,0:T(8,128)(2,1)} %get-tuple-element.56.packed_ref, ...), custom_call_target="tpu_custom_call" | custom-call | flops 1000 | bytes 1000 | tf_op jit(solution)/shard_map/attention_pull/pallas_call | solution.py:206
  363.2 5.3 %fusion.19 = (f32[768]{0:T(1024)S(1)}, f32[512]{0:T(512)S(1)}, f32[512,768]{1,0:T(8,128)S(1)}) fusion(bf16[512,768]{1,0:T(8,128)(2,1)} %tokens_ref.1, f32[512]{0:T(512)S(1)} %copy-done.33, f32[768]{0:T(1024)S(1)} %copy-done.32, bf16[512,2304]{1,0:T(8,128)(2,1)} %get-tuple-element.79, bf16[768,1152]{1,0:T(8,128)(2,1)} %convolution_convert_fusion.2, ...), kind=kOutput, calls=%fused_computation.39 | convolution fusion | flops 1821768448 | bytes 8267776 | tf_op jit(solution)/shard_map/dot_general | solution.py:35
  369.2 3.2 add_bitcast_fusion.1
  373.2 2.9 add_bitcast_fusion
  376.1 2.0 collective-permute-start.16
  378.2 1.6 fusion.15
  382.5 2.1 collective-permute-start.29
  384.6 2.4 collective-permute-done.33
  387.1 1.6 collective-permute-start.34
  391.5 2.2 collective-permute-done.30
  395.2 1.9 collective-permute-start.20
  397.2 7.7 %collective-permute-done.20 = bf16[192,1152]{1,0:T(8,128)(2,1)S(1)} collective-permute-done((bf16[192,1152]{1,0:T(8,128)(2,1)S(1)}, bf16[192,1152]{1,0:T(8,128)(2,1)S(1)}, u32[]{:S(2)}, u32[]{:S(2)}) %collective-permute-start.20) | collective-permute-done | bytes 442400 | tf_op jit(solution)/shard_map/ppermute | solution.py:637
  409.0 2.5 collective-permute-start.17
  413.8 1.9 collective-permute-start.35
  417.9 1.9 collective-permute-start.31
  422.2 1.9 collective-permute-start.26
  424.1 6.9 %finish.1 = bf16[512,768]{1,0:T(8,128)(2,1)} custom-call(s32[512,2]{1,0:T(8,128)} %copy-done.12, f32[512,2]{1,0:T(8,128)} %get-tuple-element.72.gates_ref, f32[512,768]{1,0:T(8,128)} %get-tuple-element.58.mixed_ref, bf16[8,256,768]{2,1,0:T(8,128)(2,1)} %copy-done.2), custom_call_target="tpu_custom_call" | custom-call | flops 1000 | bytes 1000 | tf_op jit(solution)/shard_map/finish/pallas_call | solution.py:619
  445.2 1.6 collective-permute-done.27
  (298 shorter events, 67.7 us)
Async XLA Ops:
  7.2 61.7 %copy-start = (f32[12,32]{1,0:T(8,128)S(1)}, f32[12,32]{1,0:T(8,128)}, u32[]{:S(2)}) copy-start(f32[12,32]{1,0:T(8,128)} %param.21) | copy-start | bytes 4612
  7.2 111.1 %all-gather.4.cloned.1.call-start = ((), (), s32[]{:S(2)}) async-start(), calls=%async_computation.6 | async-start | bytes 1216512 | tf_op jit(solution)/shard_map/all_gather | solution.py:794
  7.9 174.6 %all-gather.6.cloned.1.call-start = ((), (), s32[]{:S(2)}) async-start(), calls=%async_computation.7 | async-start | bytes 5898240 | tf_op jit(solution)/shard_map/all_gather | solution.py:826
  11.9 15.5 %collective-permute-start.2 = (bf16[24,2432]{1,0:T(8,128)(2,1)S(1)}, bf16[24,2432]{1,0:T(8,128)(2,1)S(1)}, u32[]{:S(2)}, u32[]{:S(2)}) collective-permute-start(bf16[24,2432]{1,0:T(8,128)(2,1)S(1)} %concatenate.66), channel_id=1, source_target_pairs={{0,24},{4,28},{8,16},{12,20},{16,8},{20,12},{24,0},{28,4},{1,25},{... | collective-permute-start | bytes 350216 | tf_op jit(solution)/shard_map/ppermute | solution.py:637
  17.1 10.4 %collective-permute-start.1 = (bf16[24,2432]{1,0:T(8,128)(2,1)S(1)}, bf16[24,2432]{1,0:T(8,128)(2,1)S(1)}, u32[]{:S(2)}, u32[]{:S(2)}) collective-permute-start(bf16[24,2432]{1,0:T(8,128)(2,1)S(1)} %concatenate.66), channel_id=1, source_target_pairs={{0,16},{4,20},{8,24},{12,28},{16,0},{20,4},{24,8},{28,12},{1,17},{... | collective-permute-start | bytes 350216 | tf_op jit(solution)/shard_map/ppermute | solution.py:637
  17.1 10.4 %collective-permute-start = (bf16[24,2432]{1,0:T(8,128)(2,1)S(1)}, bf16[24,2432]{1,0:T(8,128)(2,1)S(1)}, u32[]{:S(2)}, u32[]{:S(2)}) collective-permute-start(bf16[24,2432]{1,0:T(8,128)(2,1)S(1)} %concatenate.66), channel_id=1, source_target_pairs={{0,8},{4,12},{8,0},{12,4},{16,24},{20,28},{24,16},{28,20},{1,9},{5... | collective-permute-start | bytes 350216 | tf_op jit(solution)/shard_map/ppermute | solution.py:637
  27.5 97.5 %all-to-all-start = ((bf16[8,256,768]{2,1,0:T(8,128)(2,1)}), bf16[8,256,768]{2,1,0:T(8,128)(2,1)}, u32[]{:S(2)}, u32[]{:S(2)}) async-start(bf16[8,256,768]{2,1,0:T(8,128)(2,1)} %spread.1), calls=%async_computation | async-start | bytes 6291456 | tf_op jit(solution)/shard_map/all_to_all | solution.py:645
  33.5 153.1 %all-gather.8.cloned.1.call-start = ((), (), s32[]{:S(2)}) async-start(), calls=%async_computation.8 | async-start | bytes 5898240 | tf_op jit(solution)/shard_map/all_gather | solution.py:827
  34.0 97.7 %collective-permute-start.11 = (s32[1,512,2]{1,2,0:T(2,128)S(1)}, s32[1,512,2]{1,2,0:T(2,128)S(1)}, u32[]{:S(2)}, u32[]{:S(2)}) collective-permute-start(s32[1,512,2]{1,2,0:T(2,128)S(1)} %bitcast.68), channel_id=1, source_target_pairs={{0,4},{4,0},{8,12},{12,8},{16,20},{20,16},{24,28},{28,24},{1,5},{5... | collective-permute-start | bytes 12296 | tf_op jit(solution)/shard_map/ppermute | solution.py:637
  36.2 30.0 %collective-permute-start.8 = (bf16[96,1280]{1,0:T(8,128)(2,1)S(1)}, bf16[96,1280]{1,0:T(8,128)(2,1)S(1)}, u32[]{:S(2)}, u32[]{:S(2)}) collective-permute-start(bf16[96,1280]{1,0:T(8,128)(2,1)S(1)} %slice.284), channel_id=1, source_target_pairs={{0,4},{4,0},{8,12},{12,8},{16,20},{20,16},{24,28},{28,24},{1,5},{5... | collective-permute-start | bytes 737288 | tf_op jit(solution)/shard_map/ppermute | solution.py:637
  36.3 43.5 %copy-start.41 = (s32[32]{0:T(128)}, s32[32]{0:T(128)S(1)}, u32[]{:S(2)}) copy-start(s32[32]{0:T(128)S(1)} %iota_add_fusion) | copy-start | bytes 388
  36.8 32.0 %copy-start.34 = (s32[512]{0:T(512)}, s32[512]{0:T(512)S(1)}, u32[]{:S(2)}) copy-start(s32[512]{0:T(512)S(1)} %select_reduce_fusion.1) | copy-start | bytes 6148
  36.9 43.0 %collective-permute-start.7 = (bf16[96,1280]{1,0:T(8,128)(2,1)S(1)}, bf16[96,1280]{1,0:T(8,128)(2,1)S(1)}, u32[]{:S(2)}, u32[]{:S(2)}) collective-permute-start(bf16[96,1280]{1,0:T(8,128)(2,1)S(1)} %slice.284), channel_id=1, source_target_pairs={{0,2},{1,3},{2,0},{3,1},{4,6},{5,7},{6,4},{7,5},{8,10},{9,11},{10,... | collective-permute-start | bytes 737288 | tf_op jit(solution)/shard_map/ppermute | solution.py:637
  66.1 13.7 %collective-permute-start.9 = (bf16[96,1280]{1,0:T(8,128)(2,1)S(1)}, bf16[96,1280]{1,0:T(8,128)(2,1)S(1)}, u32[]{:S(2)}, u32[]{:S(2)}) collective-permute-start(bf16[96,1280]{1,0:T(8,128)(2,1)S(1)} %collective-permute-done.8), channel_id=1, source_target_pairs={{0,2},{1,3},{2,0},{3,1},{4,6},{5,7},{6,4},{7,5},{8,10},{9,11},{10,... | collective-permute-start | bytes 737288 | tf_op jit(solution)/shard_map/ppermute | solution.py:637
  68.4 8.8 %collective-permute-start.3 = (bf16[96,1152]{1,0:T(8,128)(2,1)S(1)}, bf16[96,1152]{1,0:T(8,128)(2,1)S(1)}, u32[]{:S(2)}, u32[]{:S(2)}) collective-permute-start(bf16[96,1152]{1,0:T(8,128)(2,1)S(1)} %get-tuple-element.160), channel_id=1, source_target_pairs={{0,2},{1,3},{2,0},{3,1},{4,6},{5,7},{6,4},{7,5},{8,10},{9,11},{10,... | collective-permute-start | bytes 663560 | tf_op jit(solution)/shard_map/ppermute | solution.py:637
  69.8 24.3 %copy-start.8 = (bf16[512,768]{1,0:T(8,128)(2,1)S(1)}, bf16[512,768]{1,0:T(8,128)(2,1)}, u32[]{:S(2)}) copy-start(bf16[512,768]{1,0:T(8,128)(2,1)} %tokens_ref.1) | copy-start | bytes 2359300
  69.8 17.8 %collective-permute-start.4 = (bf16[96,1152]{1,0:T(8,128)(2,1)S(1)}, bf16[96,1152]{1,0:T(8,128)(2,1)S(1)}, u32[]{:S(2)}, u32[]{:S(2)}) collective-permute-start(bf16[96,1152]{1,0:T(8,128)(2,1)S(1)} %get-tuple-element.160), channel_id=1, source_target_pairs={{0,4},{4,0},{8,12},{12,8},{16,20},{20,16},{24,28},{28,24},{1,5},{5... | collective-permute-start | bytes 663560 | tf_op jit(solution)/shard_map/ppermute | solution.py:637
  77.1 14.1 %collective-permute-start.5 = (bf16[96,1152]{1,0:T(8,128)(2,1)S(1)}, bf16[96,1152]{1,0:T(8,128)(2,1)S(1)}, u32[]{:S(2)}, u32[]{:S(2)}) collective-permute-start(bf16[96,1152]{1,0:T(8,128)(2,1)S(1)} %collective-permute-done.3), channel_id=1, source_target_pairs={{0,4},{4,0},{8,12},{12,8},{16,20},{20,16},{24,28},{28,24},{1,5},{5... | collective-permute-start | bytes 663560 | tf_op jit(solution)/shard_map/ppermute | solution.py:637
  80.0 15.9 %copy-start.4 = (bf16[384,1280]{1,0:T(8,128)(2,1)}, bf16[384,1280]{1,0:T(8,128)(2,1)S(1)}, u32[]{:S(2)}) copy-start(bf16[384,1280]{1,0:T(8,128)(2,1)S(1)} %pad_maximum_fusion.refs_2_) | copy-start | bytes 2949124
  80.0 15.9 %collective-permute-start.10 = (bf16[384,1280]{1,0:T(8,128)(2,1)S(1)}, bf16[384,1280]{1,0:T(8,128)(2,1)S(1)}, u32[]{:S(2)}, u32[]{:S(2)}) collective-permute-start(bf16[384,1280]{1,0:T(8,128)(2,1)S(1)} %pad_maximum_fusion.refs_2_), channel_id=1, source_target_pairs={{0,1},{1,0},{2,3},{3,2},{4,5},{5,4},{6,7},{7,6},{8,9},{9,8},{10,11... | collective-permute-start | bytes 2949128 | tf_op jit(solution)/shard_map/ppermute | solution.py:637
  92.2 3.6 collective-permute-start.6
  125.0 45.0 %all-to-all-start.1 = ((bf16[8,128,768]{2,1,0:T(8,128)(2,1)}), bf16[8,128,768]{2,1,0:T(8,128)(2,1)S(1)}, u32[]{:S(2)}, u32[]{:S(2)}) async-start(bf16[8,128,768]{2,1,0:T(8,128)(2,1)} %get-tuple-element.61), calls=%async_computation.1 | async-start | bytes 3145728 | tf_op jit(solution)/shard_map/all_to_all | solution.py:645
  130.6 29.4 %copy-start.30 = (f32[512]{0:T(512)}, f32[512]{0:T(512)S(1)}, u32[]{:S(2)}) copy-start(f32[512]{0:T(512)S(1)} %fusion.16) | copy-start | bytes 6148
  131.8 24.8 %collective-permute-start.12 = (s32[2,512,2]{1,2,0:T(2,128)S(1)}, s32[2,512,2]{1,2,0:T(2,128)S(1)}, u32[]{:S(2)}, u32[]{:S(2)}) collective-permute-start(s32[2,512,2]{1,2,0:T(2,128)S(1)} %pad_add_fusion.4), channel_id=1, source_target_pairs={{0,8},{4,12},{8,0},{12,4},{16,24},{20,28},{24,16},{28,20},{1,9},{5... | collective-permute-start | bytes 24584 | tf_op jit(solution)/shard_map/ppermute | solution.py:637
  156.6 10.8 %collective-permute-start.13 = (s32[4,512,2]{1,2,0:T(2,128)S(1)}, s32[4,512,2]{1,2,0:T(2,128)S(1)}, u32[]{:S(2)}, u32[]{:S(2)}) collective-permute-start(s32[4,512,2]{1,2,0:T(2,128)S(1)} %pad_add_fusion.2), channel_id=1, source_target_pairs={{0,16},{4,20},{8,24},{12,28},{16,0},{20,4},{24,8},{28,12},{1,17},{... | collective-permute-start | bytes 49160 | tf_op jit(solution)/shard_map/ppermute | solution.py:637
  170.1 46.3 %all-to-all-start.3 = ((bf16[8,128,768]{2,1,0:T(8,128)(2,1)}), bf16[8,128,768]{2,1,0:T(8,128)(2,1)}, u32[]{:S(2)}, u32[]{:S(2)}) async-start(bf16[8,128,768]{2,1,0:T(8,128)(2,1)} %get-tuple-element.64), calls=%async_computation.3 | async-start | bytes 3145728 | tf_op jit(solution)/shard_map/all_to_all | solution.py:645
  216.4 48.7 %all-to-all-start.2 = ((bf16[8,144,768]{2,1,0:T(8,128)(2,1)}), bf16[8,144,768]{2,1,0:T(8,128)(2,1)S(1)}, u32[]{:S(2)}, u32[]{:S(2)}) async-start(bf16[8,144,768]{2,1,0:T(8,128)(2,1)} %get-tuple-element.62), calls=%async_computation.2 | async-start | bytes 3538944 | tf_op jit(solution)/shard_map/all_to_all | solution.py:645
  265.2 47.1 %all-to-all-start.4 = ((bf16[8,144,768]{2,1,0:T(8,128)(2,1)}), bf16[8,144,768]{2,1,0:T(8,128)(2,1)S(1)}, u32[]{:S(2)}, u32[]{:S(2)}) async-start(bf16[8,144,768]{2,1,0:T(8,128)(2,1)} %get-tuple-element.71), calls=%async_computation.4 | async-start | bytes 3538944 | tf_op jit(solution)/shard_map/all_to_all | solution.py:645
  282.0 22.5 %collective-permute-start.40 = (bf16[768,768]{1,0:T(8,128)(2,1)S(1)}, bf16[768,768]{1,0:T(8,128)(2,1)S(1)}, u32[]{:S(2)}, u32[]{:S(2)}) collective-permute-start(bf16[768,768]{1,0:T(8,128)(2,1)S(1)} %fusion.20), channel_id=1, source_target_pairs={{0,1},{1,0},{2,3},{3,2},{4,5},{5,4},{6,7},{7,6},{8,9},{9,8},{10,11... | collective-permute-start | bytes 3538952 | tf_op jit(solution)/shard_map/ppermute | solution.py:637
  282.1 6.7 %collective-permute-start.41 = (bf16[768,768]{1,0:T(8,128)(2,1)S(1)}, bf16[768,768]{1,0:T(8,128)(2,1)S(1)}, u32[]{:S(2)}, u32[]{:S(2)}) collective-permute-start(bf16[768,768]{1,0:T(8,128)(2,1)S(1)} %fusion.23), channel_id=1, source_target_pairs={{0,1},{1,0},{2,3},{3,2},{4,5},{5,4},{6,7},{7,6},{8,9},{9,8},{10,11... | collective-permute-start | bytes 3538952 | tf_op jit(solution)/shard_map/ppermute | solution.py:637
  285.4 9.9 %collective-permute-start.38 = (bf16[192,3072]{1,0:T(8,128)(2,1)S(1)}, bf16[192,3072]{1,0:T(8,128)(2,1)S(1)}, u32[]{:S(2)}, u32[]{:S(2)}) collective-permute-start(bf16[192,3072]{1,0:T(8,128)(2,1)S(1)} %convolution_convert_fusion), channel_id=1, source_target_pairs={{0,1},{1,0},{2,3},{3,2},{4,5},{5,4},{6,7},{7,6},{8,9},{9,8},{10,11... | collective-permute-start | bytes 3538952 | tf_op jit(solution)/shard_map/ppermute | solution.py:637
  288.3 12.1 %collective-permute-start.37 = (bf16[192,3072]{1,0:T(8,128)(2,1)S(1)}, bf16[192,3072]{1,0:T(8,128)(2,1)S(1)}, u32[]{:S(2)}, u32[]{:S(2)}) collective-permute-start(bf16[192,3072]{1,0:T(8,128)(2,1)S(1)} %convolution_convert_fusion.1), channel_id=1, source_target_pairs={{0,1},{1,0},{2,3},{3,2},{4,5},{5,4},{6,7},{7,6},{8,9},{9,8},{10,11... | collective-permute-start | bytes 3538952 | tf_op jit(solution)/shard_map/ppermute | solution.py:637
  294.6 68.5 %collective-permute-start.42 = (bf16[768,768]{1,0:T(8,128)(2,1)}, bf16[768,768]{1,0:T(8,128)(2,1)}, u32[]{:S(2)}, u32[]{:S(2)}) collective-permute-start(bf16[768,768]{1,0:T(8,128)(2,1)} %add_convert_fusion), channel_id=1, source_target_pairs={{0,2},{1,3},{2,0},{3,1},{4,6},{5,7},{6,4},{7,5},{8,10},{9,11},{10,... | collective-permute-start | bytes 3538952 | tf_op jit(solution)/shard_map/ppermute | solution.py:637
  299.1 69.4 %collective-permute-start.39 = (bf16[192,3072]{1,0:T(8,128)(2,1)}, bf16[192,3072]{1,0:T(8,128)(2,1)}, u32[]{:S(2)}, u32[]{:S(2)}) collective-permute-start(bf16[192,3072]{1,0:T(8,128)(2,1)} %add_convert_fusion.1), channel_id=1, source_target_pairs={{0,2},{1,3},{2,0},{3,1},{4,6},{5,7},{6,4},{7,5},{8,10},{9,11},{10,... | collective-permute-start | bytes 3538952 | tf_op jit(solution)/shard_map/ppermute | solution.py:637
  313.5 95.5 %all-to-all-start.5 = ((bf16[8,256,768]{2,1,0:T(8,128)(2,1)}), bf16[8,256,768]{2,1,0:T(8,128)(2,1)S(1)}, u32[]{:S(2)}, u32[]{:S(2)}) async-start(bf16[8,256,768]{2,1,0:T(8,128)(2,1)} %get-tuple-element.74), calls=%async_computation.5 | async-start | bytes 6291456 | tf_op jit(solution)/shard_map/all_to_all | solution.py:645
  329.5 50.4 %collective-permute-start.28 = (bf16[384,896]{1,0:T(8,128)(2,1)}, bf16[384,896]{1,0:T(8,128)(2,1)}, u32[]{:S(2)}, u32[]{:S(2)}) collective-permute-start(bf16[384,896]{1,0:T(8,128)(2,1)} %get-tuple-element.87), channel_id=1, source_target_pairs={{0,1},{1,0},{2,3},{3,2},{4,5},{5,4},{6,7},{7,6},{8,9},{9,8},{10,11... | collective-permute-start | bytes 2064392 | tf_op jit(solution)/shard_map/ppermute | solution.py:637
  329.5 32.6 %copy-start.35 = (s32[512]{0:T(512)S(1)}, s32[512]{0:T(512)}, u32[]{:S(2)}) copy-start(s32[512]{0:T(512)} %copy-done.34) | copy-start | bytes 6148
  329.5 32.6 %copy-start.42 = (s32[32]{0:T(128)S(1)}, s32[32]{0:T(128)}, u32[]{:S(2)}) copy-start(s32[32]{0:T(128)} %copy-done.41) | copy-start | bytes 388
  329.5 33.7 %copy-start.32 = (f32[768]{0:T(1024)S(1)}, f32[768]{0:T(1024)}, u32[]{:S(2)}) copy-start(f32[768]{0:T(1024)} %get-tuple-element.161) | copy-start | bytes 9220
  329.5 33.7 %copy-start.33 = (f32[512]{0:T(512)S(1)}, f32[512]{0:T(512)}, u32[]{:S(2)}) copy-start(f32[512]{0:T(512)} %fusion.70) | copy-start | bytes 6148
  368.6 3.8 collective-permute-start.14
  369.1 24.6 %collective-permute-start.19 = (bf16[384,2304]{1,0:T(8,128)(2,1)S(1)}, bf16[384,2304]{1,0:T(8,128)(2,1)S(1)}, u32[]{:S(2)}, u32[]{:S(2)}) collective-permute-start(bf16[384,2304]{1,0:T(8,128)(2,1)S(1)} %copy-done.39), channel_id=1, source_target_pairs={{0,1},{1,0},{2,3},{3,2},{4,5},{5,4},{6,7},{7,6},{8,9},{9,8},{10,11... | collective-permute-start | bytes 5308424 | tf_op jit(solution)/shard_map/ppermute | solution.py:637
  372.4 3.7 collective-permute-start.15
  376.1 3.7 collective-permute-start.16
  381.2 5.9 %collective-permute-start.33 = (bf16[192,384]{1,0:T(8,128)(2,1)S(1)}, bf16[192,384]{1,0:T(8,128)(2,1)S(1)}, u32[]{:S(2)}, u32[]{:S(2)}) collective-permute-start(bf16[192,384]{1,0:T(8,128)(2,1)S(1)} %pad_maximum_fusion.5), channel_id=1, source_target_pairs={{0,2},{1,3},{2,0},{3,1},{4,6},{5,7},{6,4},{7,5},{8,10},{9,11},{10,... | collective-permute-start | bytes 442376 | tf_op jit(solution)/shard_map/ppermute | solution.py:637
  382.5 6.4 %collective-permute-start.29 = (bf16[192,512]{1,0:T(8,128)(2,1)S(1)}, bf16[192,512]{1,0:T(8,128)(2,1)S(1)}, u32[]{:S(2)}, u32[]{:S(2)}) collective-permute-start(bf16[192,512]{1,0:T(8,128)(2,1)S(1)} %slice.315), channel_id=1, source_target_pairs={{0,4},{4,0},{8,12},{12,8},{16,20},{20,16},{24,28},{28,24},{1,5},{5... | collective-permute-start | bytes 589832 | tf_op jit(solution)/shard_map/ppermute | solution.py:637
  387.1 4.4 collective-permute-start.34
  389.0 4.7 %collective-permute-start.30 = (bf16[96,512]{1,0:T(8,128)(2,1)S(1)}, bf16[96,512]{1,0:T(8,128)(2,1)S(1)}, u32[]{:S(2)}, u32[]{:S(2)}) collective-permute-start(bf16[96,512]{1,0:T(8,128)(2,1)S(1)} %slice.371), channel_id=1, source_target_pairs={{0,2},{1,3},{2,0},{3,1},{4,6},{5,7},{6,4},{7,5},{8,10},{9,11},{10,... | collective-permute-start | bytes 294920 | tf_op jit(solution)/shard_map/ppermute | solution.py:637
  394.2 12.5 %collective-permute-start.24 = (bf16[192,1152]{1,0:T(8,128)(2,1)S(1)}, bf16[192,1152]{1,0:T(8,128)(2,1)S(1)}, u32[]{:S(2)}, u32[]{:S(2)}) collective-permute-start(bf16[192,1152]{1,0:T(8,128)(2,1)S(1)} %pad_maximum_fusion.3), channel_id=1, source_target_pairs={{0,2},{1,3},{2,0},{3,1},{4,6},{5,7},{6,4},{7,5},{8,10},{9,11},{10,... | collective-permute-start | bytes 1327112 | tf_op jit(solution)/shard_map/ppermute | solution.py:637
  395.2 9.7 %collective-permute-start.20 = (bf16[192,1152]{1,0:T(8,128)(2,1)S(1)}, bf16[192,1152]{1,0:T(8,128)(2,1)S(1)}, u32[]{:S(2)}, u32[]{:S(2)}) collective-permute-start(bf16[192,1152]{1,0:T(8,128)(2,1)S(1)} %slice.299), channel_id=1, source_target_pairs={{0,4},{4,0},{8,12},{12,8},{16,20},{20,16},{24,28},{28,24},{1,5},{5... | collective-permute-start | bytes 1327112 | tf_op jit(solution)/shard_map/ppermute | solution.py:637
  405.8 6.2 %collective-permute-start.21 = (bf16[96,1152]{1,0:T(8,128)(2,1)}, bf16[96,1152]{1,0:T(8,128)(2,1)}, u32[]{:S(2)}, u32[]{:S(2)}) collective-permute-start(bf16[96,1152]{1,0:T(8,128)(2,1)} %slice.368), channel_id=1, source_target_pairs={{0,2},{1,3},{2,0},{3,1},{4,6},{5,7},{6,4},{7,5},{8,10},{9,11},{10,... | collective-permute-start | bytes 663560 | tf_op jit(solution)/shard_map/ppermute | solution.py:637
  407.9 8.9 %collective-permute-start.25 = (bf16[96,1152]{1,0:T(8,128)(2,1)}, bf16[96,1152]{1,0:T(8,128)(2,1)}, u32[]{:S(2)}, u32[]{:S(2)}) collective-permute-start(bf16[96,1152]{1,0:T(8,128)(2,1)} %slice.367), channel_id=1, source_target_pairs={{0,4},{4,0},{8,12},{12,8},{16,20},{20,16},{24,28},{28,24},{1,5},{5... | collective-permute-start | bytes 663560 | tf_op jit(solution)/shard_map/ppermute | solution.py:637
  409.0 15.1 %copy-start.2 = (bf16[8,256,768]{2,1,0:T(8,128)(2,1)}, bf16[8,256,768]{2,1,0:T(8,128)(2,1)S(1)}, u32[]{:S(2)}) copy-start(bf16[8,256,768]{2,1,0:T(8,128)(2,1)S(1)} %all-to-all-done.5.produced_ref) | copy-start | bytes 9437188
  409.0 6.7 %collective-permute-start.17 = (f32[1152]{0:T(1024)S(1)}, f32[1152]{0:T(1024)S(1)}, u32[]{:S(2)}, u32[]{:S(2)}) collective-permute-start(f32[1152]{0:T(1024)S(1)} %add.345), channel_id=1, source_target_pairs={{0,8},{4,12},{8,0},{12,4},{16,24},{20,28},{24,16},{28,20},{1,9},{5... | collective-permute-start | bytes 13832 | tf_op jit(solution)/shard_map/ppermute | solution.py:637
  413.8 18.4 %collective-permute-start.35 = (bf16[48,384]{1,0:T(8,128)(2,1)}, bf16[48,384]{1,0:T(8,128)(2,1)}, u32[]{:S(2)}, u32[]{:S(2)}) collective-permute-start(bf16[48,384]{1,0:T(8,128)(2,1)} %slice.376), channel_id=1, source_target_pairs={{0,16},{4,20},{8,24},{12,28},{16,0},{20,4},{24,8},{28,12},{1,17},{... | collective-permute-start | bytes 110600 | tf_op jit(solution)/shard_map/ppermute | solution.py:637
  415.7 15.3 %collective-permute-start.18 = (f32[1152]{0:T(1024)S(1)}, f32[1152]{0:T(1024)S(1)}, u32[]{:S(2)}, u32[]{:S(2)}) collective-permute-start(f32[1152]{0:T(1024)S(1)} %add.346), channel_id=1, source_target_pairs={{0,16},{4,20},{8,24},{12,28},{16,0},{20,4},{24,8},{28,12},{1,17},{... | collective-permute-start | bytes 13832 | tf_op jit(solution)/shard_map/ppermute | solution.py:637
  417.9 16.7 %collective-permute-start.31 = (bf16[48,512]{1,0:T(8,128)(2,1)S(1)}, bf16[48,512]{1,0:T(8,128)(2,1)}, u32[]{:S(2)}, u32[]{:S(2)}) collective-permute-start(bf16[48,512]{1,0:T(8,128)(2,1)S(1)} %slice.375), channel_id=1, source_target_pairs={{0,16},{4,20},{8,24},{12,28},{16,0},{20,4},{24,8},{28,12},{1,17},{... | collective-permute-start | bytes 147464 | tf_op jit(solution)/shard_map/ppermute | solution.py:637
  420.5 19.5 %collective-permute-start.22 = (bf16[48,1152]{1,0:T(8,128)(2,1)}, bf16[48,1152]{1,0:T(8,128)(2,1)}, u32[]{:S(2)}, u32[]{:S(2)}) collective-permute-start(bf16[48,1152]{1,0:T(8,128)(2,1)} %slice.370), channel_id=1, source_target_pairs={{0,16},{4,20},{8,24},{12,28},{16,0},{20,4},{24,8},{28,12},{1,17},{... | collective-permute-start | bytes 331784 | tf_op jit(solution)/shard_map/ppermute | solution.py:637
  422.2 19.4 %collective-permute-start.26 = (bf16[48,1152]{1,0:T(8,128)(2,1)}, bf16[48,1152]{1,0:T(8,128)(2,1)}, u32[]{:S(2)}, u32[]{:S(2)}) collective-permute-start(bf16[48,1152]{1,0:T(8,128)(2,1)} %slice.369), channel_id=1, source_target_pairs={{0,16},{4,20},{8,24},{12,28},{16,0},{20,4},{24,8},{28,12},{1,17},{... | collective-permute-start | bytes 331784 | tf_op jit(solution)/shard_map/ppermute | solution.py:637
  424.1 23.5 %copy-start.1 = (f32[12,32]{1,0:T(8,128)S(1)}, f32[12,32]{1,0:T(8,128)}, u32[]{:S(2)}) copy-start(f32[12,32]{1,0:T(8,128)} %param.21) | copy-start | bytes 4612
  433.0 3.8 collective-permute-start.36
  435.4 3.9 collective-permute-start.32
  441.0 4.2 collective-permute-start.23
  442.6 4.2 collective-permute-start.27
  (37 other events, 222.6 us)
Sparse Core Ops, SparseCore 0:
  10.9 99.2 all-gather.3
  111.8 35.6 all-gather.5
  149.1 37.4 all-gather.7

commit v3 on v2

--- a/solution.py
+++ b/solution.py
@@ -74,22 +74,20 @@
     return pltpu.roll(spread, 0, 1, stride=1, stride_axis=0)
 
 
-def tile_probs(query_tile, keys, strip, starts, tile, scale):
+def tile_score(query_tile, keys, strip, starts, tile, scale):
     row_count = strip.shape[1]
     width = TILE * (tile + 1)
     score = times_trans(query_tile, keys[:width]) * scale + strip[:, row_count - width :]
     place = lax.broadcasted_iota(jnp.int32, score.shape, 1)
     row = lax.broadcasted_iota(jnp.int32, score.shape, 0) + TILE * tile
-    score = jnp.where((place <= row) & (place >= starts), score, MASKED)
-    exponent = jnp.exp(score - jnp.max(score, axis=1, keepdims=True))
-    return exponent * (1.0 / jnp.sum(exponent, axis=1, keepdims=True))
+    return jnp.where((place <= row) & (place >= starts), score, MASKED)
 
 
 def lane_block(first):
     return pl.ds(pl.multiple_of(first, LANES), LANES)
 
 
-def attention_kernel(head_size, base_ref, starts_ref, packed_ref, attended_ref):
+def attention_kernel(head_size, base_ref, starts_ref, packed_ref, attended_ref, level_ref):
     row_count, width = attended_ref.shape
     per_block = LANES // head_size
     scale = head_size ** (-0.5)
@@ -105,9 +103,14 @@
             starts = starts_ref[rows, :]
             total = jnp.zeros((TILE, LANES), jnp.float32)
             for own in range(per_block):
-                probs = tile_probs(
+                score = tile_score(
                     head_lanes(queries[rows], own, head_size), keys, strips[own], starts, tile, scale
-                ).astype(jnp.bfloat16)
+                )
+                peak = jnp.max(score, axis=1, keepdims=True)
+                exponent = jnp.exp(score - peak)
+                whole = jnp.sum(exponent, axis=1, keepdims=True)
+                level_ref[block, rows, own : own + 1] = peak + jnp.log(whole)
+                probs = (exponent * (1.0 / whole)).astype(jnp.bfloat16)
                 total += times(probs, head_lanes(values[: probs.shape[1]], own, head_size))
             attended_ref[rows, lane_block(block * LANES)] = total.astype(jnp.bfloat16)
 
@@ -117,7 +120,10 @@
     width = packed.shape[1] // 3
     return pl.pallas_call(
         functools.partial(attention_kernel, head_size),
-        out_shape=jax.ShapeDtypeStruct((row_count, width), jnp.bfloat16),
+        out_shape=(
+            jax.ShapeDtypeStruct((row_count, width), jnp.bfloat16),
+            jax.ShapeDtypeStruct((width // LANES, row_count, LANES // head_size), jnp.float32),
+        ),
         compiler_params=pltpu.CompilerParams(vmem_limit_bytes=VMEM_BYTES),
         cost_estimate=pl.CostEstimate(flops=1000, bytes_accessed=1000, transcendentals=0),
         name="attention",
@@ -130,8 +136,11 @@
     starts_ref,
     packed_ref,
     grad_ref,
+    level_ref,
     kept_rows_ref,
     sent_rows_ref,
+    out_keep_ref,
+    out_send_ref,
     d_packed_ref,
     d_base_ref,
     keep_ref,
@@ -162,7 +171,8 @@
             for own in range(per_block):
                 own_queries = head_lanes(queries[rows], own, head_size)
                 own_grads = head_lanes(grads[rows], own, head_size)
-                probs = tile_probs(own_queries, keys, strips[own], starts, tile, scale)
+                score = tile_score(own_queries, keys, strips[own], starts, tile, scale)
+                probs = jnp.exp(score - level_ref[block, rows, own : own + 1])
                 d_probs = times_trans(own_grads, values[:reach])
                 row_delta = jnp.sum(probs * d_probs, axis=1, keepdims=True)
                 d_score = (probs * (d_probs - row_delta)).astype(jnp.bfloat16)
@@ -192,6 +202,8 @@
                 folded, axis=0, keepdims=True
             )
 
+    keep_ref[:, 3 * width :] = out_keep_ref[...]
+    send_ref[:, 3 * width :] = out_send_ref[...]
     for start in range(0, 3 * width, width):
         columns = slice(start, start + width)
         send_ref[:, columns] = trans_times(sent_rows_ref[...], d_packed_ref[:, columns]).astype(
@@ -200,16 +212,18 @@
         keep_ref[:, columns] = trans_times(kept_rows_ref[...], d_packed_ref[:, columns])
 
 
-def attention_pull(base, starts, packed, grads, rows, head_size):
-    row_count, width = grads.shape
+def attention_pull(base, starts, packed, grads, levels, rows, out_pieces, head_size):
+    row_count = grads.shape[0]
     half = rows[0].shape[1]
+    columns = packed.shape[1] + out_pieces[0].shape[1]
+    shape = jax.ShapeDtypeStruct
     return pl.pallas_call(
         functools.partial(attention_pull_kernel, head_size),
         out_shape=(
-            jax.ShapeDtypeStruct(packed.shape, jnp.bfloat16),
-            jax.ShapeDtypeStruct(base.shape, jnp.float32),
-            jax.ShapeDtypeStruct((half, packed.shape[1]), jnp.float32),
-            jax.ShapeDtypeStruct((half, packed.shape[1]), jnp.bfloat16),
+            shape(packed.shape, jnp.bfloat16),
+            shape(base.shape, jnp.float32),
+            shape((half, columns), jnp.float32),
+            shape((half, columns), jnp.bfloat16),
         ),
         scratch_shapes=[
             pltpu.VMEM((row_count, LANES), jnp.float32),
@@ -219,7 +233,7 @@
         compiler_params=pltpu.CompilerParams(vmem_limit_bytes=VMEM_BYTES),
         cost_estimate=pl.CostEstimate(flops=1000, bytes_accessed=1000, transcendentals=0),
         name="attention_pull",
-    )(base, starts, packed, grads, *rows)
+    )(base, starts, packed, grads, levels, *rows, *out_pieces)
 
 
 def gelu_parts(values):
@@ -333,6 +347,7 @@
 
 
 def expert_kernel(
+    part,
     place_ref,
     rows_ref,
     grads_ref,
@@ -342,7 +357,8 @@
     out_ref,
     *refs,
 ):
-    payload_ref, produced_ref, rows_all, slot_grad_all, active_ref, d_hidden_ref = refs[-10:-4]
+    payload_ref, produced_ref, rows_all, slot_grad_all, active_ref, d_hidden_ref = refs[-11:-5]
+    tails_ref = refs[-5] if part == 0 else refs[0]
     rows, slot_grad, produced_sum, row_sum = refs[-4:]
     sources, capacity, width = rows_ref.shape
     count = sources * capacity
@@ -385,10 +401,14 @@
             )
             across = jnp.transpose(jnp.broadcast_to(d_gate, (capacity, LANES)))[:TAIL, :]
             high = across.astype(jnp.bfloat16).astype(jnp.float32)
-            row = lax.broadcasted_iota(jnp.int32, across.shape, 0)
+            row = lax.broadcasted_iota(jnp.int32, across.shape, 0) - 2 * part
             tail = jnp.where(row == 0, high, jnp.where(row == 1, across - high, 0.0))
-            payload_ref[source, capacity:, :] = jnp.zeros((TAIL, width), jnp.bfloat16)
-            payload_ref[source, capacity:, :capacity] = tail.astype(jnp.bfloat16)
+            if part == 0:
+                tails_ref[source, :, :] = tail
+            else:
+                tail = (tails_ref[source, :, :] + tail).astype(jnp.bfloat16)
+                payload_ref[source, capacity:, :] = jnp.zeros((TAIL, width), jnp.bfloat16)
+                payload_ref[source, capacity:, :capacity] = tail
 
 
 def expert_rows(place, part, rows, grads, other, router, weight_in, weight_out, earlier):
@@ -424,22 +444,26 @@
     ]
     aliases = {}
     if earlier is not None:
+        earlier, tails = earlier[:-1], earlier[-1]
+        operands = operands + (tails,)
+        in_specs = in_specs + [whole(tails.shape)]
         aliases = {1 + len(operands) + which: 1 + which for which in range(5)}
         operands = operands + tuple(earlier)
         in_specs = in_specs + [pl.BlockSpec(memory_space=pl.ANY)] * 5
     results = pl.pallas_call(
-        expert_kernel,
+        functools.partial(expert_kernel, part),
         grid_spec=pltpu.PrefetchScalarGridSpec(
             num_scalar_prefetch=1,
             grid=(4,),
             in_specs=in_specs,
             out_specs=[
-                whole((sources, capacity + TAIL, width)),
+                whole((sources, capacity + part * TAIL, width)),
                 part_of(sources, capacity, width),
                 part_block(width),
                 part_block(width),
                 part_chunk(),
                 part_chunk(),
+                whole((sources, TAIL, capacity)),
             ],
             scratch_shapes=[
                 pltpu.VMEM((count, width), jnp.bfloat16),
@@ -449,12 +473,13 @@
             ],
         ),
         out_shape=[
-            full(sources, capacity + TAIL, width),
+            full(sources, capacity + part * TAIL, width),
             full(sources, PARTS * capacity, width),
             full(total, width),
             full(total, width),
             full(total, hidden_width),
             full(total, hidden_width),
+            jax.ShapeDtypeStruct((sources, TAIL, capacity), jnp.float32),
         ],
         input_output_aliases=aliases,
         compiler_params=pltpu.CompilerParams(vmem_limit_bytes=VMEM_BYTES),
@@ -486,7 +511,7 @@
     payload_refs = refs[:-5]
     d_mixed_ref, d_attended_ref, gates_ref, keep_ref, send_ref = refs[-5:]
     row_count, width = mixed_ref.shape
-    experts, capacity = payload_refs[0].shape[0], payload_refs[0].shape[1] - TAIL
+    experts, capacity, _ = payload_refs[0].shape
     first_slots, second_slots = slots_ref[:, 0:1], slots_ref[:, 1:2]
     first_grad = jnp.zeros((row_count, 1), jnp.float32)
     second_grad = jnp.zeros((row_count, 1), jnp.float32)
@@ -494,13 +519,12 @@
     for part, payload_ref in enumerate(payload_refs):
         places = places_ref[part : part + 1, :]
         select = jnp.where((places == first_slots) | (places == second_slots), 1.0, 0.0)
-        rows = payload_ref[...].reshape(experts * (capacity + TAIL), width)
-        d_normed += times(select.astype(jnp.bfloat16), rows)
+        d_normed += times(select.astype(jnp.bfloat16), payload_ref[:, :capacity, :].reshape(-1, width))
         for expert in range(experts):
             first_place = (expert * len(payload_refs) + part) * capacity
             place = first_place + lax.broadcasted_iota(jnp.int32, (row_count, capacity), 1)
-            tail = payload_ref[expert, capacity:, :capacity].astype(jnp.float32)
-            d_gate = tail[0:1, :] + tail[1:2, :]
+            tail = payload_refs[-1][expert, capacity:, :capacity].astype(jnp.float32)
+            d_gate = tail[2 * part : 2 * part + 1, :] + tail[2 * part + 1 : 2 * part + 2, :]
             first_grad += jnp.sum(
                 jnp.where(place == first_slots, d_gate, 0.0), axis=1, keepdims=True
             )
@@ -557,20 +581,13 @@
     payloads,
 ):
     row_count, width = mixed.shape
-    sources, tall, _ = payloads[0].shape
-    inside = jnp.arange(tall, dtype=jnp.int32)
-    places = jnp.stack(
-        [
-            jnp.where(
-                inside[None, :] < tall - TAIL,
-                (jnp.arange(sources, dtype=jnp.int32)[:, None] * len(payloads) + part)
-                * (tall - TAIL)
-                + inside[None, :],
-                -1,
-            ).reshape(-1)
-            for part in range(len(payloads))
-        ]
-    )
+    sources, size, _ = payloads[0].shape
+    places = (
+        (jnp.arange(sources, dtype=jnp.int32)[None, :, None] * len(payloads)
+        + jnp.arange(len(payloads), dtype=jnp.int32)[:, None, None])
+        * size
+        + jnp.arange(size, dtype=jnp.int32)[None, None, :]
+    ).reshape(len(payloads), sources * size)
     columns = width + router.shape[1]
     return pl.pallas_call(
         collect_kernel,
@@ -701,8 +718,8 @@
         if not self.relative:
             whole = jnp.concatenate([keep, send.astype(jnp.float32)])
             return lax.psum_scatter(whole, ("fsdp", "rep"), scatter_dimension=0, tiled=True)
+        total = keep + self.hop(send, 1).astype(jnp.float32)
         low = jnp.bfloat16
-        total = keep + self.hop(send, 1).astype(jnp.float32)
         cut = -(-total.shape[1] // 256) * 128
         results = []
         quarter = self.half // 4
@@ -834,7 +851,7 @@
     small = natural([half[:, qkv_width - cut :] for half in second])
     gains = small.T.astype(jnp.float32)
     gain_one, gain_two = gains[experts : experts + 1], gains[experts + 1 : experts + 2]
-    attended = attention(base, starts, packed, head_size)
+    attended, levels = attention(base, starts, packed, head_size)
     mixed, normed_two, *sending = mix(
         slot_ids_across, tokens, attended, weight_out, gain_two, experts, capacity
     )
@@ -856,7 +873,7 @@
             kept,
         )
         payloads.append(payload)
-    produced, rows_all, slot_grad, active, d_hidden = kept
+    produced, rows_all, slot_grad, active, d_hidden, unused_tails = kept
     payloads[0] = trade(payloads[0])
     payloads[1] = trade(after(payloads[1], payloads[0]))
     rows_all, slot_grad, active, d_hidden = lax.optimization_barrier(
@@ -895,12 +912,10 @@
         normed_rel,
         payloads,
     )
-    owned_out_weight = ring.scatter(*out_pieces, returned)
-    early = owned_out_weight[:, model_width:]
-    d_packed, d_base, *qkv_pieces = attention_pull(
-        base, starts, packed, d_attended, normed_halves, head_size
-    )
-    owned_qkv = ring.scatter(*qkv_pieces, returned)
+    d_packed, d_base, *pieces = attention_pull(
+        base, starts, packed, d_attended, levels, normed_halves, out_pieces, head_size
+    )
+    owned = ring.scatter(*pieces, returned)
     weight_qkv = jnp.concatenate(
         [natural(first), natural([half[:, : qkv_width - cut] for half in second])], axis=1
     )
@@ -917,10 +932,10 @@
         output,
         token_grad,
         ring.own(late[:model_width]),
-        owned_qkv,
-        owned_out_weight[:, :model_width],
-        early[:, -1],
-        early[:, :experts],
+        owned[:, :qkv_width],
+        owned[:, qkv_width : qkv_width + model_width],
+        owned[:, -1],
+        owned[:, qkv_width + model_width : qkv_width + model_width + experts],
         add_late(*owned_in, d_packed)[None],
         add_late(*owned_out, d_packed)[None],
         late[model_width:].reshape(bias_table.shape),

time: 459 us -> 440 us (0.959)
  starting transfers between devices: 86 us -> 71.1 us
    ppermute x43 -> x34, starting transfers between devices: 54.4 us -> 39.3 us  [swap(): lax.ppermute(rows, axis, [(index, index ^ step) for index in range(size)])]
    ppermute x43 -> x34, waiting for transfers between devices: 93.2 us -> 96.7 us  [swap(): lax.ppermute(rows, axis, [(index, index ^ step) for index in range(size)])]
    unnamed x102 -> x81, local copies, waits for them, and re-layouts: 10.5 us -> 13.4 us
  transfers between devices with their start and end apart: 52 -> 43, of which waited for: 19 -> 15; matrix products, arithmetic and copies ran while one was open for 24% -> 24% of each run, Pallas kernels for 31% -> 32%
where the time goes in v3:
time: 440 us; the launch traced here: 436 us
  Pallas kernels  138 us (31%)
  waiting for transfers between devices  103 us (23%)
  starting transfers between devices  71.1 us (16%)
  matrix products  56.1 us (13%)
  local copies, waits for them, and re-layouts  30.2 us (7%)
  other arithmetic  23.1 us (5%)
  between operations  14.8 us (3%)
    ppermute x34, waiting for transfers between devices, swap(): lax.ppermute(rows, axis, [(index, index ^ step) for index in range(size)])  96.7 us
    pallas_call x2, Pallas kernels, expert_rows(): pl.pallas_call(functools.partial(expert_kernel, part), grid_spec=pltpu.Pr...  60 us
    dot_general x11, matrix products, trans_times(): lax.dot_general(left_side, right_side, (((0,), (0,)), ((), ())), preferre...  43.7 us
    ppermute x34, starting transfers between devices, swap(): lax.ppermute(rows, axis, [(index, index ^ step) for index in range(size)])  39.3 us
    all_to_all x6, starting transfers between devices, trade(): lax.all_to_all(blocks, 'fsdp', split_axis=0, concat_axis=0, tiled=True)  31.1 us
    pallas_call x1, Pallas kernels, attention_pull(): pl.pallas_call(functools.partial(attention_pull_kernel, head_size), out_s...  29 us
    pallas_call x1, Pallas kernels, attention(): pl.pallas_call(functools.partial(attention_kernel, head_size), out_shape=...  14.2 us
    unnamed x81, local copies, waits for them, and re-layouts  13.4 us
  transfers between devices with their start and end apart: 43, of which 15 were waited for; matrix products, arithmetic and copies ran while one was open for 24% of the time, Pallas kernels for 32%

profile of v3, /device:TPU:0, one launch (start us, length us, event | category | flops | bytes accessed | tf_op | source)
XLA Modules:
  0.0 435.9 jit_solution(13971149733932747620)
XLA Ops:
  11.9 5.1 %collective-permute-start.2 = (bf16[24,2432]{1,0:T(8,128)(2,1)S(1)}, bf16[24,2432]{1,0:T(8,128)(2,1)S(1)}, u32[]{:S(2)}, u32[]{:S(2)}) collective-permute-start(bf16[24,2432]{1,0:T(8,128)(2,1)S(1)} %concatenate.56), channel_id=1, source_target_pairs={{0,24},{4,28},{8,16},{12,20},{16,8},{20,12},{24,0},{28,4},{1,25},{... | collective-permute-start | bytes 350216 | tf_op jit(solution)/shard_map/ppermute | solution.py:654
  18.7 2.3 reduce-window.21
  22.8 4.6 %spread.1 = bf16[8,256,768]{2,1,0:T(8,128)(2,1)} custom-call(s32[2,512]{1,0:T(2,128)} %copy.87.ids_ref, bf16[512,768]{1,0:T(8,128)(2,1)} %cotangent_ref.1), custom_call_target="tpu_custom_call" | custom-call | flops 1000 | bytes 1000 | tf_op jit(solution)/shard_map/spread/pallas_call | solution.py:314
  27.5 6.1 %all-to-all-start = ((bf16[8,256,768]{2,1,0:T(8,128)(2,1)}), bf16[8,256,768]{2,1,0:T(8,128)(2,1)}, u32[]{:S(2)}, u32[]{:S(2)}) async-start(bf16[8,256,768]{2,1,0:T(8,128)(2,1)} %spread.1), calls=%async_computation | async-start | bytes 6291456 | tf_op jit(solution)/shard_map/all_to_all | solution.py:662
  34.2 2.0 collective-permute-start.11
  38.1 1.5 collective-permute-start.7
  39.6 26.7 %collective-permute-done.8 = bf16[96,1280]{1,0:T(8,128)(2,1)S(1)} collective-permute-done((bf16[96,1280]{1,0:T(8,128)(2,1)S(1)}, bf16[96,1280]{1,0:T(8,128)(2,1)S(1)}, u32[]{:S(2)}, u32[]{:S(2)}) %collective-permute-start.8) | collective-permute-done | bytes 245792 | tf_op jit(solution)/shard_map/ppermute | solution.py:654
  66.3 1.5 collective-permute-start.9
  69.0 2.5 collective-permute-start.4
  71.5 5.8 %collective-permute-done.3 = bf16[96,1152]{1,0:T(8,128)(2,1)S(1)} collective-permute-done((bf16[96,1152]{1,0:T(8,128)(2,1)S(1)}, bf16[96,1152]{1,0:T(8,128)(2,1)S(1)}, u32[]{:S(2)}, u32[]{:S(2)}) %collective-permute-start.3) | collective-permute-done | bytes 221216 | tf_op jit(solution)/shard_map/ppermute | solution.py:654
  77.3 2.7 collective-permute-start.5
  80.2 7.0 %collective-permute-done.4 = bf16[96,1152]{1,0:T(8,128)(2,1)S(1)} collective-permute-done((bf16[96,1152]{1,0:T(8,128)(2,1)S(1)}, bf16[96,1152]{1,0:T(8,128)(2,1)S(1)}, u32[]{:S(2)}, u32[]{:S(2)}) %collective-permute-start.4) | collective-permute-done | bytes 221216 | tf_op jit(solution)/shard_map/ppermute | solution.py:654
  87.2 4.2 collective-permute-done.5
  93.8 1.7 fusion.26.tokens_ref
  96.5 6.1 %project.1 = (bf16[512,2304]{1,0:T(8,128)(2,1)}, bf16[512,384]{1,0:T(8,128)(2,1)}, bf16[512,384]{1,0:T(8,128)(2,1)}) custom-call(bf16[512,768]{1,0:T(8,128)(2,1)} %fusion.26.tokens_ref, bf16[384,1152]{1,0:T(8,128)(2,1)} %pad_maximum_fusion.1.refs_0_, bf16[384,1152]{1,0:T(8,128)(2,1)} %collective-permute-done.6.refs_1_, bf16[384,1280]{1,0:T(8,128)(2,1)} %copy-done.4, ...), custom_call_target="tpu_custom_call" | custom-call | flops 1000 | bytes 1000 | tf_op jit(solution)/shard_map/project/pallas_call | solution.py:285
  102.6 14.2 %attention.1 = (bf16[512,768]{1,0:T(8,128)(2,1)}, f32[6,512,2]{2,1,0:T(8,128)}) custom-call(f32[12,512]{1,0:T(8,128)} %convolution_bitcast_fusion.base_ref, s32[512,1]{1,0:T(8,128)} %copy.86.starts_ref, bf16[512,2304]{1,0:T(8,128)(2,1)} %get-tuple-element.57.packed_ref), custom_call_target="tpu_custom_call" | custom-call | flops 1000 | bytes 1000 | tf_op jit(solution)/shard_map/attention/pallas_call | solution.py:121
  117.8 6.4 %mix.1 = (f32[512,768]{1,0:T(8,128)}, bf16[512,768]{1,0:T(8,128)(2,1)}, bf16[8,128,768]{2,1,0:T(8,128)(2,1)}, bf16[8,128,768]{2,1,0:T(8,128)(2,1)}) custom-call(s32[2,512]{1,0:T(2,128)} %copy.87.ids_ref, bf16[512,768]{1,0:T(8,128)(2,1)} %tokens_ref.1, bf16[512,768]{1,0:T(8,128)(2,1)} %get-tuple-element.58.attended_ref, ...), custom_call_target="tpu_custom_call" | custom-call | flops 1000 | bytes 1000 | tf_op jit(solution)/shard_map/mix/pallas_call | solution.py:336
  124.2 3.6 all-to-all-start.1
  127.8 1.3 fusion.76.pick_ref
  129.7 2.0 collective-permute-start.12
  131.7 24.0 %collective-permute-done.12 = s32[2,512,2]{1,2,0:T(2,128)S(1)} collective-permute-done((s32[2,512,2]{1,2,0:T(2,128)S(1)}, s32[2,512,2]{1,2,0:T(2,128)S(1)}, u32[]{:S(2)}, u32[]{:S(2)}) %collective-permute-start.12) | collective-permute-done | bytes 8224 | tf_op jit(solution)/shard_map/ppermute | solution.py:654
  155.7 3.4 collective-permute-start.13
  159.1 7.4 %collective-permute-done.13 = s32[4,512,2]{1,2,0:T(2,128)S(1)} collective-permute-done((s32[4,512,2]{1,2,0:T(2,128)S(1)}, s32[4,512,2]{1,2,0:T(2,128)S(1)}, u32[]{:S(2)}, u32[]{:S(2)}) %collective-permute-start.13) | collective-permute-done | bytes 16416 | tf_op jit(solution)/shard_map/ppermute | solution.py:654
  171.3 4.7 %all-to-all-start.3 = ((bf16[8,128,768]{2,1,0:T(8,128)(2,1)}), bf16[8,128,768]{2,1,0:T(8,128)(2,1)}, u32[]{:S(2)}, u32[]{:S(2)}) async-start(bf16[8,128,768]{2,1,0:T(8,128)(2,1)} %get-tuple-element.66), calls=%async_computation.3 | async-start | bytes 3145728 | tf_op jit(solution)/shard_map/all_to_all | solution.py:662
  176.0 1.6 constant_dynamic-update-slice_fusion.3
  177.7 1.6 constant_dynamic-update-slice_fusion.2
  179.3 1.6 constant_dynamic-update-slice_fusion.1
  181.0 2.1 constant_dynamic-update-slice_fusion
  184.0 2.8 all-gather.8.cloned.1.call-done
  186.8 29.9 %expert_rows.2 = (bf16[8,128,768]{2,1,0:T(8,128)(2,1)}, bf16[8,256,768]{2,1,0:T(8,128)(2,1)}, bf16[2048,768]{1,0:T(8,128)(2,1)}, bf16[2048,768]{1,0:T(8,128)(2,1...) custom-call(s32[1]{0:T(128)} %bitcast.11.place_ref, ...), custom_call_target="tpu_custom_call" | custom-call | flops 19327352832 | bytes 34603008 | tf_op jit(solution)/shard_map/expert_rows/pallas_call | solution.py:453
  216.7 5.8 %all-to-all-start.2 = ((bf16[8,128,768]{2,1,0:T(8,128)(2,1)}), bf16[8,128,768]{2,1,0:T(8,128)(2,1)S(1)}, u32[]{:S(2)}, u32[]{:S(2)}) async-start(bf16[8,128,768]{2,1,0:T(8,128)(2,1)} %get-tuple-element.64), calls=%async_computation.2 | async-start | bytes 3145728 | tf_op jit(solution)/shard_map/all_to_all | solution.py:662
  222.5 4.5 %convolution_convert_fusion.3 = bf16[768,1152]{1,0:T(8,128)(2,1)} fusion(bf16[768,1152]{1,0:T(8,128)(2,1)} %constant_dynamic-update-slice_fusion, pred[384,768]{1,0:T(32,128)(4,1)S(1)} %iota_compare_fusion.1, pred[384,768]{1,0:T(32,128)(4,1)S(1)} %iota_compare_fusion.2), kind=kOutput, calls=%fused_computation.11 | convolution fusion | flops 1360429056 | bytes 4128768 | tf_op jit(solution)/shard_map/dot_general | solution.py:41
  227.0 3.0 convolution_convert_fusion.2
  230.0 1.7 convolution_convert_fusion.5.attended_ref
  231.7 1.7 convolution_convert_fusion.4.normed_rel_ref
  233.5 30.1 %expert_rows.3 = (bf16[8,144,768]{2,1,0:T(8,128)(2,1)}, bf16[8,256,768]{2,1,0:T(8,128)(2,1)}, bf16[2048,768]{1,0:T(8,128)(2,1)}, bf16[2048,768]{1,0:T(8,128)(2,1...) custom-call(s32[1]{0:T(128)} %bitcast.11.place_ref, ...), custom_call_target="tpu_custom_call", output_to_operand_aliasing={{1}: (8, {}), {2}: (9, {}), {3}: (10, {}), {4}: (11, {}), {... | custom-call | flops 19327352832 | bytes 34603008 | tf_op jit(solution)/shard_map/expert_rows/pallas_call | solution.py:453
  264.7 6.4 %all-to-all-start.4 = ((bf16[8,144,768]{2,1,0:T(8,128)(2,1)}), bf16[8,144,768]{2,1,0:T(8,128)(2,1)S(1)}, u32[]{:S(2)}, u32[]{:S(2)}) async-start(bf16[8,144,768]{2,1,0:T(8,128)(2,1)} %get-tuple-element.74), calls=%async_computation.4 | async-start | bytes 3538944 | tf_op jit(solution)/shard_map/all_to_all | solution.py:662
  271.2 5.7 %fusion.23 = bf16[768,768]{1,0:T(8,128)(2,1)S(1)} fusion(bf16[2048,768]{1,0:T(8,128)(2,1)} %get-tuple-element.101, bf16[2048,3072]{1,0:T(8,128)(2,1)} %get-tuple-element.100, s32[]{:T(128)S(6)} %select_n.130), kind=kOutput, calls=%fused_computation.41 | convolution fusion | flops 2416508928 | bytes 7471108 | tf_op jit(solution)/shard_map/dot_general | solution.py:41
  276.9 4.7 %fusion.20 = bf16[768,768]{1,0:T(8,128)(2,1)S(1)} fusion(bf16[2048,768]{1,0:T(8,128)(2,1)S(1)} %copy-done.30, bf16[2048,3072]{1,0:T(8,128)(2,1)} %get-tuple-element.100, s32[]{:T(128)S(6)} %select_n.128), kind=kOutput, calls=%fused_computation.40 | convolution fusion | flops 2416508928 | bytes 7471108 | tf_op jit(solution)/shard_map/dot_general | solution.py:41
  282.2 2.8 convolution_convert_fusion
  285.1 2.7 convolution_convert_fusion.1
  288.4 5.8 %add_convert_fusion = bf16[768,768]{1,0:T(8,128)(2,1)} fusion(bf16[768,768]{1,0:T(8,128)(2,1)S(1)} %collective-permute-done.32, bf16[2048,768]{1,0:T(8,128)(2,1)S(1)} %copy-done.30, bf16[2048,3072]{1,0:T(8,128)(2,1)} %get-tuple-element.100, s32[]{:T(128)S(6)} %select_n.129), kind=kOutput, calls=%fused_computation.26 | convolution fusion | flops 2417688576 | bytes 8650756 | tf_op jit(solution)/shard_map/dot_general | solution.py:41
  294.7 3.8 add_convert_fusion.1
  298.6 1.4 collective-permute-start.30
  300.0 6.0 %convert_add_fusion.1 = f32[768,768]{1,0:T(8,128)} fusion(bf16[768,768]{1,0:T(8,128)(2,1)S(1)} %collective-permute-done.31, bf16[2048,768]{1,0:T(8,128)(2,1)S(1)} %copy-done.30, bf16[2048,3072]{1,0:T(8,128)(2,1)} %get-tuple-element.100, s32[]{:T(128)S(6)} %select_n.127), kind=kOutput, calls=%fused_computation.27 | convolution fusion | flops 2417098752 | bytes 9830404 | tf_op jit(solution)/shard_map/dot_general | solution.py:41
  306.0 4.2 convert_add_fusion.2
  310.2 1.6 all-to-all-done.4.refs_1_
  313.0 4.6 %all-to-all-start.5 = ((bf16[8,256,768]{2,1,0:T(8,128)(2,1)}), bf16[8,256,768]{2,1,0:T(8,128)(2,1)S(1)}, u32[]{:S(2)}, u32[]{:S(2)}) async-start(bf16[8,256,768]{2,1,0:T(8,128)(2,1)} %get-tuple-element.77), calls=%async_computation.5 | async-start | bytes 6291456 | tf_op jit(solution)/shard_map/all_to_all | solution.py:662
  317.6 11.0 %collect.1 = (f32[512,768]{1,0:T(8,128)}, bf16[512,768]{1,0:T(8,128)(2,1)}, f32[512,2]{1,0:T(8,128)}, f32[384,896]{1,0:T(8,128)}, bf16[384,896]{1,0:T(8,128)(2,1)}) custom-call(s32[512,2]{1,0:T(8,128)} %copy-done.11, s32[512,2]{1,0:T(8,128)} %copy-done.12, s32[2,1024]{1,0:T(2,128)} %bitcast_add_fusion.places_ref, ...), custom_call_target="tpu_custom_call" | custom-call | flops 1000 | bytes 1000 | tf_op jit(solution)/shard_map/collect/pallas_call | solution.py:592
  328.6 29.0 %attention_pull.1 = (bf16[512,2304]{1,0:T(8,128)(2,1)}, f32[12,512]{1,0:T(8,128)}, f32[384,3200]{1,0:T(8,128)}, bf16[384,3200]{1,0:T(8,128)(2,1)}) custom-call(f32[12,512]{1,0:T(8,128)} %convolution_bitcast_fusion.base_ref, s32[512,1]{1,0:T(8,128)} %copy.86.starts_ref, bf16[512,2304]{1,0:T(8,128)(2,1)} %get-tuple-element.57.packed_ref, ...), custom_call_target="tpu_custom_call" | custom-call | flops 1000 | bytes 1000 | tf_op jit(solution)/shard_map/attention_pull/pallas_call | solution.py:220
  358.8 5.3 %fusion.19 = (f32[768]{0:T(1024)S(1)}, f32[512]{0:T(512)S(1)}, f32[512,768]{1,0:T(8,128)S(1)}) fusion(bf16[512,768]{1,0:T(8,128)(2,1)} %tokens_ref.1, f32[512]{0:T(512)S(1)} %fusion.70, f32[768]{0:T(1024)S(1)} %get-tuple-element.157, bf16[512,2304]{1,0:T(8,128)(2,1)} %get-tuple-element.85, bf16[768,1152]{1,0:T(8,128)(2,1)} %convolution_convert_fusion.2, ...), kind=kOutput, calls=%fused_computation.39 | convolution fusion | flops 1821768448 | bytes 8267776 | tf_op jit(solution)/shard_map/dot_general | solution.py:35
  364.7 3.2 add_bitcast_fusion.1
  367.9 2.9 add_bitcast_fusion
  371.6 2.9 collective-permute-done.15
  374.5 2.0 collective-permute-start.16
  376.5 2.3 fusion.77
  380.5 1.6 fusion.15
  382.4 10.8 %collective-permute-done.24 = bf16[192,1536]{1,0:T(8,128)(2,1)S(1)} collective-permute-done((bf16[192,1536]{1,0:T(8,128)(2,1)S(1)}, bf16[192,1536]{1,0:T(8,128)(2,1)S(1)}, u32[]{:S(2)}, u32[]{:S(2)}) %collective-permute-start.24) | collective-permute-done | bytes 589856 | tf_op jit(solution)/shard_map/ppermute | solution.py:654
  394.5 5.1 %collective-permute-done.20 = bf16[192,1664]{1,0:T(8,128)(2,1)S(1)} collective-permute-done((bf16[192,1664]{1,0:T(8,128)(2,1)S(1)}, bf16[192,1664]{1,0:T(8,128)(2,1)S(1)}, u32[]{:S(2)}, u32[]{:S(2)}) %collective-permute-start.20) | collective-permute-done | bytes 639008 | tf_op jit(solution)/shard_map/ppermute | solution.py:654
  401.6 1.5 collective-permute-start.17
  405.8 2.1 collective-permute-start.26
  409.7 2.1 collective-permute-start.22
  411.8 6.9 %finish.1 = bf16[512,768]{1,0:T(8,128)(2,1)} custom-call(s32[512,2]{1,0:T(8,128)} %copy-done.11, f32[512,2]{1,0:T(8,128)} %get-tuple-element.75.gates_ref, f32[512,768]{1,0:T(8,128)} %get-tuple-element.60.mixed_ref, bf16[8,256,768]{2,1,0:T(8,128)(2,1)} %copy-done.2), custom_call_target="tpu_custom_call" | custom-call | flops 1000 | bytes 1000 | tf_op jit(solution)/shard_map/finish/pallas_call | solution.py:636
  421.3 1.6 collective-permute-start.27
  (239 shorter events, 48.0 us)
Async XLA Ops:
  7.2 30.0 %copy-start = (f32[12,32]{1,0:T(8,128)S(1)}, f32[12,32]{1,0:T(8,128)}, u32[]{:S(2)}) copy-start(f32[12,32]{1,0:T(8,128)} %param.21) | copy-start | bytes 4612
  7.2 14.3 %copy-start.27 = (s32[512,2]{0,1:T(2,128)S(1)}, s32[512,2]{0,1:T(2,128)}, u32[]{:S(2)}) copy-start(s32[512,2]{0,1:T(2,128)} %param.24) | copy-start | bytes 12292
  7.2 110.6 %all-gather.4.cloned.1.call-start = ((), (), s32[]{:S(2)}) async-start(), calls=%async_computation.6 | async-start | bytes 1216512 | tf_op jit(solution)/shard_map/all_gather | solution.py:811
  7.9 176.1 %all-gather.6.cloned.1.call-start = ((), (), s32[]{:S(2)}) async-start(), calls=%async_computation.7 | async-start | bytes 5898240 | tf_op jit(solution)/shard_map/all_gather | solution.py:843
  11.9 15.5 %collective-permute-start.2 = (bf16[24,2432]{1,0:T(8,128)(2,1)S(1)}, bf16[24,2432]{1,0:T(8,128)(2,1)S(1)}, u32[]{:S(2)}, u32[]{:S(2)}) collective-permute-start(bf16[24,2432]{1,0:T(8,128)(2,1)S(1)} %concatenate.56), channel_id=1, source_target_pairs={{0,24},{4,28},{8,16},{12,20},{16,8},{20,12},{24,0},{28,4},{1,25},{... | collective-permute-start | bytes 350216 | tf_op jit(solution)/shard_map/ppermute | solution.py:654
  17.1 10.4 %collective-permute-start.1 = (bf16[24,2432]{1,0:T(8,128)(2,1)S(1)}, bf16[24,2432]{1,0:T(8,128)(2,1)S(1)}, u32[]{:S(2)}, u32[]{:S(2)}) collective-permute-start(bf16[24,2432]{1,0:T(8,128)(2,1)S(1)} %concatenate.56), channel_id=1, source_target_pairs={{0,16},{4,20},{8,24},{12,28},{16,0},{20,4},{24,8},{28,12},{1,17},{... | collective-permute-start | bytes 350216 | tf_op jit(solution)/shard_map/ppermute | solution.py:654
  17.1 10.4 %collective-permute-start = (bf16[24,2432]{1,0:T(8,128)(2,1)S(1)}, bf16[24,2432]{1,0:T(8,128)(2,1)S(1)}, u32[]{:S(2)}, u32[]{:S(2)}) collective-permute-start(bf16[24,2432]{1,0:T(8,128)(2,1)S(1)} %concatenate.56), channel_id=1, source_target_pairs={{0,8},{4,12},{8,0},{12,4},{16,24},{20,28},{24,16},{28,20},{1,9},{5... | collective-permute-start | bytes 350216 | tf_op jit(solution)/shard_map/ppermute | solution.py:654
  18.5 8.9 %copy-start.12 = (s32[512,2]{1,0:T(8,128)}, s32[512,2]{1,0:T(8,128)S(1)}, u32[]{:S(2)}) copy-start(s32[512,2]{1,0:T(8,128)S(1)} %copy.79.experts_ref) | copy-start | bytes 12292
  27.5 8.8 %copy-start.28 = (s32[384]{0:T(512)S(1)}, s32[384]{0:T(512)}, u32[]{:S(2)}) copy-start(s32[384]{0:T(512)} %param.23) | copy-start | bytes 4612
  27.5 9.0 %copy-start.7 = (bf16[512,768]{1,0:T(8,128)(2,1)S(1)}, bf16[512,768]{1,0:T(8,128)(2,1)}, u32[]{:S(2)}) copy-start(bf16[512,768]{1,0:T(8,128)(2,1)} %tokens_ref.1) | copy-start | bytes 2359300
  27.5 96.7 %all-to-all-start = ((bf16[8,256,768]{2,1,0:T(8,128)(2,1)}), bf16[8,256,768]{2,1,0:T(8,128)(2,1)}, u32[]{:S(2)}, u32[]{:S(2)}) async-start(bf16[8,256,768]{2,1,0:T(8,128)(2,1)} %spread.1), calls=%async_computation | async-start | bytes 6291456 | tf_op jit(solution)/shard_map/all_to_all | solution.py:662
  33.6 153.2 %all-gather.8.cloned.1.call-start = ((), (), s32[]{:S(2)}) async-start(), calls=%async_computation.8 | async-start | bytes 5898240 | tf_op jit(solution)/shard_map/all_gather | solution.py:844
  34.2 95.5 %collective-permute-start.11 = (s32[1,512,2]{1,2,0:T(2,128)S(1)}, s32[1,512,2]{1,2,0:T(2,128)S(1)}, u32[]{:S(2)}, u32[]{:S(2)}) collective-permute-start(s32[1,512,2]{1,2,0:T(2,128)S(1)} %bitcast.76), channel_id=1, source_target_pairs={{0,4},{4,0},{8,12},{12,8},{16,20},{20,16},{24,28},{28,24},{1,5},{5... | collective-permute-start | bytes 12296 | tf_op jit(solution)/shard_map/ppermute | solution.py:654
  36.8 29.5 %collective-permute-start.8 = (bf16[96,1280]{1,0:T(8,128)(2,1)S(1)}, bf16[96,1280]{1,0:T(8,128)(2,1)S(1)}, u32[]{:S(2)}, u32[]{:S(2)}) collective-permute-start(bf16[96,1280]{1,0:T(8,128)(2,1)S(1)} %slice.196), channel_id=1, source_target_pairs={{0,4},{4,0},{8,12},{12,8},{16,20},{20,16},{24,28},{28,24},{1,5},{5... | collective-permute-start | bytes 737288 | tf_op jit(solution)/shard_map/ppermute | solution.py:654
  38.1 41.9 %collective-permute-start.7 = (bf16[96,1280]{1,0:T(8,128)(2,1)S(1)}, bf16[96,1280]{1,0:T(8,128)(2,1)S(1)}, u32[]{:S(2)}, u32[]{:S(2)}) collective-permute-start(bf16[96,1280]{1,0:T(8,128)(2,1)S(1)} %slice.196), channel_id=1, source_target_pairs={{0,2},{1,3},{2,0},{3,1},{4,6},{5,7},{6,4},{7,5},{8,10},{9,11},{10,... | collective-permute-start | bytes 737288 | tf_op jit(solution)/shard_map/ppermute | solution.py:654
  66.3 13.7 %collective-permute-start.9 = (bf16[96,1280]{1,0:T(8,128)(2,1)S(1)}, bf16[96,1280]{1,0:T(8,128)(2,1)S(1)}, u32[]{:S(2)}, u32[]{:S(2)}) collective-permute-start(bf16[96,1280]{1,0:T(8,128)(2,1)S(1)} %collective-permute-done.8), channel_id=1, source_target_pairs={{0,2},{1,3},{2,0},{3,1},{4,6},{5,7},{6,4},{7,5},{8,10},{9,11},{10,... | collective-permute-start | bytes 737288 | tf_op jit(solution)/shard_map/ppermute | solution.py:654
  68.5 8.8 %collective-permute-start.3 = (bf16[96,1152]{1,0:T(8,128)(2,1)S(1)}, bf16[96,1152]{1,0:T(8,128)(2,1)S(1)}, u32[]{:S(2)}, u32[]{:S(2)}) collective-permute-start(bf16[96,1152]{1,0:T(8,128)(2,1)S(1)} %get-tuple-element.156), channel_id=1, source_target_pairs={{0,2},{1,3},{2,0},{3,1},{4,6},{5,7},{6,4},{7,5},{8,10},{9,11},{10,... | collective-permute-start | bytes 663560 | tf_op jit(solution)/shard_map/ppermute | solution.py:654
  69.0 18.1 %collective-permute-start.4 = (bf16[96,1152]{1,0:T(8,128)(2,1)S(1)}, bf16[96,1152]{1,0:T(8,128)(2,1)S(1)}, u32[]{:S(2)}, u32[]{:S(2)}) collective-permute-start(bf16[96,1152]{1,0:T(8,128)(2,1)S(1)} %get-tuple-element.156), channel_id=1, source_target_pairs={{0,4},{4,0},{8,12},{12,8},{16,20},{20,16},{24,28},{28,24},{1,5},{5... | collective-permute-start | bytes 663560 | tf_op jit(solution)/shard_map/ppermute | solution.py:654
  77.3 14.1 %copy-start.22 = (bf16[96,1152]{1,0:T(8,128)(2,1)}, bf16[96,1152]{1,0:T(8,128)(2,1)S(1)}, u32[]{:S(2)}) copy-start(bf16[96,1152]{1,0:T(8,128)(2,1)S(1)} %collective-permute-done.3) | copy-start | bytes 663556
  77.3 14.1 %collective-permute-start.5 = (bf16[96,1152]{1,0:T(8,128)(2,1)S(1)}, bf16[96,1152]{1,0:T(8,128)(2,1)S(1)}, u32[]{:S(2)}, u32[]{:S(2)}) collective-permute-start(bf16[96,1152]{1,0:T(8,128)(2,1)S(1)} %collective-permute-done.3), channel_id=1, source_target_pairs={{0,4},{4,0},{8,12},{12,8},{16,20},{20,16},{24,28},{28,24},{1,5},{5... | collective-permute-start | bytes 663560 | tf_op jit(solution)/shard_map/ppermute | solution.py:654
  80.1 15.4 %copy-start.4 = (bf16[384,1280]{1,0:T(8,128)(2,1)}, bf16[384,1280]{1,0:T(8,128)(2,1)S(1)}, u32[]{:S(2)}) copy-start(bf16[384,1280]{1,0:T(8,128)(2,1)S(1)} %pad_maximum_fusion.refs_2_) | copy-start | bytes 2949124
  80.1 15.4 %collective-permute-start.10 = (bf16[384,1280]{1,0:T(8,128)(2,1)S(1)}, bf16[384,1280]{1,0:T(8,128)(2,1)S(1)}, u32[]{:S(2)}, u32[]{:S(2)}) collective-permute-start(bf16[384,1280]{1,0:T(8,128)(2,1)S(1)} %pad_maximum_fusion.refs_2_), channel_id=1, source_target_pairs={{0,1},{1,0},{2,3},{3,2},{4,5},{5,4},{6,7},{7,6},{8,9},{9,8},{10,11... | collective-permute-start | bytes 2949128 | tf_op jit(solution)/shard_map/ppermute | solution.py:654
  92.3 3.2 collective-permute-start.6
  102.6 14.2 %slice-start.5 = ((bf16[384,1280]{1,0:T(8,128)(2,1)}), bf16[384,128]{1,0:T(8,128)(2,1)S(1)}, s32[]{:S(2)}) async-start(bf16[384,1280]{1,0:T(8,128)(2,1)} %copy-done.13), calls=%async_computation.14 | async-start | bytes 196608 | tf_op jit(solution)/shard_map/slice | solution.py:851
  124.2 47.1 %all-to-all-start.1 = ((bf16[8,128,768]{2,1,0:T(8,128)(2,1)}), bf16[8,128,768]{2,1,0:T(8,128)(2,1)S(1)}, u32[]{:S(2)}, u32[]{:S(2)}) async-start(bf16[8,128,768]{2,1,0:T(8,128)(2,1)} %get-tuple-element.63), calls=%async_computation.1 | async-start | bytes 3145728 | tf_op jit(solution)/shard_map/all_to_all | solution.py:662
  129.7 26.0 %collective-permute-start.12 = (s32[2,512,2]{1,2,0:T(2,128)S(1)}, s32[2,512,2]{1,2,0:T(2,128)S(1)}, u32[]{:S(2)}, u32[]{:S(2)}) collective-permute-start(s32[2,512,2]{1,2,0:T(2,128)S(1)} %pad_add_fusion.3), channel_id=1, source_target_pairs={{0,8},{4,12},{8,0},{12,4},{16,24},{20,28},{24,16},{28,20},{1,9},{5... | collective-permute-start | bytes 24584 | tf_op jit(solution)/shard_map/ppermute | solution.py:654
  155.7 10.8 %collective-permute-start.13 = (s32[4,512,2]{1,2,0:T(2,128)S(1)}, s32[4,512,2]{1,2,0:T(2,128)S(1)}, u32[]{:S(2)}, u32[]{:S(2)}) collective-permute-start(s32[4,512,2]{1,2,0:T(2,128)S(1)} %pad_add_fusion.2), channel_id=1, source_target_pairs={{0,16},{4,20},{8,24},{12,28},{16,0},{20,4},{24,8},{28,12},{1,17},{... | collective-permute-start | bytes 49160 | tf_op jit(solution)/shard_map/ppermute | solution.py:654
  171.3 8.0 %copy-start.20 = (bf16[8,128,768]{2,1,0:T(8,128)(2,1)}, bf16[8,128,768]{2,1,0:T(8,128)(2,1)S(1)}, u32[]{:S(2)}) copy-start(bf16[8,128,768]{2,1,0:T(8,128)(2,1)S(1)} %all-to-all-done.1.rows_ref) | copy-start | bytes 4718596
  171.3 9.7 %copy-start.5 = (bf16[384,1280]{1,0:T(8,128)(2,1)S(1)}, bf16[384,1280]{1,0:T(8,128)(2,1)}, u32[]{:S(2)}) copy-start(bf16[384,1280]{1,0:T(8,128)(2,1)} %copy-done.4) | copy-start | bytes 2949124
  171.3 45.4 %all-to-all-start.3 = ((bf16[8,128,768]{2,1,0:T(8,128)(2,1)}), bf16[8,128,768]{2,1,0:T(8,128)(2,1)}, u32[]{:S(2)}, u32[]{:S(2)}) async-start(bf16[8,128,768]{2,1,0:T(8,128)(2,1)} %get-tuple-element.66), calls=%async_computation.3 | async-start | bytes 3145728 | tf_op jit(solution)/shard_map/all_to_all | solution.py:662
  216.7 46.9 %all-to-all-start.2 = ((bf16[8,128,768]{2,1,0:T(8,128)(2,1)}), bf16[8,128,768]{2,1,0:T(8,128)(2,1)S(1)}, u32[]{:S(2)}, u32[]{:S(2)}) async-start(bf16[8,128,768]{2,1,0:T(8,128)(2,1)} %get-tuple-element.64), calls=%async_computation.2 | async-start | bytes 3145728 | tf_op jit(solution)/shard_map/all_to_all | solution.py:662
  264.7 47.1 %all-to-all-start.4 = ((bf16[8,144,768]{2,1,0:T(8,128)(2,1)}), bf16[8,144,768]{2,1,0:T(8,128)(2,1)S(1)}, u32[]{:S(2)}, u32[]{:S(2)}) async-start(bf16[8,144,768]{2,1,0:T(8,128)(2,1)} %get-tuple-element.74), calls=%async_computation.4 | async-start | bytes 3538944 | tf_op jit(solution)/shard_map/all_to_all | solution.py:662
  271.1 5.7 %copy-start.30 = (bf16[2048,768]{1,0:T(8,128)(2,1)S(1)}, bf16[2048,768]{1,0:T(8,128)(2,1)}, u32[]{:S(2)}) copy-start(bf16[2048,768]{1,0:T(8,128)(2,1)} %get-tuple-element.101) | copy-start | bytes 9437188
  271.1 11.0 %slice-start = ((s8[12582912]{0:T(1024)(128)(4,1)}), s8[4194304]{0:T(1024)(128)(4,1)S(1)}, s32[]{:S(2)}) async-start(s8[12582912]{0:T(1024)(128)(4,1)} %bitcast.71), calls=%async_computation.9 | async-start | bytes 8388608
  271.2 11.0 %slice-start.1 = ((s8[12582912]{0:T(1024)(128)(4,1)}), s8[4194304]{0:T(1024)(128)(4,1)S(1)}, s32[]{:S(2)}) async-start(s8[12582912]{0:T(1024)(128)(4,1)} %bitcast.71), calls=%async_computation.10 | async-start | bytes 8388608
  276.9 5.3 %slice-start.2 = ((s8[12582912]{0:T(1024)(128)(4,1)}), s8[4194304]{0:T(1024)(128)(4,1)S(1)}, s32[]{:S(2)}) async-start(s8[12582912]{0:T(1024)(128)(4,1)} %bitcast.71), calls=%async_computation.11 | async-start | bytes 8388608
  276.9 5.3 %copy-start.10 = (bf16[2048,768]{1,0:T(8,128)(2,1)S(1)}, bf16[2048,768]{1,0:T(8,128)(2,1)}, u32[]{:S(2)}) copy-start(bf16[2048,768]{1,0:T(8,128)(2,1)} %get-tuple-element.96) | copy-start | bytes 9437188
  281.6 18.4 %collective-permute-start.31 = (bf16[768,768]{1,0:T(8,128)(2,1)S(1)}, bf16[768,768]{1,0:T(8,128)(2,1)S(1)}, u32[]{:S(2)}, u32[]{:S(2)}) collective-permute-start(bf16[768,768]{1,0:T(8,128)(2,1)S(1)} %fusion.20), channel_id=1, source_target_pairs={{0,1},{1,0},{2,3},{3,2},{4,5},{5,4},{6,7},{7,6},{8,9},{9,8},{10,11... | collective-permute-start | bytes 3538952 | tf_op jit(solution)/shard_map/ppermute | solution.py:654
  281.7 6.7 %collective-permute-start.32 = (bf16[768,768]{1,0:T(8,128)(2,1)S(1)}, bf16[768,768]{1,0:T(8,128)(2,1)S(1)}, u32[]{:S(2)}, u32[]{:S(2)}) collective-permute-start(bf16[768,768]{1,0:T(8,128)(2,1)S(1)} %fusion.23), channel_id=1, source_target_pairs={{0,1},{1,0},{2,3},{3,2},{4,5},{5,4},{6,7},{7,6},{8,9},{9,8},{10,11... | collective-permute-start | bytes 3538952 | tf_op jit(solution)/shard_map/ppermute | solution.py:654
  285.0 9.7 %collective-permute-start.29 = (bf16[192,3072]{1,0:T(8,128)(2,1)S(1)}, bf16[192,3072]{1,0:T(8,128)(2,1)S(1)}, u32[]{:S(2)}, u32[]{:S(2)}) collective-permute-start(bf16[192,3072]{1,0:T(8,128)(2,1)S(1)} %convolution_convert_fusion), channel_id=1, source_target_pairs={{0,1},{1,0},{2,3},{3,2},{4,5},{5,4},{6,7},{7,6},{8,9},{9,8},{10,11... | collective-permute-start | bytes 3538952 | tf_op jit(solution)/shard_map/ppermute | solution.py:654
  287.9 18.1 %collective-permute-start.28 = (bf16[192,3072]{1,0:T(8,128)(2,1)S(1)}, bf16[192,3072]{1,0:T(8,128)(2,1)S(1)}, u32[]{:S(2)}, u32[]{:S(2)}) collective-permute-start(bf16[192,3072]{1,0:T(8,128)(2,1)S(1)} %convolution_convert_fusion.1), channel_id=1, source_target_pairs={{0,1},{1,0},{2,3},{3,2},{4,5},{5,4},{6,7},{7,6},{8,9},{9,8},{10,11... | collective-permute-start | bytes 3538952 | tf_op jit(solution)/shard_map/ppermute | solution.py:654
  294.2 64.6 %collective-permute-start.33 = (bf16[768,768]{1,0:T(8,128)(2,1)}, bf16[768,768]{1,0:T(8,128)(2,1)}, u32[]{:S(2)}, u32[]{:S(2)}) collective-permute-start(bf16[768,768]{1,0:T(8,128)(2,1)} %add_convert_fusion), channel_id=1, source_target_pairs={{0,2},{1,3},{2,0},{3,1},{4,6},{5,7},{6,4},{7,5},{8,10},{9,11},{10,... | collective-permute-start | bytes 3538952 | tf_op jit(solution)/shard_map/ppermute | solution.py:654
  298.6 60.2 %collective-permute-start.30 = (bf16[192,3072]{1,0:T(8,128)(2,1)}, bf16[192,3072]{1,0:T(8,128)(2,1)}, u32[]{:S(2)}, u32[]{:S(2)}) collective-permute-start(bf16[192,3072]{1,0:T(8,128)(2,1)} %add_convert_fusion.1), channel_id=1, source_target_pairs={{0,2},{1,3},{2,0},{3,1},{4,6},{5,7},{6,4},{7,5},{8,10},{9,11},{10,... | collective-permute-start | bytes 3538952 | tf_op jit(solution)/shard_map/ppermute | solution.py:654
  313.0 88.6 %all-to-all-start.5 = ((bf16[8,256,768]{2,1,0:T(8,128)(2,1)}), bf16[8,256,768]{2,1,0:T(8,128)(2,1)S(1)}, u32[]{:S(2)}, u32[]{:S(2)}) async-start(bf16[8,256,768]{2,1,0:T(8,128)(2,1)} %get-tuple-element.77), calls=%async_computation.5 | async-start | bytes 6291456 | tf_op jit(solution)/shard_map/all_to_all | solution.py:662
  357.6 18.9 %collective-permute-start.19 = (bf16[384,3200]{1,0:T(8,128)(2,1)}, bf16[384,3200]{1,0:T(8,128)(2,1)}, u32[]{:S(2)}, u32[]{:S(2)}) collective-permute-start(bf16[384,3200]{1,0:T(8,128)(2,1)} %get-tuple-element.89), channel_id=1, source_target_pairs={{0,1},{1,0},{2,3},{3,2},{4,5},{5,4},{6,7},{7,6},{8,9},{9,8},{10,11... | collective-permute-start | bytes 7372808 | tf_op jit(solution)/shard_map/ppermute | solution.py:654
  358.8 17.7 %slice-start.3 = ((s8[4915200]{0:T(1024)(128)(4,1)}), s8[4194304]{0:T(1024)(128)(4,1)S(1)}, s32[]{:S(2)}) async-start(s8[4915200]{0:T(1024)(128)(4,1)} %bitcast.73), calls=%async_computation.12 | async-start | bytes 8388608
  358.8 5.9 %copy-start.3 = (f32[192,3072]{1,0:T(8,128)S(1)}, f32[192,3072]{1,0:T(8,128)}, u32[]{:S(2)}) copy-start(f32[192,3072]{1,0:T(8,128)} %convert_add_fusion.2) | copy-start | bytes 7077892
  358.8 17.7 %slice-start.4 = ((s8[4915200]{0:T(1024)(128)(4,1)}), s8[720896]{0:T(1024)(128)(4,1)S(1)}, s32[]{:S(2)}) async-start(s8[4915200]{0:T(1024)(128)(4,1)} %bitcast.73), calls=%async_computation.13 | async-start | bytes 1441792
  364.1 6.6 %collective-permute-start.14 = (f32[1152]{0:T(1024)S(1)}, f32[1152]{0:T(1024)S(1)}, u32[]{:S(2)}, u32[]{:S(2)}) collective-permute-start(f32[1152]{0:T(1024)S(1)} %pad_maximum_fusion.5), channel_id=1, source_target_pairs={{0,1},{1,0},{2,3},{3,2},{4,5},{5,4},{6,7},{7,6},{8,9},{9,8},{10,11... | collective-permute-start | bytes 13832 | tf_op jit(solution)/shard_map/ppermute | solution.py:654
  370.8 3.7 collective-permute-start.15
  374.5 7.6 %collective-permute-start.16 = (f32[1152]{0:T(1024)S(1)}, f32[1152]{0:T(1024)S(1)}, u32[]{:S(2)}, u32[]{:S(2)}) collective-permute-start(f32[1152]{0:T(1024)S(1)} %add.307), channel_id=1, source_target_pairs={{0,4},{4,0},{8,12},{12,8},{16,20},{20,16},{24,28},{28,24},{1,5},{5... | collective-permute-start | bytes 13832 | tf_op jit(solution)/shard_map/ppermute | solution.py:654
  379.0 14.2 %collective-permute-start.24 = (bf16[192,1536]{1,0:T(8,128)(2,1)S(1)}, bf16[192,1536]{1,0:T(8,128)(2,1)S(1)}, u32[]{:S(2)}, u32[]{:S(2)}) collective-permute-start(bf16[192,1536]{1,0:T(8,128)(2,1)S(1)} %pad_maximum_fusion.2), channel_id=1, source_target_pairs={{0,2},{1,3},{2,0},{3,1},{4,6},{5,7},{6,4},{7,5},{8,10},{9,11},{10,... | collective-permute-start | bytes 1769480 | tf_op jit(solution)/shard_map/ppermute | solution.py:654
  382.2 17.4 %collective-permute-start.20 = (bf16[192,1664]{1,0:T(8,128)(2,1)S(1)}, bf16[192,1664]{1,0:T(8,128)(2,1)S(1)}, u32[]{:S(2)}, u32[]{:S(2)}) collective-permute-start(bf16[192,1664]{1,0:T(8,128)(2,1)S(1)} %slice.211), channel_id=1, source_target_pairs={{0,4},{4,0},{8,12},{12,8},{16,20},{20,16},{24,28},{28,24},{1,5},{5... | collective-permute-start | bytes 1916936 | tf_op jit(solution)/shard_map/ppermute | solution.py:654
  394.1 9.7 %collective-permute-start.25 = (bf16[96,1536]{1,0:T(8,128)(2,1)}, bf16[96,1536]{1,0:T(8,128)(2,1)}, u32[]{:S(2)}, u32[]{:S(2)}) collective-permute-start(bf16[96,1536]{1,0:T(8,128)(2,1)} %slice.252), channel_id=1, source_target_pairs={{0,4},{4,0},{8,12},{12,8},{16,20},{20,16},{24,28},{28,24},{1,5},{5... | collective-permute-start | bytes 884744 | tf_op jit(solution)/shard_map/ppermute | solution.py:654
  400.9 7.9 %collective-permute-start.21 = (bf16[96,1664]{1,0:T(8,128)(2,1)}, bf16[96,1664]{1,0:T(8,128)(2,1)S(1)}, u32[]{:S(2)}, u32[]{:S(2)}) collective-permute-start(bf16[96,1664]{1,0:T(8,128)(2,1)} %slice.251), channel_id=1, source_target_pairs={{0,2},{1,3},{2,0},{3,1},{4,6},{5,7},{6,4},{7,5},{8,10},{9,11},{10,... | collective-permute-start | bytes 958472 | tf_op jit(solution)/shard_map/ppermute | solution.py:654
  401.6 10.2 %copy-start.2 = (bf16[8,256,768]{2,1,0:T(8,128)(2,1)}, bf16[8,256,768]{2,1,0:T(8,128)(2,1)S(1)}, u32[]{:S(2)}) copy-start(bf16[8,256,768]{2,1,0:T(8,128)(2,1)S(1)} %all-to-all-done.5.produced_ref) | copy-start | bytes 9437188
  401.6 7.1 %copy-start.15 = (f32[192,1664]{1,0:T(8,128)S(1)}, f32[192,1664]{1,0:T(8,128)}, u32[]{:S(2)}) copy-start(f32[192,1664]{1,0:T(8,128)} %copy-done.14) | copy-start | bytes 3833860
  401.6 6.3 %collective-permute-start.17 = (f32[1152]{0:T(1024)S(1)}, f32[1152]{0:T(1024)S(1)}, u32[]{:S(2)}, u32[]{:S(2)}) collective-permute-start(f32[1152]{0:T(1024)S(1)} %add.308), channel_id=1, source_target_pairs={{0,8},{4,12},{8,0},{12,4},{16,24},{20,28},{24,16},{28,20},{1,9},{5... | collective-permute-start | bytes 13832 | tf_op jit(solution)/shard_map/ppermute | solution.py:654
  405.8 14.4 %collective-permute-start.26 = (bf16[48,1536]{1,0:T(8,128)(2,1)}, bf16[48,1536]{1,0:T(8,128)(2,1)}, u32[]{:S(2)}, u32[]{:S(2)}) collective-permute-start(bf16[48,1536]{1,0:T(8,128)(2,1)} %slice.254), channel_id=1, source_target_pairs={{0,16},{4,20},{8,24},{12,28},{16,0},{20,4},{24,8},{28,12},{1,17},{... | collective-permute-start | bytes 442376 | tf_op jit(solution)/shard_map/ppermute | solution.py:654
  407.9 11.1 %collective-permute-start.18 = (f32[1152]{0:T(1024)S(1)}, f32[1152]{0:T(1024)S(1)}, u32[]{:S(2)}, u32[]{:S(2)}) collective-permute-start(f32[1152]{0:T(1024)S(1)} %add.309), channel_id=1, source_target_pairs={{0,16},{4,20},{8,24},{12,28},{16,0},{20,4},{24,8},{28,12},{1,17},{... | collective-permute-start | bytes 13832 | tf_op jit(solution)/shard_map/ppermute | solution.py:654
  409.7 13.2 %collective-permute-start.22 = (bf16[48,1664]{1,0:T(8,128)(2,1)S(1)}, bf16[48,1664]{1,0:T(8,128)(2,1)S(1)}, u32[]{:S(2)}, u32[]{:S(2)}) collective-permute-start(bf16[48,1664]{1,0:T(8,128)(2,1)S(1)} %slice.253), channel_id=1, source_target_pairs={{0,16},{4,20},{8,24},{12,28},{16,0},{20,4},{24,8},{28,12},{1,17},{... | collective-permute-start | bytes 479240 | tf_op jit(solution)/shard_map/ppermute | solution.py:654
  411.8 17.3 %copy-start.1 = (f32[12,32]{1,0:T(8,128)S(1)}, f32[12,32]{1,0:T(8,128)}, u32[]{:S(2)}) copy-start(f32[12,32]{1,0:T(8,128)} %param.21) | copy-start | bytes 4612
  421.3 4.4 %collective-permute-start.27 = (bf16[24,1536]{1,0:T(8,128)(2,1)S(1)}, bf16[24,1536]{1,0:T(8,128)(2,1)S(1)}, u32[]{:S(2)}, u32[]{:S(2)}) collective-permute-start(bf16[24,1536]{1,0:T(8,128)(2,1)S(1)} %slice.256), channel_id=1, source_target_pairs={{0,8},{4,12},{8,0},{12,4},{16,24},{20,28},{24,16},{28,20},{1,9},{5... | collective-permute-start | bytes 221192 | tf_op jit(solution)/shard_map/ppermute | solution.py:654
  423.9 4.5 %collective-permute-start.23 = (bf16[24,1664]{1,0:T(8,128)(2,1)S(1)}, bf16[24,1664]{1,0:T(8,128)(2,1)S(1)}, u32[]{:S(2)}, u32[]{:S(2)}) collective-permute-start(bf16[24,1664]{1,0:T(8,128)(2,1)S(1)} %slice.255), channel_id=1, source_target_pairs={{0,8},{4,12},{8,0},{12,4},{16,24},{20,28},{24,16},{28,20},{1,9},{5... | collective-permute-start | bytes 239624 | tf_op jit(solution)/shard_map/ppermute | solution.py:654
  (17 other events, 40.8 us)
Sparse Core Ops, SparseCore 0:
  10.9 99.3 all-gather.3
  111.9 35.7 all-gather.5
  149.3 37.4 all-gather.7

commit v4 on v3

--- a/solution.py
+++ b/solution.py
@@ -714,11 +714,13 @@
         order = lax.axis_index("fsdp") ^ jnp.arange(self.fsdp, dtype=jnp.int32)
         return jnp.take(rows, order, axis=0)
 
-    def scatter(self, keep, send, earlier):
+    def scatter(self, keep, send, earlier, riders):
         if not self.relative:
             whole = jnp.concatenate([keep, send.astype(jnp.float32)])
-            return lax.psum_scatter(whole, ("fsdp", "rep"), scatter_dimension=0, tiled=True)
+            whole = lax.psum_scatter(whole, ("fsdp", "rep"), scatter_dimension=0, tiled=True)
+            return whole, riders, keep
         total = keep + self.hop(send, 1).astype(jnp.float32)
+        total, riders = lax.optimization_barrier((total, riders))
         low = jnp.bfloat16
         cut = -(-total.shape[1] // 256) * 128
         results = []
@@ -730,6 +732,7 @@
                 kept = jnp.concatenate([columns[:quarter], columns[2 * quarter : 3 * quarter]])
                 sent = jnp.concatenate([columns[quarter : 2 * quarter], columns[3 * quarter :]])
             columns = kept + self.hop(sent.astype(low), first).astype(jnp.float32)
+            mark = columns
             for bit in (6 - first, 16, 8):
                 if bit == 16:
                     columns = after(columns, earlier)
@@ -737,7 +740,7 @@
                 got = self.hop(columns[middle:].astype(low), bit)
                 columns = columns[:middle] + got.astype(jnp.float32)
             results.append(columns)
-        return jnp.concatenate(results, axis=1)
+        return jnp.concatenate(results, axis=1), riders, mark
 
     def total(self, values, earlier):
         if not self.relative:
@@ -915,7 +918,9 @@
     d_packed, d_base, *pieces = attention_pull(
         base, starts, packed, d_attended, levels, normed_halves, out_pieces, head_size
     )
-    owned = ring.scatter(*pieces, returned)
+    owned, (owned_in, owned_out), mark = ring.scatter(
+        *pieces, returned, (owned_in, owned_out)
+    )
     weight_qkv = jnp.concatenate(
         [natural(first), natural([half[:, : qkv_width - cut] for half in second])], axis=1
     )
@@ -936,8 +941,8 @@
         owned[:, qkv_width : qkv_width + model_width],
         owned[:, -1],
         owned[:, qkv_width + model_width : qkv_width + model_width + experts],
-        add_late(*owned_in, d_packed)[None],
-        add_late(*owned_out, d_packed)[None],
+        add_late(*owned_in, mark)[None],
+        add_late(*owned_out, mark)[None],
         late[model_width:].reshape(bias_table.shape),
     )
 

time: 440 us -> 486 us (1.10)
  waiting for transfers between devices: 103 us -> 140 us
  matrix products: 56.1 us -> 63.4 us
    ppermute x34, waiting for transfers between devices: 96.7 us -> 116 us  [swap(): lax.ppermute(rows, axis, [(index, index ^ step) for index in range(size)])]
    all_to_all x6, waiting for transfers between devices: 1.64 us -> 20.2 us  [trade(): lax.all_to_all(blocks, 'fsdp', split_axis=0, concat_axis=0, tiled=True)]
    dot_general x11, matrix products: 43.7 us -> 51.5 us  [trans_times(): lax.dot_general(left_side, right_side, (((0,), (0,)), ((), ())), preferre...]
    unnamed x81 -> x87, local copies, waits for them, and re-layouts: 13.4 us -> 14 us
  transfers between devices with their start and end apart: 43 -> 43, of which waited for: 15 -> 15; matrix products, arithmetic and copies ran while one was open for 24% -> 23% of each run, Pallas kernels for 32% -> 29%
where the time goes in v4:
time: 486 us; the launch traced here: 482 us
  waiting for transfers between devices  140 us (29%)
  Pallas kernels  138 us (28%)
  starting transfers between devices  69.9 us (14%)
  matrix products  63.4 us (13%)
  local copies, waits for them, and re-layouts  30.7 us (6%)
  other arithmetic  25.2 us (5%)
  between operations  14.8 us (3%)
    ppermute x34, waiting for transfers between devices, swap(): lax.ppermute(rows, axis, [(index, index ^ step) for index in range(size)])  116 us
    pallas_call x2, Pallas kernels, expert_rows(): pl.pallas_call(functools.partial(expert_kernel, part), grid_spec=pltpu.Pr...  59.8 us
    dot_general x11, matrix products, trans_times(): lax.dot_general(left_side, right_side, (((0,), (0,)), ((), ())), preferre...  51.5 us
    ppermute x34, starting transfers between devices, swap(): lax.ppermute(rows, axis, [(index, index ^ step) for index in range(size)])  38.5 us
    all_to_all x6, starting transfers between devices, trade(): lax.all_to_all(blocks, 'fsdp', split_axis=0, concat_axis=0, tiled=True)  30.8 us
    pallas_call x1, Pallas kernels, attention_pull(): pl.pallas_call(functools.partial(attention_pull_kernel, head_size), out_s...  29.1 us
    all_to_all x6, waiting for transfers between devices, trade(): lax.all_to_all(blocks, 'fsdp', split_axis=0, concat_axis=0, tiled=True)  20.2 us
    pallas_call x1, Pallas kernels, attention(): pl.pallas_call(functools.partial(attention_kernel, head_size), out_shape=...  14.2 us
  transfers between devices with their start and end apart: 43, of which 15 were waited for; matrix products, arithmetic and copies ran while one was open for 23% of the time, Pallas kernels for 29%

profile of v4, /device:TPU:0, one launch (start us, length us, event | category | flops | bytes accessed | tf_op | source)
XLA Modules:
  0.0 482.1 jit_solution(17093495093674867750)
XLA Ops:
  11.9 5.1 %collective-permute-start.2 = (bf16[24,2432]{1,0:T(8,128)(2,1)S(1)}, bf16[24,2432]{1,0:T(8,128)(2,1)S(1)}, u32[]{:S(2)}, u32[]{:S(2)}) collective-permute-start(bf16[24,2432]{1,0:T(8,128)(2,1)S(1)} %concatenate.56), channel_id=1, source_target_pairs={{0,24},{4,28},{8,16},{12,20},{16,8},{20,12},{24,0},{28,4},{1,25},{... | collective-permute-start | bytes 350216 | tf_op jit(solution)/shard_map/ppermute | solution.py:654
  18.7 2.3 reduce-window.21
  22.8 4.7 spread.1
  27.7 6.1 %all-to-all-start = ((bf16[8,256,768]{2,1,0:T(8,128)(2,1)}), bf16[8,256,768]{2,1,0:T(8,128)(2,1)}, u32[]{:S(2)}, u32[]{:S(2)}) async-start(bf16[8,256,768]{2,1,0:T(8,128)(2,1)} %spread.1), calls=%async_computation | async-start | bytes 6291456 | tf_op jit(solution)/shard_map/all_to_all | solution.py:662
  34.3 2.0 collective-permute-start.11
  38.2 1.5 collective-permute-start.7
  39.8 26.7 %collective-permute-done.8 = bf16[96,1280]{1,0:T(8,128)(2,1)S(1)} collective-permute-done((bf16[96,1280]{1,0:T(8,128)(2,1)S(1)}, bf16[96,1280]{1,0:T(8,128)(2,1)S(1)}, u32[]{:S(2)}, u32[]{:S(2)}) %collective-permute-start.8) | collective-permute-done | bytes 245792 | tf_op jit(solution)/shard_map/ppermute | solution.py:654
  66.4 1.5 collective-permute-start.9
  69.2 2.5 collective-permute-start.4
  71.7 5.8 %collective-permute-done.3 = bf16[96,1152]{1,0:T(8,128)(2,1)S(1)} collective-permute-done((bf16[96,1152]{1,0:T(8,128)(2,1)S(1)}, bf16[96,1152]{1,0:T(8,128)(2,1)S(1)}, u32[]{:S(2)}, u32[]{:S(2)}) %collective-permute-start.3) | collective-permute-done | bytes 221216 | tf_op jit(solution)/shard_map/ppermute | solution.py:654
  77.4 2.7 collective-permute-start.5
  80.3 7.0 %collective-permute-done.4 = bf16[96,1152]{1,0:T(8,128)(2,1)S(1)} collective-permute-done((bf16[96,1152]{1,0:T(8,128)(2,1)S(1)}, bf16[96,1152]{1,0:T(8,128)(2,1)S(1)}, u32[]{:S(2)}, u32[]{:S(2)}) %collective-permute-start.4) | collective-permute-done | bytes 221216 | tf_op jit(solution)/shard_map/ppermute | solution.py:654
  87.3 4.2 collective-permute-done.5
  93.9 1.7 fusion.26.tokens_ref
  96.6 6.1 %project.1 = (bf16[512,2304]{1,0:T(8,128)(2,1)}, bf16[512,384]{1,0:T(8,128)(2,1)}, bf16[512,384]{1,0:T(8,128)(2,1)}) custom-call(bf16[512,768]{1,0:T(8,128)(2,1)} %fusion.26.tokens_ref, bf16[384,1152]{1,0:T(8,128)(2,1)} %pad_maximum_fusion.1.refs_0_, bf16[384,1152]{1,0:T(8,128)(2,1)} %collective-permute-done.6.refs_1_, bf16[384,1280]{1,0:T(8,128)(2,1)} %copy-done.4, ...), custom_call_target="tpu_custom_call" | custom-call | flops 1000 | bytes 1000 | tf_op jit(solution)/shard_map/project/pallas_call | solution.py:285
  102.7 14.2 %attention.1 = (bf16[512,768]{1,0:T(8,128)(2,1)}, f32[6,512,2]{2,1,0:T(8,128)}) custom-call(f32[12,512]{1,0:T(8,128)} %convolution_bitcast_fusion.base_ref, s32[512,1]{1,0:T(8,128)} %copy.86.starts_ref, bf16[512,2304]{1,0:T(8,128)(2,1)} %get-tuple-element.62.packed_ref), custom_call_target="tpu_custom_call" | custom-call | flops 1000 | bytes 1000 | tf_op jit(solution)/shard_map/attention/pallas_call | solution.py:121
  118.0 6.4 %mix.1 = (f32[512,768]{1,0:T(8,128)}, bf16[512,768]{1,0:T(8,128)(2,1)}, bf16[8,128,768]{2,1,0:T(8,128)(2,1)}, bf16[8,128,768]{2,1,0:T(8,128)(2,1)}) custom-call(s32[2,512]{1,0:T(2,128)} %copy.87.ids_ref, bf16[512,768]{1,0:T(8,128)(2,1)} %tokens_ref.1, bf16[512,768]{1,0:T(8,128)(2,1)} %get-tuple-element.63.attended_ref, ...), custom_call_target="tpu_custom_call" | custom-call | flops 1000 | bytes 1000 | tf_op jit(solution)/shard_map/mix/pallas_call | solution.py:336
  124.4 3.6 all-to-all-start.1
  129.9 2.0 collective-permute-start.12
  131.9 24.0 %collective-permute-done.12 = s32[2,512,2]{1,2,0:T(2,128)S(1)} collective-permute-done((s32[2,512,2]{1,2,0:T(2,128)S(1)}, s32[2,512,2]{1,2,0:T(2,128)S(1)}, u32[]{:S(2)}, u32[]{:S(2)}) %collective-permute-start.12) | collective-permute-done | bytes 8224 | tf_op jit(solution)/shard_map/ppermute | solution.py:654
  155.9 3.4 collective-permute-start.13
  159.3 7.4 %collective-permute-done.13 = s32[4,512,2]{1,2,0:T(2,128)S(1)} collective-permute-done((s32[4,512,2]{1,2,0:T(2,128)S(1)}, s32[4,512,2]{1,2,0:T(2,128)S(1)}, u32[]{:S(2)}, u32[]{:S(2)}) %collective-permute-start.13) | collective-permute-done | bytes 16416 | tf_op jit(solution)/shard_map/ppermute | solution.py:654
  171.5 4.7 all-to-all-start.3
  176.3 1.6 constant_dynamic-update-slice_fusion.3
  177.9 1.6 constant_dynamic-update-slice_fusion.2
  179.5 1.7 constant_dynamic-update-slice_fusion.1
  181.3 2.1 constant_dynamic-update-slice_fusion
  184.2 2.7 all-gather.8.cloned.1.call-done
  186.9 29.9 %expert_rows.2 = (bf16[8,128,768]{2,1,0:T(8,128)(2,1)}, bf16[8,256,768]{2,1,0:T(8,128)(2,1)}, bf16[2048,768]{1,0:T(8,128)(2,1)}, bf16[2048,768]{1,0:T(8,128)(2,1...) custom-call(s32[1]{0:T(128)} %bitcast.11.place_ref, ...), custom_call_target="tpu_custom_call" | custom-call | flops 19327352832 | bytes 34603008 | tf_op jit(solution)/shard_map/expert_rows/pallas_call | solution.py:453
  216.9 5.8 %all-to-all-start.2 = ((bf16[8,128,768]{2,1,0:T(8,128)(2,1)}), bf16[8,128,768]{2,1,0:T(8,128)(2,1)S(1)}, u32[]{:S(2)}, u32[]{:S(2)}) async-start(bf16[8,128,768]{2,1,0:T(8,128)(2,1)} %get-tuple-element.69), calls=%async_computation.2 | async-start | bytes 3145728 | tf_op jit(solution)/shard_map/all_to_all | solution.py:662
  222.6 4.5 convolution_convert_fusion.3
  227.2 3.0 convolution_convert_fusion.2
  230.2 1.7 convolution_convert_fusion.5.attended_ref
  231.9 1.8 convolution_convert_fusion.4.normed_rel_ref
  233.6 29.9 %expert_rows.3 = (bf16[8,144,768]{2,1,0:T(8,128)(2,1)}, bf16[8,256,768]{2,1,0:T(8,128)(2,1)}, bf16[2048,768]{1,0:T(8,128)(2,1)}, bf16[2048,768]{1,0:T(8,128)(2,1...) custom-call(s32[1]{0:T(128)} %bitcast.11.place_ref, ...), custom_call_target="tpu_custom_call", output_to_operand_aliasing={{1}: (8, {}), {2}: (9, {}), {3}: (10, {}), {4}: (11, {}), {... | custom-call | flops 19327352832 | bytes 34603008 | tf_op jit(solution)/shard_map/expert_rows/pallas_call | solution.py:453
  263.6 6.4 %all-to-all-start.4 = ((bf16[8,144,768]{2,1,0:T(8,128)(2,1)}), bf16[8,144,768]{2,1,0:T(8,128)(2,1)S(1)}, u32[]{:S(2)}, u32[]{:S(2)}) async-start(bf16[8,144,768]{2,1,0:T(8,128)(2,1)} %get-tuple-element.79), calls=%async_computation.4 | async-start | bytes 3538944 | tf_op jit(solution)/shard_map/all_to_all | solution.py:662
  270.0 5.7 %fusion.23 = bf16[768,768]{1,0:T(8,128)(2,1)S(1)} fusion(bf16[2048,768]{1,0:T(8,128)(2,1)} %get-tuple-element.102, bf16[2048,3072]{1,0:T(8,128)(2,1)} %get-tuple-element.101, s32[]{:T(128)S(6)} %select_n.130), kind=kOutput, calls=%fused_computation.41 | convolution fusion | flops 2416508928 | bytes 7471108 | tf_op jit(solution)/shard_map/dot_general | solution.py:41
  275.7 5.7 %fusion.20 = bf16[768,768]{1,0:T(8,128)(2,1)} fusion(bf16[2048,768]{1,0:T(8,128)(2,1)S(1)} %copy-done.34, bf16[2048,3072]{1,0:T(8,128)(2,1)} %get-tuple-element.101, s32[]{:T(128)S(6)} %select_n.128), kind=kOutput, calls=%fused_computation.40 | convolution fusion | flops 2416508928 | bytes 7471108 | tf_op jit(solution)/shard_map/dot_general | solution.py:41
  282.0 2.8 convolution_convert_fusion
  284.9 3.7 convolution_convert_fusion.1
  289.1 5.8 %add_convert_fusion = bf16[768,768]{1,0:T(8,128)(2,1)} fusion(bf16[768,768]{1,0:T(8,128)(2,1)S(1)} %collective-permute-done.24, bf16[2048,768]{1,0:T(8,128)(2,1)S(1)} %copy-done.34, bf16[2048,3072]{1,0:T(8,128)(2,1)} %get-tuple-element.101, s32[]{:T(128)S(6)} %select_n.129), kind=kOutput, calls=%fused_computation.27 | convolution fusion | flops 2417688576 | bytes 8650756 | tf_op jit(solution)/shard_map/dot_general | solution.py:41
  295.5 3.9 add_convert_fusion.1
  299.3 1.4 collective-permute-start.22
  300.7 9.9 %all-to-all-done.4.refs_1_ = bf16[8,144,768]{2,1,0:T(8,128)(2,1)S(1)} async-done(((bf16[8,144,768]{2,1,0:T(8,128)(2,1)}), bf16[8,144,768]{2,1,0:T(8,128)(2,1)S(1)}, u32[]{:S(2)}, u32[]{:S(2)}) %all-to-all-start.4) | async-done | bytes 1769504 | tf_op jit(solution)/shard_map/all_to_all | solution.py:662
  311.9 11.0 %collect.1 = (f32[512,768]{1,0:T(8,128)}, bf16[512,768]{1,0:T(8,128)(2,1)}, f32[512,2]{1,0:T(8,128)}, f32[384,896]{1,0:T(8,128)}, bf16[384,896]{1,0:T(8,128)(2,1)}) custom-call(s32[512,2]{1,0:T(8,128)} %copy-done.12, s32[512,2]{1,0:T(8,128)} %copy-done.13, s32[2,1024]{1,0:T(2,128)} %bitcast_add_fusion.places_ref, ...), custom_call_target="tpu_custom_call" | custom-call | flops 1000 | bytes 1000 | tf_op jit(solution)/shard_map/collect/pallas_call | solution.py:592
  322.8 29.1 %attention_pull.1 = (bf16[512,2304]{1,0:T(8,128)(2,1)}, f32[12,512]{1,0:T(8,128)}, f32[384,3200]{1,0:T(8,128)}, bf16[384,3200]{1,0:T(8,128)(2,1)}) custom-call(f32[12,512]{1,0:T(8,128)} %convolution_bitcast_fusion.base_ref, s32[512,1]{1,0:T(8,128)} %copy.86.starts_ref, bf16[512,2304]{1,0:T(8,128)(2,1)} %get-tuple-element.62.packed_ref, ...), custom_call_target="tpu_custom_call" | custom-call | flops 1000 | bytes 1000 | tf_op jit(solution)/shard_map/attention_pull/pallas_call | solution.py:220
  352.0 9.6 %convert_add_fusion.2 = f32[192,3072]{1,0:T(8,128)} fusion(bf16[192,3072]{1,0:T(8,128)(2,1)} %collective-permute-done.20, bf16[2048,3072]{1,0:T(8,128)(2,1)} %get-tuple-element.100, bf16[2048,768]{1,0:T(8,128)(2,1)} %get-tuple-element.99, s32[]{:T(128)S(6)} %select_n.123), kind=kOutput, calls=%fused_computation.30 | convolution fusion | flops 2417098752 | bytes 17170436 | tf_op jit(solution)/shard_map/dot_general | solution.py:41
  362.0 5.5 %fusion.19 = (f32[768]{0:T(1024)S(1)}, f32[512]{0:T(512)S(1)}, f32[512,768]{1,0:T(8,128)}) fusion(bf16[512,768]{1,0:T(8,128)(2,1)S(1)} %copy-done.8, f32[512]{0:T(512)S(1)} %fusion.70, f32[768]{0:T(1024)S(1)} %get-tuple-element.165, bf16[512,2304]{1,0:T(8,128)(2,1)S(1)} %copy-done.31, bf16[768,1152]{1,0:T(8,128)(2,1)} %convolution_convert_fusion.2, ...), kind=kOutput, calls=%fused_computation.39 | convolution fusion | flops 1821768448 | bytes 8267776 | tf_op jit(solution)/shard_map/dot_general | solution.py:35
  367.9 6.4 %convert_add_fusion.1 = f32[768,768]{1,0:T(8,128)} fusion(bf16[768,768]{1,0:T(8,128)(2,1)} %collective-permute-done.23, bf16[2048,768]{1,0:T(8,128)(2,1)S(1)} %copy-done.35, bf16[2048,3072]{1,0:T(8,128)(2,1)} %get-tuple-element.101, s32[]{:T(128)S(6)} %select_n.127), kind=kOutput, calls=%fused_computation.28 | convolution fusion | flops 2417098752 | bytes 9830404 | tf_op jit(solution)/shard_map/dot_general | solution.py:41
  374.2 4.2 all-to-all-start.5
  379.0 3.2 collective-permute-done.15
  382.2 2.0 collective-permute-start.16
  384.2 3.6 convert_add_fusion
  390.0 1.6 fusion.15
  391.6 12.8 %collective-permute-done.16 = f32[1152]{0:T(1024)S(1)} collective-permute-done((f32[1152]{0:T(1024)S(1)}, f32[1152]{0:T(1024)S(1)}, u32[]{:S(2)}, u32[]{:S(2)}) %collective-permute-start.16) | collective-permute-done | bytes 4640 | tf_op jit(solution)/shard_map/ppermute | solution.py:654
  404.5 2.5 collective-permute-start.26
  409.2 3.0 add_bitcast_fusion
  412.3 2.9 add_bitcast_fusion.1
  415.2 21.8 %collective-permute-done.26 = bf16[192,1664]{1,0:T(8,128)(2,1)S(1)} collective-permute-done((bf16[192,1664]{1,0:T(8,128)(2,1)S(1)}, bf16[192,1664]{1,0:T(8,128)(2,1)S(1)}, u32[]{:S(2)}, u32[]{:S(2)}) %collective-permute-start.26) | collective-permute-done | bytes 639008 | tf_op jit(solution)/shard_map/ppermute | solution.py:654
  439.1 10.3 %all-to-all-done.5.produced_ref = bf16[8,256,768]{2,1,0:T(8,128)(2,1)S(1)} async-done(((bf16[8,256,768]{2,1,0:T(8,128)(2,1)}), bf16[8,256,768]{2,1,0:T(8,128)(2,1)S(1)}, u32[]{:S(2)}, u32[]{:S(2)}) %all-to-all-start.5) | async-done | bytes 3145760 | tf_op jit(solution)/shard_map/all_to_all | solution.py:662
  449.4 2.0 slice_add_fusion.1
  452.1 2.1 collective-permute-start.32
  456.0 2.1 collective-permute-start.28
  458.1 6.9 %finish.1 = bf16[512,768]{1,0:T(8,128)(2,1)} custom-call(s32[512,2]{1,0:T(8,128)} %copy-done.12, f32[512,2]{1,0:T(8,128)} %get-tuple-element.80.gates_ref, f32[512,768]{1,0:T(8,128)} %get-tuple-element.65.mixed_ref, bf16[8,256,768]{2,1,0:T(8,128)(2,1)} %copy-done.2), custom_call_target="tpu_custom_call" | custom-call | flops 1000 | bytes 1000 | tf_op jit(solution)/shard_map/finish/pallas_call | solution.py:636
  (245 shorter events, 47.7 us)
Async XLA Ops:
  7.2 30.1 %copy-start = (f32[12,32]{1,0:T(8,128)S(1)}, f32[12,32]{1,0:T(8,128)}, u32[]{:S(2)}) copy-start(f32[12,32]{1,0:T(8,128)} %param.21) | copy-start | bytes 4612
  7.2 14.3 %copy-start.29 = (s32[512,2]{0,1:T(2,128)S(1)}, s32[512,2]{0,1:T(2,128)}, u32[]{:S(2)}) copy-start(s32[512,2]{0,1:T(2,128)} %param.24) | copy-start | bytes 12292
  7.2 110.8 %all-gather.4.cloned.1.call-start = ((), (), s32[]{:S(2)}) async-start(), calls=%async_computation.6 | async-start | bytes 1216512 | tf_op jit(solution)/shard_map/all_gather | solution.py:814
  7.9 176.3 %all-gather.6.cloned.1.call-start = ((), (), s32[]{:S(2)}) async-start(), calls=%async_computation.7 | async-start | bytes 5898240 | tf_op jit(solution)/shard_map/all_gather | solution.py:846
  11.9 15.6 %collective-permute-start.2 = (bf16[24,2432]{1,0:T(8,128)(2,1)S(1)}, bf16[24,2432]{1,0:T(8,128)(2,1)S(1)}, u32[]{:S(2)}, u32[]{:S(2)}) collective-permute-start(bf16[24,2432]{1,0:T(8,128)(2,1)S(1)} %concatenate.56), channel_id=1, source_target_pairs={{0,24},{4,28},{8,16},{12,20},{16,8},{20,12},{24,0},{28,4},{1,25},{... | collective-permute-start | bytes 350216 | tf_op jit(solution)/shard_map/ppermute | solution.py:654
  17.1 10.5 %collective-permute-start.1 = (bf16[24,2432]{1,0:T(8,128)(2,1)S(1)}, bf16[24,2432]{1,0:T(8,128)(2,1)S(1)}, u32[]{:S(2)}, u32[]{:S(2)}) collective-permute-start(bf16[24,2432]{1,0:T(8,128)(2,1)S(1)} %concatenate.56), channel_id=1, source_target_pairs={{0,16},{4,20},{8,24},{12,28},{16,0},{20,4},{24,8},{28,12},{1,17},{... | collective-permute-start | bytes 350216 | tf_op jit(solution)/shard_map/ppermute | solution.py:654
  17.1 10.5 %collective-permute-start = (bf16[24,2432]{1,0:T(8,128)(2,1)S(1)}, bf16[24,2432]{1,0:T(8,128)(2,1)S(1)}, u32[]{:S(2)}, u32[]{:S(2)}) collective-permute-start(bf16[24,2432]{1,0:T(8,128)(2,1)S(1)} %concatenate.56), channel_id=1, source_target_pairs={{0,8},{4,12},{8,0},{12,4},{16,24},{20,28},{24,16},{28,20},{1,9},{5... | collective-permute-start | bytes 350216 | tf_op jit(solution)/shard_map/ppermute | solution.py:654
  27.6 8.8 %copy-start.30 = (s32[384]{0:T(512)S(1)}, s32[384]{0:T(512)}, u32[]{:S(2)}) copy-start(s32[384]{0:T(512)} %param.23) | copy-start | bytes 4612
  27.7 9.0 %copy-start.7 = (bf16[512,768]{1,0:T(8,128)(2,1)S(1)}, bf16[512,768]{1,0:T(8,128)(2,1)}, u32[]{:S(2)}) copy-start(bf16[512,768]{1,0:T(8,128)(2,1)} %tokens_ref.1) | copy-start | bytes 2359300
  27.7 96.7 %all-to-all-start = ((bf16[8,256,768]{2,1,0:T(8,128)(2,1)}), bf16[8,256,768]{2,1,0:T(8,128)(2,1)}, u32[]{:S(2)}, u32[]{:S(2)}) async-start(bf16[8,256,768]{2,1,0:T(8,128)(2,1)} %spread.1), calls=%async_computation | async-start | bytes 6291456 | tf_op jit(solution)/shard_map/all_to_all | solution.py:662
  33.8 153.2 %all-gather.8.cloned.1.call-start = ((), (), s32[]{:S(2)}) async-start(), calls=%async_computation.8 | async-start | bytes 5898240 | tf_op jit(solution)/shard_map/all_gather | solution.py:847
  34.3 95.6 %collective-permute-start.11 = (s32[1,512,2]{1,2,0:T(2,128)S(1)}, s32[1,512,2]{1,2,0:T(2,128)S(1)}, u32[]{:S(2)}, u32[]{:S(2)}) collective-permute-start(s32[1,512,2]{1,2,0:T(2,128)S(1)} %bitcast.74), channel_id=1, source_target_pairs={{0,4},{4,0},{8,12},{12,8},{16,20},{20,16},{24,28},{28,24},{1,5},{5... | collective-permute-start | bytes 12296 | tf_op jit(solution)/shard_map/ppermute | solution.py:654
  37.0 29.5 %collective-permute-start.8 = (bf16[96,1280]{1,0:T(8,128)(2,1)S(1)}, bf16[96,1280]{1,0:T(8,128)(2,1)S(1)}, u32[]{:S(2)}, u32[]{:S(2)}) collective-permute-start(bf16[96,1280]{1,0:T(8,128)(2,1)S(1)} %slice.196), channel_id=1, source_target_pairs={{0,4},{4,0},{8,12},{12,8},{16,20},{20,16},{24,28},{28,24},{1,5},{5... | collective-permute-start | bytes 737288 | tf_op jit(solution)/shard_map/ppermute | solution.py:654
  38.2 41.9 %collective-permute-start.7 = (bf16[96,1280]{1,0:T(8,128)(2,1)S(1)}, bf16[96,1280]{1,0:T(8,128)(2,1)S(1)}, u32[]{:S(2)}, u32[]{:S(2)}) collective-permute-start(bf16[96,1280]{1,0:T(8,128)(2,1)S(1)} %slice.196), channel_id=1, source_target_pairs={{0,2},{1,3},{2,0},{3,1},{4,6},{5,7},{6,4},{7,5},{8,10},{9,11},{10,... | collective-permute-start | bytes 737288 | tf_op jit(solution)/shard_map/ppermute | solution.py:654
  66.4 13.7 %collective-permute-start.9 = (bf16[96,1280]{1,0:T(8,128)(2,1)S(1)}, bf16[96,1280]{1,0:T(8,128)(2,1)S(1)}, u32[]{:S(2)}, u32[]{:S(2)}) collective-permute-start(bf16[96,1280]{1,0:T(8,128)(2,1)S(1)} %collective-permute-done.8), channel_id=1, source_target_pairs={{0,2},{1,3},{2,0},{3,1},{4,6},{5,7},{6,4},{7,5},{8,10},{9,11},{10,... | collective-permute-start | bytes 737288 | tf_op jit(solution)/shard_map/ppermute | solution.py:654
  68.7 8.8 %collective-permute-start.3 = (bf16[96,1152]{1,0:T(8,128)(2,1)S(1)}, bf16[96,1152]{1,0:T(8,128)(2,1)S(1)}, u32[]{:S(2)}, u32[]{:S(2)}) collective-permute-start(bf16[96,1152]{1,0:T(8,128)(2,1)S(1)} %get-tuple-element.164), channel_id=1, source_target_pairs={{0,2},{1,3},{2,0},{3,1},{4,6},{5,7},{6,4},{7,5},{8,10},{9,11},{10,... | collective-permute-start | bytes 663560 | tf_op jit(solution)/shard_map/ppermute | solution.py:654
  69.2 18.2 %collective-permute-start.4 = (bf16[96,1152]{1,0:T(8,128)(2,1)S(1)}, bf16[96,1152]{1,0:T(8,128)(2,1)S(1)}, u32[]{:S(2)}, u32[]{:S(2)}) collective-permute-start(bf16[96,1152]{1,0:T(8,128)(2,1)S(1)} %get-tuple-element.164), channel_id=1, source_target_pairs={{0,4},{4,0},{8,12},{12,8},{16,20},{20,16},{24,28},{28,24},{1,5},{5... | collective-permute-start | bytes 663560 | tf_op jit(solution)/shard_map/ppermute | solution.py:654
  77.4 14.1 %copy-start.24 = (bf16[96,1152]{1,0:T(8,128)(2,1)}, bf16[96,1152]{1,0:T(8,128)(2,1)S(1)}, u32[]{:S(2)}) copy-start(bf16[96,1152]{1,0:T(8,128)(2,1)S(1)} %collective-permute-done.3) | copy-start | bytes 663556
  77.4 14.1 %collective-permute-start.5 = (bf16[96,1152]{1,0:T(8,128)(2,1)S(1)}, bf16[96,1152]{1,0:T(8,128)(2,1)S(1)}, u32[]{:S(2)}, u32[]{:S(2)}) collective-permute-start(bf16[96,1152]{1,0:T(8,128)(2,1)S(1)} %collective-permute-done.3), channel_id=1, source_target_pairs={{0,4},{4,0},{8,12},{12,8},{16,20},{20,16},{24,28},{28,24},{1,5},{5... | collective-permute-start | bytes 663560 | tf_op jit(solution)/shard_map/ppermute | solution.py:654
  80.2 15.4 %copy-start.4 = (bf16[384,1280]{1,0:T(8,128)(2,1)}, bf16[384,1280]{1,0:T(8,128)(2,1)S(1)}, u32[]{:S(2)}) copy-start(bf16[384,1280]{1,0:T(8,128)(2,1)S(1)} %pad_maximum_fusion.refs_2_) | copy-start | bytes 2949124
  80.2 15.4 %collective-permute-start.10 = (bf16[384,1280]{1,0:T(8,128)(2,1)S(1)}, bf16[384,1280]{1,0:T(8,128)(2,1)S(1)}, u32[]{:S(2)}, u32[]{:S(2)}) collective-permute-start(bf16[384,1280]{1,0:T(8,128)(2,1)S(1)} %pad_maximum_fusion.refs_2_), channel_id=1, source_target_pairs={{0,1},{1,0},{2,3},{3,2},{4,5},{5,4},{6,7},{7,6},{8,9},{9,8},{10,11... | collective-permute-start | bytes 2949128 | tf_op jit(solution)/shard_map/ppermute | solution.py:654
  92.5 3.2 collective-permute-start.6
  102.7 14.2 %slice-start.3 = ((bf16[384,1280]{1,0:T(8,128)(2,1)}), bf16[384,128]{1,0:T(8,128)(2,1)S(1)}, s32[]{:S(2)}) async-start(bf16[384,1280]{1,0:T(8,128)(2,1)} %copy-done.14), calls=%async_computation.12 | async-start | bytes 196608 | tf_op jit(solution)/shard_map/slice | solution.py:854
  124.4 47.1 %all-to-all-start.1 = ((bf16[8,128,768]{2,1,0:T(8,128)(2,1)}), bf16[8,128,768]{2,1,0:T(8,128)(2,1)S(1)}, u32[]{:S(2)}, u32[]{:S(2)}) async-start(bf16[8,128,768]{2,1,0:T(8,128)(2,1)} %get-tuple-element.68), calls=%async_computation.1 | async-start | bytes 3145728 | tf_op jit(solution)/shard_map/all_to_all | solution.py:662
  129.9 26.0 %collective-permute-start.12 = (s32[2,512,2]{1,2,0:T(2,128)S(1)}, s32[2,512,2]{1,2,0:T(2,128)S(1)}, u32[]{:S(2)}, u32[]{:S(2)}) collective-permute-start(s32[2,512,2]{1,2,0:T(2,128)S(1)} %pad_add_fusion.3), channel_id=1, source_target_pairs={{0,8},{4,12},{8,0},{12,4},{16,24},{20,28},{24,16},{28,20},{1,9},{5... | collective-permute-start | bytes 24584 | tf_op jit(solution)/shard_map/ppermute | solution.py:654
  155.9 10.8 %collective-permute-start.13 = (s32[4,512,2]{1,2,0:T(2,128)S(1)}, s32[4,512,2]{1,2,0:T(2,128)S(1)}, u32[]{:S(2)}, u32[]{:S(2)}) collective-permute-start(s32[4,512,2]{1,2,0:T(2,128)S(1)} %pad_add_fusion.2), channel_id=1, source_target_pairs={{0,16},{4,20},{8,24},{12,28},{16,0},{20,4},{24,8},{28,12},{1,17},{... | collective-permute-start | bytes 49160 | tf_op jit(solution)/shard_map/ppermute | solution.py:654
  171.5 8.0 %copy-start.21 = (bf16[8,128,768]{2,1,0:T(8,128)(2,1)}, bf16[8,128,768]{2,1,0:T(8,128)(2,1)S(1)}, u32[]{:S(2)}) copy-start(bf16[8,128,768]{2,1,0:T(8,128)(2,1)S(1)} %all-to-all-done.1.rows_ref) | copy-start | bytes 4718596
  171.5 9.7 %copy-start.5 = (bf16[384,1280]{1,0:T(8,128)(2,1)S(1)}, bf16[384,1280]{1,0:T(8,128)(2,1)}, u32[]{:S(2)}) copy-start(bf16[384,1280]{1,0:T(8,128)(2,1)} %copy-done.4) | copy-start | bytes 2949124
  171.5 45.3 %all-to-all-start.3 = ((bf16[8,128,768]{2,1,0:T(8,128)(2,1)}), bf16[8,128,768]{2,1,0:T(8,128)(2,1)}, u32[]{:S(2)}, u32[]{:S(2)}) async-start(bf16[8,128,768]{2,1,0:T(8,128)(2,1)} %get-tuple-element.71), calls=%async_computation.3 | async-start | bytes 3145728 | tf_op jit(solution)/shard_map/all_to_all | solution.py:662
  216.9 46.7 %all-to-all-start.2 = ((bf16[8,128,768]{2,1,0:T(8,128)(2,1)}), bf16[8,128,768]{2,1,0:T(8,128)(2,1)S(1)}, u32[]{:S(2)}, u32[]{:S(2)}) async-start(bf16[8,128,768]{2,1,0:T(8,128)(2,1)} %get-tuple-element.69), calls=%async_computation.2 | async-start | bytes 3145728 | tf_op jit(solution)/shard_map/all_to_all | solution.py:662
  263.6 12.1 %copy-start.10 = (bf16[8,128,768]{2,1,0:T(8,128)(2,1)}, bf16[8,128,768]{2,1,0:T(8,128)(2,1)S(1)}, u32[]{:S(2)}) copy-start(bf16[8,128,768]{2,1,0:T(8,128)(2,1)S(1)} %all-to-all-done.2.refs_0_) | copy-start | bytes 4718596
  263.6 47.1 %all-to-all-start.4 = ((bf16[8,144,768]{2,1,0:T(8,128)(2,1)}), bf16[8,144,768]{2,1,0:T(8,128)(2,1)S(1)}, u32[]{:S(2)}, u32[]{:S(2)}) async-start(bf16[8,144,768]{2,1,0:T(8,128)(2,1)} %get-tuple-element.79), calls=%async_computation.4 | async-start | bytes 3538944 | tf_op jit(solution)/shard_map/all_to_all | solution.py:662
  270.0 5.7 %copy-start.34 = (bf16[2048,768]{1,0:T(8,128)(2,1)S(1)}, bf16[2048,768]{1,0:T(8,128)(2,1)}, u32[]{:S(2)}) copy-start(bf16[2048,768]{1,0:T(8,128)(2,1)} %get-tuple-element.102) | copy-start | bytes 9437188
  270.0 12.0 %slice-start = ((s8[12582912]{0:T(1024)(128)(4,1)}), s8[4194304]{0:T(1024)(128)(4,1)S(1)}, s32[]{:S(2)}) async-start(s8[12582912]{0:T(1024)(128)(4,1)} %bitcast.71), calls=%async_computation.9 | async-start | bytes 8388608
  270.0 12.0 %slice-start.1 = ((s8[12582912]{0:T(1024)(128)(4,1)}), s8[4194304]{0:T(1024)(128)(4,1)S(1)}, s32[]{:S(2)}) async-start(s8[12582912]{0:T(1024)(128)(4,1)} %bitcast.71), calls=%async_computation.10 | async-start | bytes 8388608
  275.7 6.3 %slice-start.2 = ((s8[12582912]{0:T(1024)(128)(4,1)}), s8[4194304]{0:T(1024)(128)(4,1)S(1)}, s32[]{:S(2)}) async-start(s8[12582912]{0:T(1024)(128)(4,1)} %bitcast.71), calls=%async_computation.11 | async-start | bytes 8388608
  275.7 6.3 %copy-start.11 = (bf16[2048,768]{1,0:T(8,128)(2,1)S(1)}, bf16[2048,768]{1,0:T(8,128)(2,1)}, u32[]{:S(2)}) copy-start(bf16[2048,768]{1,0:T(8,128)(2,1)} %get-tuple-element.99) | copy-start | bytes 9437188
  281.5 86.4 %collective-permute-start.23 = (bf16[768,768]{1,0:T(8,128)(2,1)}, bf16[768,768]{1,0:T(8,128)(2,1)}, u32[]{:S(2)}, u32[]{:S(2)}) collective-permute-start(bf16[768,768]{1,0:T(8,128)(2,1)} %fusion.20), channel_id=1, source_target_pairs={{0,1},{1,0},{2,3},{3,2},{4,5},{5,4},{6,7},{7,6},{8,9},{9,8},{10,11... | collective-permute-start | bytes 3538952 | tf_op jit(solution)/shard_map/ppermute | solution.py:654
  281.5 7.6 %collective-permute-start.24 = (bf16[768,768]{1,0:T(8,128)(2,1)S(1)}, bf16[768,768]{1,0:T(8,128)(2,1)S(1)}, u32[]{:S(2)}, u32[]{:S(2)}) collective-permute-start(bf16[768,768]{1,0:T(8,128)(2,1)S(1)} %fusion.23), channel_id=1, source_target_pairs={{0,1},{1,0},{2,3},{3,2},{4,5},{5,4},{6,7},{7,6},{8,9},{9,8},{10,11... | collective-permute-start | bytes 3538952 | tf_op jit(solution)/shard_map/ppermute | solution.py:654
  284.8 10.7 %collective-permute-start.21 = (bf16[192,3072]{1,0:T(8,128)(2,1)S(1)}, bf16[192,3072]{1,0:T(8,128)(2,1)S(1)}, u32[]{:S(2)}, u32[]{:S(2)}) collective-permute-start(bf16[192,3072]{1,0:T(8,128)(2,1)S(1)} %convolution_convert_fusion), channel_id=1, source_target_pairs={{0,1},{1,0},{2,3},{3,2},{4,5},{5,4},{6,7},{7,6},{8,9},{9,8},{10,11... | collective-permute-start | bytes 3538952 | tf_op jit(solution)/shard_map/ppermute | solution.py:654
  288.6 63.4 %collective-permute-start.20 = (bf16[192,3072]{1,0:T(8,128)(2,1)}, bf16[192,3072]{1,0:T(8,128)(2,1)}, u32[]{:S(2)}, u32[]{:S(2)}) collective-permute-start(bf16[192,3072]{1,0:T(8,128)(2,1)} %convolution_convert_fusion.1), channel_id=1, source_target_pairs={{0,1},{1,0},{2,3},{3,2},{4,5},{5,4},{6,7},{7,6},{8,9},{9,8},{10,11... | collective-permute-start | bytes 3538952 | tf_op jit(solution)/shard_map/ppermute | solution.py:654
  294.9 92.9 %collective-permute-start.25 = (bf16[768,768]{1,0:T(8,128)(2,1)}, bf16[768,768]{1,0:T(8,128)(2,1)}, u32[]{:S(2)}, u32[]{:S(2)}) collective-permute-start(bf16[768,768]{1,0:T(8,128)(2,1)} %add_convert_fusion), channel_id=1, source_target_pairs={{0,2},{1,3},{2,0},{3,1},{4,6},{5,7},{6,4},{7,5},{8,10},{9,11},{10,... | collective-permute-start | bytes 3538952 | tf_op jit(solution)/shard_map/ppermute | solution.py:654
  299.3 88.5 %collective-permute-start.22 = (bf16[192,3072]{1,0:T(8,128)(2,1)}, bf16[192,3072]{1,0:T(8,128)(2,1)}, u32[]{:S(2)}, u32[]{:S(2)}) collective-permute-start(bf16[192,3072]{1,0:T(8,128)(2,1)} %add_convert_fusion.1), channel_id=1, source_target_pairs={{0,2},{1,3},{2,0},{3,1},{4,6},{5,7},{6,4},{7,5},{8,10},{9,11},{10,... | collective-permute-start | bytes 3538952 | tf_op jit(solution)/shard_map/ppermute | solution.py:654
  351.9 9.7 %copy-start.32 = (f32[12,512]{1,0:T(8,128)S(1)}, f32[12,512]{1,0:T(8,128)}, u32[]{:S(2)}) copy-start(f32[12,512]{1,0:T(8,128)} %get-tuple-element.91) | copy-start | bytes 73732
  351.9 10.1 %copy-start.8 = (bf16[512,768]{1,0:T(8,128)(2,1)S(1)}, bf16[512,768]{1,0:T(8,128)(2,1)}, u32[]{:S(2)}) copy-start(bf16[512,768]{1,0:T(8,128)(2,1)} %tokens_ref.1) | copy-start | bytes 2359300
  351.9 10.1 %copy-start.31 = (bf16[512,2304]{1,0:T(8,128)(2,1)S(1)}, bf16[512,2304]{1,0:T(8,128)(2,1)}, u32[]{:S(2)}) copy-start(bf16[512,2304]{1,0:T(8,128)(2,1)} %get-tuple-element.90) | copy-start | bytes 7077892
  351.9 32.3 %collective-permute-start.19 = (bf16[384,3200]{1,0:T(8,128)(2,1)}, bf16[384,3200]{1,0:T(8,128)(2,1)}, u32[]{:S(2)}, u32[]{:S(2)}) collective-permute-start(bf16[384,3200]{1,0:T(8,128)(2,1)} %get-tuple-element.94), channel_id=1, source_target_pairs={{0,1},{1,0},{2,3},{3,2},{4,5},{5,4},{6,7},{7,6},{8,9},{9,8},{10,11... | collective-permute-start | bytes 7372808 | tf_op jit(solution)/shard_map/ppermute | solution.py:654
  362.0 5.9 %copy-start.35 = (bf16[2048,768]{1,0:T(8,128)(2,1)S(1)}, bf16[2048,768]{1,0:T(8,128)(2,1)}, u32[]{:S(2)}) copy-start(bf16[2048,768]{1,0:T(8,128)(2,1)} %get-tuple-element.102) | copy-start | bytes 9437188
  367.5 11.0 %collective-permute-start.14 = (f32[1152]{0:T(1024)S(1)}, f32[1152]{0:T(1024)S(1)}, u32[]{:S(2)}, u32[]{:S(2)}) collective-permute-start(f32[1152]{0:T(1024)S(1)} %pad_maximum_fusion.5), channel_id=1, source_target_pairs={{0,1},{1,0},{2,3},{3,2},{4,5},{5,4},{6,7},{7,6},{8,9},{9,8},{10,11... | collective-permute-start | bytes 13832 | tf_op jit(solution)/shard_map/ppermute | solution.py:654
  374.2 75.2 %all-to-all-start.5 = ((bf16[8,256,768]{2,1,0:T(8,128)(2,1)}), bf16[8,256,768]{2,1,0:T(8,128)(2,1)S(1)}, u32[]{:S(2)}, u32[]{:S(2)}) async-start(bf16[8,256,768]{2,1,0:T(8,128)(2,1)} %get-tuple-element.82), calls=%async_computation.5 | async-start | bytes 6291456 | tf_op jit(solution)/shard_map/all_to_all | solution.py:662
  378.5 3.7 collective-permute-start.15
  382.2 22.2 %collective-permute-start.16 = (f32[1152]{0:T(1024)S(1)}, f32[1152]{0:T(1024)S(1)}, u32[]{:S(2)}, u32[]{:S(2)}) collective-permute-start(f32[1152]{0:T(1024)S(1)} %add.307), channel_id=1, source_target_pairs={{0,4},{4,0},{8,12},{12,8},{16,20},{20,16},{24,28},{28,24},{1,5},{5... | collective-permute-start | bytes 13832 | tf_op jit(solution)/shard_map/ppermute | solution.py:654
  388.2 18.9 %collective-permute-start.30 = (bf16[192,1536]{1,0:T(8,128)(2,1)S(1)}, bf16[192,1536]{1,0:T(8,128)(2,1)S(1)}, u32[]{:S(2)}, u32[]{:S(2)}) collective-permute-start(bf16[192,1536]{1,0:T(8,128)(2,1)S(1)} %pad_maximum_fusion.2), channel_id=1, source_target_pairs={{0,2},{1,3},{2,0},{3,1},{4,6},{5,7},{6,4},{7,5},{8,10},{9,11},{10,... | collective-permute-start | bytes 1769480 | tf_op jit(solution)/shard_map/ppermute | solution.py:654
  404.5 32.5 %collective-permute-start.26 = (bf16[192,1664]{1,0:T(8,128)(2,1)S(1)}, bf16[192,1664]{1,0:T(8,128)(2,1)S(1)}, u32[]{:S(2)}, u32[]{:S(2)}) collective-permute-start(bf16[192,1664]{1,0:T(8,128)(2,1)S(1)} %slice.210), channel_id=1, source_target_pairs={{0,4},{4,0},{8,12},{12,8},{16,20},{20,16},{24,28},{28,24},{1,5},{5... | collective-permute-start | bytes 1916936 | tf_op jit(solution)/shard_map/ppermute | solution.py:654
  409.1 40.3 %collective-permute-start.31 = (bf16[96,1536]{1,0:T(8,128)(2,1)}, bf16[96,1536]{1,0:T(8,128)(2,1)}, u32[]{:S(2)}, u32[]{:S(2)}) collective-permute-start(bf16[96,1536]{1,0:T(8,128)(2,1)} %slice.249), channel_id=1, source_target_pairs={{0,4},{4,0},{8,12},{12,8},{16,20},{20,16},{24,28},{28,24},{1,5},{5... | collective-permute-start | bytes 884744 | tf_op jit(solution)/shard_map/ppermute | solution.py:654
  438.3 16.7 %collective-permute-start.27 = (bf16[96,1664]{1,0:T(8,128)(2,1)}, bf16[96,1664]{1,0:T(8,128)(2,1)S(1)}, u32[]{:S(2)}, u32[]{:S(2)}) collective-permute-start(bf16[96,1664]{1,0:T(8,128)(2,1)} %slice.248), channel_id=1, source_target_pairs={{0,2},{1,3},{2,0},{3,1},{4,6},{5,7},{6,4},{7,5},{8,10},{9,11},{10,... | collective-permute-start | bytes 958472 | tf_op jit(solution)/shard_map/ppermute | solution.py:654
  449.4 8.7 %copy-start.2 = (bf16[8,256,768]{2,1,0:T(8,128)(2,1)}, bf16[8,256,768]{2,1,0:T(8,128)(2,1)S(1)}, u32[]{:S(2)}) copy-start(bf16[8,256,768]{2,1,0:T(8,128)(2,1)S(1)} %all-to-all-done.5.produced_ref) | copy-start | bytes 9437188
  449.4 4.8 collective-permute-start.17
  452.1 14.9 %collective-permute-start.32 = (bf16[48,1536]{1,0:T(8,128)(2,1)}, bf16[48,1536]{1,0:T(8,128)(2,1)}, u32[]{:S(2)}, u32[]{:S(2)}) collective-permute-start(bf16[48,1536]{1,0:T(8,128)(2,1)} %slice.251), channel_id=1, source_target_pairs={{0,16},{4,20},{8,24},{12,28},{16,0},{20,4},{24,8},{28,12},{1,17},{... | collective-permute-start | bytes 442376 | tf_op jit(solution)/shard_map/ppermute | solution.py:654
  454.2 11.6 %collective-permute-start.18 = (f32[1152]{0:T(1024)S(1)}, f32[1152]{0:T(1024)S(1)}, u32[]{:S(2)}, u32[]{:S(2)}) collective-permute-start(f32[1152]{0:T(1024)S(1)} %add.309), channel_id=1, source_target_pairs={{0,16},{4,20},{8,24},{12,28},{16,0},{20,4},{24,8},{28,12},{1,17},{... | collective-permute-start | bytes 13832 | tf_op jit(solution)/shard_map/ppermute | solution.py:654
  456.0 13.1 %collective-permute-start.28 = (bf16[48,1664]{1,0:T(8,128)(2,1)S(1)}, bf16[48,1664]{1,0:T(8,128)(2,1)S(1)}, u32[]{:S(2)}, u32[]{:S(2)}) collective-permute-start(bf16[48,1664]{1,0:T(8,128)(2,1)S(1)} %slice.250), channel_id=1, source_target_pairs={{0,16},{4,20},{8,24},{12,28},{16,0},{20,4},{24,8},{28,12},{1,17},{... | collective-permute-start | bytes 479240 | tf_op jit(solution)/shard_map/ppermute | solution.py:654
  458.1 17.2 %copy-start.1 = (f32[12,32]{1,0:T(8,128)S(1)}, f32[12,32]{1,0:T(8,128)}, u32[]{:S(2)}) copy-start(f32[12,32]{1,0:T(8,128)} %param.21) | copy-start | bytes 4612
  468.2 4.4 collective-permute-start.33
  470.1 4.5 collective-permute-start.29
  (20 other events, 52.2 us)
Sparse Core Ops, SparseCore 0:
  10.9 99.5 all-gather.3
  112.1 35.7 all-gather.5
  149.4 37.4 all-gather.7
